TPU v7x, 32 devices: a whole 2x2x4 slice. The times are simulated.
32 devices in a mesh: dp: 16 (over z, x, core), fsdp: 2 (over y).
Axes of the slice: x: 2, y: 2, z: 4, core: 2. Of those that a mesh axis runs over, the one named last changes fastest.
Arguments:
- attn: bfloat16 [18432, 1536], P(('dp', 'fsdp')), may hold values from -6 to 6
- cotangent: bfloat16 [18432, 3072], P(('dp', 'fsdp')), may hold values from -12 to 12
- weight: bfloat16 [1536, 3072], P('fsdp'), may hold values from -0.15625 to 0.15625
- projector: bfloat16 [1536, 256], replicated, may hold values from -0.15625 to 0.15625
- moment_one: float32 [3072, 256], P(('dp', 'fsdp')), may hold values from -256 to 256
- moment_two: float32 [3072, 256], P(('dp', 'fsdp')), may hold values from 30 to 3000
- step_count: int32 [1], replicated, may hold values from 1 to 10
Outputs:
- grad_input: bfloat16 [18432, 1536], P(('dp', 'fsdp'))
- weight_step: float32 [1536, 3072], P('fsdp')
- first_moment: float32 [3072, 256], P(('dp', 'fsdp'))
- second_moment: float32 [3072, 256], P(('dp', 'fsdp'))
All inputs are finite; a program needn't handle non-finite values.
Results may differ from a plain program's by a relative error of at most 0.015.
Values may be sent and summed in bfloat16 or wider, within the bound.
No kernel may reach another device: no remote copies, remote signals or barrier semaphores. Data moves between devices by JAX's collectives and lax.ppermute only.
A program may use at most 128 MiB of HBM per device.

v0:
```python
import jax
import jax.numpy as jnp
from jax import lax
from jax.sharding import PartitionSpec as P


def on_device(attn, cotangent, weight, projector, moment_one, moment_two, step_count):
    shard_rows = weight.shape[0]
    reduced = jnp.dot(attn, projector, preferred_element_type=jnp.float32).astype(jnp.bfloat16)
    grad_input = lax.dot_general(
        cotangent,
        lax.all_gather(weight, "fsdp", axis=0, tiled=True),
        (((1,), (1,)), ((), ())),
        preferred_element_type=jnp.float32,
    ).astype(jnp.bfloat16)
    projected = lax.psum_scatter(
        lax.dot_general(
            cotangent, reduced, (((0,), (0,)), ((), ())), preferred_element_type=jnp.float32
        ),
        ("dp", "fsdp"),
        scatter_dimension=0,
        tiled=True,
    )
    first_moment = 0.9 * moment_one + 0.1 * projected
    second_moment = 0.999 * moment_two + 0.001 * projected * projected
    steps = step_count[0].astype(jnp.float32)
    first_hat = first_moment / (1.0 - jnp.power(jnp.float32(0.9), steps))
    second_hat = second_moment / (1.0 - jnp.power(jnp.float32(0.999), steps))
    low_step = (first_hat / (jnp.sqrt(second_hat) + 1e-08)).astype(jnp.bfloat16)
    my_projector = lax.dynamic_slice_in_dim(
        projector, lax.axis_index("fsdp") * shard_rows, shard_rows, 0
    )
    weight_step = 0.25 * lax.dot_general(
        my_projector,
        lax.all_gather(low_step, ("dp", "fsdp"), axis=0, tiled=True),
        (((1,), (1,)), ((), ())),
        preferred_element_type=jnp.float32,
    )
    return (grad_input, weight_step, first_moment, second_moment)


def solution(mesh):
    placed = (
        P(("dp", "fsdp"), None),
        P(("dp", "fsdp"), None),
        P("fsdp", None),
        P(),
        P(("dp", "fsdp"), None),
        P(("dp", "fsdp"), None),
        P(),
    )
    return jax.shard_map(
        on_device,
        mesh=mesh,
        in_specs=placed,
        out_specs=(
            P(("dp", "fsdp"), None),
            P("fsdp", None),
            P(("dp", "fsdp"), None),
            P(("dp", "fsdp"), None),
        ),
        check_vma=False,
    )
```

profile of v0, /device:TPU:0, one launch (start us, length us, event | category | flops | bytes accessed | tf_op | source)
XLA Modules:
  0.0 316.7 jit_solution(2970010074234859417)
XLA Ops:
  7.2 0.0 copy-start
  7.2 0.0 reduce-scatter.4.cloned.1.call-start
  7.2 1.9 copy-done
  9.2 6.2 %convolution_bitcast_fusion = f32[3072,256]{0,1:T(8,128)} fusion(bf16[576,3072]{1,0:T(8,128)(2,1)S(1)} %copy-done, bf16[576,1536]{1,0:T(8,128)(2,1)} %param.7, bf16[1536,256]{1,0:T(8,128)(2,1)} %param.10), kind=kOutput, calls=%fused_computation.1 | convolution fusion | flops 1359101952 | bytes 9240576 | tf_op jit(solution)/shard_map/dot_general | solution.py:17
  15.4 3.5 %copy.20 = f32[3072,256]{1,0:T(8,128)} copy(f32[3072,256]{0,1:T(8,128)} %convolution_bitcast_fusion) | data formatting | bytes 6291456
  18.9 0.0 reduce-scatter.4.cloned.1.call-update
  18.9 0.0 all-gather.5.cloned.1.call-start
  19.7 1.6 copy.15
  21.3 1.6 copy.16
  23.0 100.3 %reduce-scatter.4.cloned.1.call-done = f32[96,256]{1,0:T(8,128)} async-done(((f32[3072,256]{1,0:T(8,128)}), f32[96,256]{1,0:T(8,128)}) %reduce-scatter.4.cloned.1.call-update) | async-done | bytes 98320
  123.3 1.6 copy.21
  124.9 1.8 divide_convert_fusion
  126.7 1.6 copy.17
  128.2 0.0 all-gather.5.cloned.1.call-update
  128.3 0.0 all-gather.3.cloned.1.call-start
  128.3 0.7 all-gather.3.cloned.1.call-update
  129.0 1.6 copy.19
  130.6 1.6 copy.18
  132.3 50.2 %all-gather.5.cloned.1.call-done = bf16[3072,256]{1,0:T(8,128)(2,1)} async-done(((bf16[96,256]{1,0:T(8,128)(2,1)}), bf16[3072,256]{1,0:T(8,128)(2,1)}) %all-gather.5.cloned.1.call-update) | async-done | bytes 1572880 | tf_op jit(solution)/shard_map/all_gather | solution.py:35
  182.5 6.7 %convolution_multiply_fusion = f32[768,3072]{1,0:T(8,128)} fusion(bf16[3072,256]{1,0:T(8,128)(2,1)} %all-gather.5.cloned.1.call-done, bf16[1536,256]{1,0:T(8,128)(2,1)} %param.10, s32[]{:T(128)S(6)} %select_n.3), kind=kOutput, calls=%fused_computation | convolution fusion | flops 1210318848 | bytes 11403268 | tf_op jit(solution)/shard_map/dot_general | solution.py:33
  189.2 111.8 %all-gather.3.cloned.1.call-done = bf16[1536,3072]{1,0:T(8,128)(2,1)} async-done(((bf16[768,3072]{1,0:T(8,128)(2,1)}), bf16[1536,3072]{1,0:T(8,128)(2,1)}) %all-gather.3.cloned.1.call-update) | async-done | bytes 9437200 | tf_op jit(solution)/shard_map/all_gather | solution.py:12
  301.0 9.2 %convolution_convert_fusion = bf16[576,1536]{1,0:T(8,128)(2,1)} fusion(bf16[576,3072]{1,0:T(8,128)(2,1)S(1)} %copy-done, bf16[1536,3072]{1,0:T(8,128)(2,1)} %all-gather.3.cloned.1.call-done), kind=kOutput, calls=%fused_computation.2 | convolution fusion | flops 5436702720 | bytes 14745600 | tf_op jit(solution)/shard_map/dot_general | solution.py:10
Async XLA Ops:
  7.2 2.0 copy-start
  7.2 116.1 %reduce-scatter.4.cloned.1.call-start = ((), (), s32[]{:S(2)}) async-start(), calls=%async_computation.3 | async-start | bytes 3244032
  18.9 163.6 %all-gather.5.cloned.1.call-start = ((), (), s32[]{:S(2)}) async-start(), calls=%async_computation.2 | async-start | bytes 1622016 | tf_op jit(solution)/shard_map/all_gather | solution.py:35
  128.3 172.7 %all-gather.3.cloned.1.call-start = ((), (), s32[]{:S(2)}) async-start(), calls=%async_computation.1 | async-start | bytes 14155776 | tf_op jit(solution)/shard_map/all_gather | solution.py:12
Sparse Core Ops, SparseCore 0:
  19.0 104.1 reduce-scatter.3
  128.4 54.0 all-gather.4
  184.0 116.8 all-gather.2
where the time goes:
time: 317 us
  waiting for transfers between devices  263 us (83%)
  matrix products  22.1 us (7%)
  local copies, waits for them, and re-layouts  15.2 us (5%)
  between operations  14.5 us (5%)
    all_gather x1, waiting for transfers between devices, on_device(): lax.all_gather(weight, 'fsdp', axis=0, tiled=True)  112 us
    unnamed x4, waiting for transfers between devices  101 us
    all_gather x1, waiting for transfers between devices, on_device(): lax.all_gather(low_step, ('dp', 'fsdp'), axis=0, tiled=True)  50.2 us
    unnamed x8, local copies, waits for them, and re-layouts  13.7 us
    dot_general x1, matrix products, on_device(): lax.dot_general(cotangent, lax.all_gather(weight, 'fsdp', axis=0, tiled=T...  9.16 us
    dot_general x1, matrix products, on_device(): lax.dot_general(my_projector, lax.all_gather(low_step, ('dp', 'fsdp'), ax...  6.71 us
  transfers between devices with their start and end apart: 3, of which 3 were waited for; matrix products, arithmetic and copies ran while one was open for 4% of the time, Pallas kernels for 0%

commit v1 on v0

v1 whole, which is shorter than its diff:
```python
import jax
import jax.numpy as jnp
from jax import lax
from jax.sharding import PartitionSpec as P

AXES = ("dp", "fsdp")


def solution(mesh):
    n_dp, n_y = mesh.shape["dp"], mesh.shape["fsdp"]
    n_z = n_dp // 4

    def send(value, move):
        pairs = []
        for z in range(n_z):
            for x in range(2):
                for c in range(2):
                    for y in range(n_y):
                        tz, tx, tc, ty = move(z, x, c, y)
                        pairs.append(
                            (((z * 2 + x) * 2 + c) * n_y + y, ((tz * 2 + tx) * 2 + tc) * n_y + ty)
                        )
        return lax.ppermute(value, AXES, pairs)

    def to_core(value):
        return send(value, lambda z, x, c, y: (z, x, 1 - c, y))

    def to_plane(value, dx, dy):
        return send(value, lambda z, x, c, y: (z, x ^ dx, c, (y + dy) % n_y))

    def to_z(value, dz):
        return send(value, lambda z, x, c, y: ((z + dz) % n_z, x, c, y))

    def to_z_pair(value):
        return send(value, lambda z, x, c, y: (z ^ 1, x, c, y))

    plane = [(dx, dy) for dx in range(2) for dy in range(n_y) if (dx, dy) != (0, 0)]

    def on_device(attn, cotangent, weight, projector, moment_one, moment_two, step_count):
        d, y = lax.axis_index("dp"), lax.axis_index("fsdp")
        c, x, z = d % 2, (d // 2) % 2, d // 4
        shard_rows, width = weight.shape
        own_rows, rank = moment_one.shape
        f32, bf16 = jnp.float32, jnp.bfloat16

        def weight_piece(q):
            return lax.dynamic_index_in_dim(
                weight.reshape(8, shard_rows // 8, width), q, 0, keepdims=False
            )

        q = (x * 2 + z % 2) * 2 + c
        shards = []
        for dy in range(1, n_y):
            own = to_plane(weight_piece(q), 0, dy)
            over_x, over_z = to_plane(own, 1, 0), to_z_pair(own)
            half = own.shape[0] // 2
            low, high = to_plane(over_z[:half], 1, 0), to_z_pair(over_x[half:])
            mine = [own, over_z, over_x, jnp.concatenate([low, high])]
            theirs = [to_core(piece) for piece in mine]
            full = jnp.zeros((8, shard_rows // 8, width), bf16)
            for k in range(4):
                qk = q ^ (2 * k)
                full = lax.dynamic_update_index_in_dim(full, mine[k], qk, 0)
                full = lax.dynamic_update_index_in_dim(full, theirs[k], qk ^ 1, 0)
            shards.append(full.reshape(shard_rows, width))

        reduced = jnp.dot(attn, projector, preferred_element_type=f32).astype(bf16)
        partial = lax.dot_general(
            cotangent, reduced, (((0,), (0,)), ((), ())), preferred_element_type=f32
        ).reshape(n_z, 2, 2, n_y, own_rows, rank)
        got = to_core(lax.dynamic_index_in_dim(partial, 1 - c, 2, keepdims=False).astype(bf16))
        chip = lax.dynamic_index_in_dim(partial, c, 2, keepdims=False) + got.astype(f32)

        def plane_part(tx, ty):
            part = lax.dynamic_index_in_dim(chip, tx, 1, keepdims=False)
            return lax.dynamic_index_in_dim(part, ty, 1, keepdims=False)

        total = plane_part(x, y)
        for dx, dy in plane:
            got = to_plane(plane_part(x ^ dx, (y + dy) % n_y).astype(bf16), dx, dy)
            total = total + got.astype(f32)
        projected = lax.dynamic_index_in_dim(total, z, 0, keepdims=False)
        for dz in range(1, n_z):
            part = lax.dynamic_index_in_dim(total, (z + dz) % n_z, 0, keepdims=False)
            projected = projected + to_z(part.astype(bf16), dz).astype(f32)

        first_moment = 0.9 * moment_one + 0.1 * projected
        second_moment = 0.999 * moment_two + 0.001 * projected * projected
        steps = step_count[0].astype(f32)
        first_hat = first_moment / (1.0 - jnp.power(f32(0.9), steps))
        second_hat = second_moment / (1.0 - jnp.power(f32(0.999), steps))
        low_step = (first_hat / (jnp.sqrt(second_hat) + 1e-08)).astype(bf16)

        column = jnp.zeros((n_z, own_rows, rank), bf16)
        column = lax.dynamic_update_index_in_dim(column, low_step, z, 0)
        for dz in range(1, n_z):
            column = lax.dynamic_update_index_in_dim(
                column, to_z(low_step, dz), (z - dz) % n_z, 0
            )
        whole = jnp.zeros((2, 2, n_y, n_z, own_rows, rank), bf16)

        def place(whole, block, px, pc, py):
            return lax.dynamic_update_slice(whole, block[None, None, None], (pc, px, py, 0, 0, 0))

        whole = place(whole, column, x, c, y)
        whole = place(whole, to_core(column), x, 1 - c, y)
        for dx, dy in plane:
            got = to_plane(column, dx, dy)
            whole = place(whole, got, x ^ dx, c, (y - dy) % n_y)
            whole = place(whole, to_core(got), x ^ dx, 1 - c, (y - dy) % n_y)
        low_full = whole.transpose(3, 1, 0, 2, 4, 5).reshape(-1, rank)

        my_projector = lax.dynamic_slice_in_dim(projector, y * shard_rows, shard_rows, 0)
        weight_step = 0.25 * lax.dot_general(
            my_projector, low_full, (((1,), (1,)), ((), ())), preferred_element_type=f32
        )

        def columns_of(rows):
            return lax.dot_general(
                cotangent, rows, (((1,), (1,)), ((), ())), preferred_element_type=f32
            ).astype(bf16)

        grad_input = jnp.zeros((attn.shape[0], shard_rows * n_y), bf16)
        grad_input = lax.dynamic_update_slice_in_dim(
            grad_input, columns_of(weight), y * shard_rows, 1
        )
        for dy in range(1, n_y):
            grad_input = lax.dynamic_update_slice_in_dim(
                grad_input, columns_of(shards[dy - 1]), ((y - dy) % n_y) * shard_rows, 1
            )
        return grad_input, weight_step, first_moment, second_moment

    rows = P(("dp", "fsdp"), None)
    return jax.shard_map(
        on_device,
        mesh=mesh,
        in_specs=(rows, rows, P("fsdp", None), P(), rows, rows, P()),
        out_specs=(rows, P("fsdp", None), rows, rows),
        check_vma=False,
    )
```

time: 317 us -> 106 us (0.33)
  waiting for transfers between devices: 263 us -> 33.4 us
  starting transfers between devices: 0.12 us -> 26.8 us
  between operations: 14.5 us -> 1.72 us
  other arithmetic: 1.78 us -> 5.01 us
    all_gather x2 -> x0, waiting for transfers between devices: 162 us -> none  [the longest x1 112 us: on_device(): lax.all_gather(weight, 'fsdp', axis=0, tiled=True)]
    unnamed x4 -> x0, waiting for transfers between devices: 101 us -> none
    ppermute x0 -> x26, waiting for transfers between devices: none -> 33.4 us  [send(): return lax.ppermute(value, AXES, pairs)]
    ppermute x0 -> x26, starting transfers between devices: none -> 26.8 us  [send(): return lax.ppermute(value, AXES, pairs)]
    unnamed x8 -> x9, local copies, waits for them, and re-layouts: 13.7 us -> 3.92 us
    dot_general x0 -> x1, local copies, waits for them, and re-layouts: none -> 3.52 us  [on_device(): lax.dot_general(cotangent, reduced, (((0,), (0,)), ((), ())), preferred_e...]
    add x0 -> x2, other arithmetic: none -> 3.19 us  [the longest x1 1.81 us: on_device(): lax.dynamic_index_in_dim(partial, c, 2, keepdims=False) + got.astype(f32)]
    dot_general x2 -> x3, matrix products: 15.9 us -> 15.2 us  [the longest x2 10.1 us: columns_of(): lax.dot_general(cotangent, rows, (((1,), (1,)), ((), ())), preferred_elem...]
  transfers between devices with their start and end apart: 3 -> 26, of which waited for: 3 -> 10; matrix products, arithmetic and copies ran while one was open for 4% -> 20% of each run, Pallas kernels for 0% -> 0%
where the time goes in v1:
time: 106 us; the launch traced here: 105 us
  waiting for transfers between devices  33.4 us (32%)
  starting transfers between devices  26.8 us (25%)
  matrix products  21.4 us (20%)
  local copies, waits for them, and re-layouts  17 us (16%)
  other arithmetic  5.01 us (5%)
  between operations  1.72 us (2%)
    ppermute x26, waiting for transfers between devices, send(): return lax.ppermute(value, AXES, pairs)  33.4 us
    ppermute x26, starting transfers between devices, send(): return lax.ppermute(value, AXES, pairs)  26.8 us
    dot_general x2, matrix products, columns_of(): lax.dot_general(cotangent, rows, (((1,), (1,)), ((), ())), preferred_elem...  10.1 us
    dot_general x1, matrix products, on_device(): lax.dot_general(cotangent, reduced, (((0,), (0,)), ((), ())), preferred_e...  6.19 us
    dot_general x1, matrix products, on_device(): lax.dot_general(my_projector, low_full, (((1,), (1,)), ((), ())), preferr...  5.17 us
    unnamed x9, local copies, waits for them, and re-layouts  3.92 us
    dot_general x1, local copies, waits for them, and re-layouts, on_device(): lax.dot_general(cotangent, reduced, (((0,), (0,)), ((), ())), preferred_e...  3.52 us
    convert_element_type x1, local copies, waits for them, and re-layouts, on_device(): lax.dynamic_index_in_dim(partial, 1 - c, 2, keepdims=False).astype(bf16)  2.38 us
  transfers between devices with their start and end apart: 26, of which 10 were waited for; matrix products, arithmetic and copies ran while one was open for 20% of the time, Pallas kernels for 0%

profile of v1, /device:TPU:0, one launch (start us, length us, event | category | flops | bytes accessed | tf_op | source)
XLA Modules:
  0.0 105.4 jit_solution(4304462134272399348)
XLA Ops:
  0.7 2.0 %copy-done = bf16[576,3072]{1,0:T(8,128)(2,1)S(1)} copy-done((bf16[576,3072]{1,0:T(8,128)(2,1)S(1)}, bf16[576,3072]{1,0:T(8,128)(2,1)}, u32[]{:S(2)}) %copy-start) | copy-done | bytes 3538968
  2.6 6.2 %convolution_bitcast_fusion = f32[3072,256]{0,1:T(8,128)} fusion(bf16[576,3072]{1,0:T(8,128)(2,1)S(1)} %copy-done, bf16[576,1536]{1,0:T(8,128)(2,1)} %param.7, bf16[1536,256]{1,0:T(8,128)(2,1)} %param.10), kind=kOutput, calls=%fused_computation.1 | convolution fusion | flops 1359101952 | bytes 9240576 | tf_op jit(solution)/shard_map/dot_general | solution.py:68
  8.8 3.5 %copy.13 = f32[3072,256]{1,0:T(8,128)} copy(f32[3072,256]{0,1:T(8,128)} %convolution_bitcast_fusion) | data formatting | bytes 6291456 | tf_op jit(solution)/shard_map/dot_general | solution.py:68
  12.3 2.4 %fusion.3 = bf16[4,2,2,96,256]{4,3,2,1,0:T(8,128)(2,1)} fusion(f32[4,2,2,2,96,256]{5,4,3,2,1,0:T(8,128)} %bitcast.120, s32[]{:T(128)S(6)} %select_n.210), kind=kLoop, calls=%fused_computation.10 | loop fusion | bytes 1572868 | tf_op jit(solution)/shard_map/convert_element_type | solution.py:71
  15.2 2.3 %collective-permute-done.9 = bf16[4,2,2,96,256]{4,3,2,1,0:T(8,128)(2,1)} collective-permute-done((bf16[4,2,2,96,256]{4,3,2,1,0:T(8,128)(2,1)}, bf16[4,2,2,96,256]{4,3,2,1,0:T(8,128)(2,1)}, u32[]{:S(2)}, u32[]{:S(2)}) %collective-permute-start.9) | collective-permute-done | bytes 786464 | tf_op jit(solution)/shard_map/ppermute | solution.py:23
  17.4 1.8 %bitcast_add_fusion = f32[4,2,2,96,256]{4,3,2,1,0:T(8,128)S(1)} fusion(bf16[4,2,2,96,256]{4,3,2,1,0:T(8,128)(2,1)} %collective-permute-done.9, f32[4,2,2,2,96,256]{5,4,3,2,1,0:T(8,128)} %bitcast.121, s32[]{:T(128)S(6)} %select_n.209), kind=kLoop, calls=%fused_computation.2 | loop fusion | flops 786432 | bytes 3932164 | tf_op jit(solution)/shard_map/add | solution.py:72
  21.2 3.8 %collective-permute-start.12 = (bf16[4,96,256]{2,1,0:T(8,128)(2,1)}, bf16[4,96,256]{2,1,0:T(8,128)(2,1)}, u32[]{:S(2)}, u32[]{:S(2)}) collective-permute-start(bf16[4,96,256]{2,1,0:T(8,128)(2,1)} %get-tuple-element.9), channel_id=1, source_target_pairs={{0,5},{1,4},{2,7},{3,6},{4,1},{5,0},{6,3},{7,2},{8,13},{9,12},{10,... | collective-permute-start | bytes 589832 | tf_op jit(solution)/shard_map/ppermute | solution.py:23
  25.6 1.9 %dynamic-slice_bitcast_fusion = bf16[96,3072]{1,0:T(8,128)(2,1)} fusion(bf16[8,96,3072]{2,1,0:T(8,128)(2,1)} %bitcast.124, s32[]{:T(128)S(6)} %select_n.199), kind=kLoop, calls=%fused_computation.19 | loop fusion | bytes 1179652 | tf_op jit(solution)/shard_map/jit(dynamic_index_in_dim)/squeeze | solution.py:47
  27.5 2.0 %collective-permute-start = (bf16[96,3072]{1,0:T(8,128)(2,1)}, bf16[96,3072]{1,0:T(8,128)(2,1)}, u32[]{:S(2)}, u32[]{:S(2)}) collective-permute-start(bf16[96,3072]{1,0:T(8,128)(2,1)} %dynamic-slice_bitcast_fusion), channel_id=1, source_target_pairs={{0,1},{1,0},{2,3},{3,2},{4,5},{5,4},{6,7},{7,6},{8,9},{9,8},{10,11... | collective-permute-start | bytes 1769480 | tf_op jit(solution)/shard_map/ppermute | solution.py:23
  29.5 1.6 %collective-permute-done.12 = bf16[4,96,256]{2,1,0:T(8,128)(2,1)} collective-permute-done((bf16[4,96,256]{2,1,0:T(8,128)(2,1)}, bf16[4,96,256]{2,1,0:T(8,128)(2,1)}, u32[]{:S(2)}, u32[]{:S(2)}) %collective-permute-start.12) | collective-permute-done | bytes 196640 | tf_op jit(solution)/shard_map/ppermute | solution.py:23
  31.1 4.0 %collective-permute-done.11 = bf16[4,96,256]{2,1,0:T(8,128)(2,1)} collective-permute-done((bf16[4,96,256]{2,1,0:T(8,128)(2,1)}, bf16[4,96,256]{2,1,0:T(8,128)(2,1)}, u32[]{:S(2)}, u32[]{:S(2)}) %collective-permute-start.11) | collective-permute-done | bytes 196640 | tf_op jit(solution)/shard_map/ppermute | solution.py:23
  37.9 3.6 %collective-permute-start.15 = (bf16[96,256]{1,0:T(8,128)(2,1)}, bf16[96,256]{1,0:T(8,128)(2,1)}, u32[]{:S(2)}, u32[]{:S(2)}) collective-permute-start(bf16[96,256]{1,0:T(8,128)(2,1)} %get-tuple-element.12), channel_id=1, source_target_pairs={{0,24},{1,25},{2,26},{3,27},{4,28},{5,29},{6,30},{7,31},{8,0},{9,1... | collective-permute-start | bytes 147464 | tf_op jit(solution)/shard_map/ppermute | solution.py:23
  43.8 6.2 %fusion = bf16[576,1536]{1,0:T(8,128)(2,1)} fusion(bf16[576,1536]{1,0:T(8,128)(2,1)} %broadcast_in_dim.74, s32[]{:T(128)S(6)} %select_n.193, bf16[576,3072]{1,0:T(8,128)(2,1)S(1)} %copy-done, bf16[768,3072]{1,0:T(8,128)(2,1)} %param.9), kind=kOutput, calls=%fused_computation.6 | convolution fusion | flops 2718351360 | bytes 9142276 | tf_op jit(solution)/shard_map/dot_general | solution.py:119
  50.9 2.5 %collective-permute-start.2 = (bf16[96,3072]{1,0:T(8,128)(2,1)}, bf16[96,3072]{1,0:T(8,128)(2,1)S(1)}, u32[]{:S(2)}, u32[]{:S(2)}) collective-permute-start(bf16[96,3072]{1,0:T(8,128)(2,1)} %collective-permute-done), channel_id=1, source_target_pairs={{0,8},{1,9},{2,10},{3,11},{4,12},{5,13},{6,14},{7,15},{8,0},{9,1},... | collective-permute-start | bytes 1769480 | tf_op jit(solution)/shard_map/ppermute | solution.py:23
  54.9 1.8 %bitcast_dynamic-update-slice_fusion.19 = (bf16[4,96,256]{2,1,0:T(8,128)(2,1)S(1)}, bf16[96,256]{1,0:T(8,128)(2,1)S(1)}, f32[96,256]{1,0:T(8,128)}, f32[96,256]{1,0:T(8,128)}) fusion(bf16[4,96,256]{2,1,0:T(8,128)(2,1)S(1)} %broadcast_in_dim.85, s32[]{:T(128)S(6)} %select_n.223, f32[]{:T(128)} %bitcast.25, f32[]{:T(128)} %bitcast.24, ...), kind=kLoop, calls=%fused_computation.54 | loop fusion | flops 442368 | bytes 737292 | tf_op jit(solution)/shard_map/jit(dynamic_update_index_in_dim)/dynamic_update_slice | solution.py:95
  60.0 9.7 %collective-permute-done.16 = bf16[96,256]{1,0:T(8,128)(2,1)S(1)} collective-permute-done((bf16[96,256]{1,0:T(8,128)(2,1)S(1)}, bf16[96,256]{1,0:T(8,128)(2,1)S(1)}, u32[]{:S(2)}, u32[]{:S(2)}) %collective-permute-start.16) | collective-permute-done | bytes 49184 | tf_op jit(solution)/shard_map/ppermute | solution.py:23
  69.7 2.1 %collective-permute-start.18 = (bf16[96,256]{1,0:T(8,128)(2,1)S(1)}, bf16[96,256]{1,0:T(8,128)(2,1)S(1)}, u32[]{:S(2)}, u32[]{:S(2)}) collective-permute-start(bf16[96,256]{1,0:T(8,128)(2,1)S(1)} %get-tuple-element.5), channel_id=1, source_target_pairs={{0,24},{1,25},{2,26},{3,27},{4,28},{5,29},{6,30},{7,31},{8,0},{9,1... | collective-permute-start | bytes 147464 | tf_op jit(solution)/shard_map/ppermute | solution.py:23
  71.8 2.0 %collective-permute-done.18 = bf16[96,256]{1,0:T(8,128)(2,1)S(1)} collective-permute-done((bf16[96,256]{1,0:T(8,128)(2,1)S(1)}, bf16[96,256]{1,0:T(8,128)(2,1)S(1)}, u32[]{:S(2)}, u32[]{:S(2)}) %collective-permute-start.18) | collective-permute-done | bytes 49184 | tf_op jit(solution)/shard_map/ppermute | solution.py:23
  73.8 1.6 %collective-permute-start.20 = (bf16[4,96,256]{2,1,0:T(8,128)(2,1)S(1)}, bf16[4,96,256]{2,1,0:T(8,128)(2,1)S(1)}, u32[]{:S(2)}, u32[]{:S(2)}) collective-permute-start(bf16[4,96,256]{2,1,0:T(8,128)(2,1)S(1)} %bitcast_dynamic-update-slice_fusion.16), channel_id=1, source_target_pairs={{0,1},{1,0},{2,3},{3,2},{4,5},{5,4},{6,7},{7,6},{8,9},{9,8},{10,11... | collective-permute-start | bytes 589832 | tf_op jit(solution)/shard_map/ppermute | solution.py:23
  75.6 1.6 %collective-permute-start.22 = (bf16[4,96,256]{2,1,0:T(8,128)(2,1)S(1)}, bf16[4,96,256]{2,1,0:T(8,128)(2,1)S(1)}, u32[]{:S(2)}, u32[]{:S(2)}) collective-permute-start(bf16[4,96,256]{2,1,0:T(8,128)(2,1)S(1)} %bitcast_dynamic-update-slice_fusion.16), channel_id=1, source_target_pairs={{0,4},{1,5},{2,6},{3,7},{4,0},{5,1},{6,2},{7,3},{8,12},{9,13},{10,... | collective-permute-start | bytes 589832 | tf_op jit(solution)/shard_map/ppermute | solution.py:23
  77.9 1.6 %collective-permute-start.6 = (bf16[48,3072]{1,0:T(8,128)(2,1)S(1)}, bf16[48,3072]{1,0:T(8,128)(2,1)S(1)}, u32[]{:S(2)}, u32[]{:S(2)}) collective-permute-start(bf16[48,3072]{1,0:T(8,128)(2,1)S(1)} %slice.8), channel_id=1, source_target_pairs={{0,4},{1,5},{2,6},{3,7},{4,0},{5,1},{6,2},{7,3},{8,12},{9,13},{10,... | collective-permute-start | bytes 884744 | tf_op jit(solution)/shard_map/ppermute | solution.py:23
  81.1 12.0 %collective-permute-done.6 = bf16[48,3072]{1,0:T(8,128)(2,1)S(1)} collective-permute-done((bf16[48,3072]{1,0:T(8,128)(2,1)S(1)}, bf16[48,3072]{1,0:T(8,128)(2,1)S(1)}, u32[]{:S(2)}, u32[]{:S(2)}) %collective-permute-start.6) | collective-permute-done | bytes 294944 | tf_op jit(solution)/shard_map/ppermute | solution.py:23
  96.0 5.2 %convolution_multiply_fusion = f32[768,3072]{1,0:T(8,128)} fusion(bf16[3072,256]{1,0:T(8,128)(2,1)S(1)} %bitcast.122, bf16[1536,256]{1,0:T(8,128)(2,1)S(1)} %copy-done.2, s32[]{:T(128)S(6)} %select_n.193), kind=kOutput, calls=%fused_computation | convolution fusion | flops 1210318848 | bytes 11403268 | tf_op jit(solution)/shard_map/dot_general | solution.py:114
  101.5 3.9 %fusion.2 = bf16[576,1536]{1,0:T(8,128)(2,1)} fusion(bf16[576,1536]{1,0:T(8,128)(2,1)} %fusion, s32[]{:T(128)S(6)} %select_n.208, bf16[768,3072]{1,0:T(8,128)(2,1)S(1)} %bitcast.123, bf16[576,3072]{1,0:T(8,128)(2,1)S(1)} %copy-done), kind=kOutput, calls=%fused_computation.8 | convolution fusion | flops 2718351360 | bytes 9142276 | tf_op jit(solution)/shard_map/dot_general | solution.py:119
  (75 shorter events, 18.6 us)
Async XLA Ops:
  14.7 2.7 %collective-permute-start.9 = (bf16[4,2,2,96,256]{4,3,2,1,0:T(8,128)(2,1)}, bf16[4,2,2,96,256]{4,3,2,1,0:T(8,128)(2,1)}, u32[]{:S(2)}, u32[]{:S(2)}) collective-permute-start(bf16[4,2,2,96,256]{4,3,2,1,0:T(8,128)(2,1)} %fusion.3), channel_id=1, source_target_pairs={{0,2},{1,3},{2,0},{3,1},{4,6},{5,7},{6,4},{7,5},{8,10},{9,11},{10,... | collective-permute-start | bytes 2359304 | tf_op jit(solution)/shard_map/ppermute | solution.py:23
  21.2 9.9 %collective-permute-start.12 = (bf16[4,96,256]{2,1,0:T(8,128)(2,1)}, bf16[4,96,256]{2,1,0:T(8,128)(2,1)}, u32[]{:S(2)}, u32[]{:S(2)}) collective-permute-start(bf16[4,96,256]{2,1,0:T(8,128)(2,1)} %get-tuple-element.9), channel_id=1, source_target_pairs={{0,5},{1,4},{2,7},{3,6},{4,1},{5,0},{6,3},{7,2},{8,13},{9,12},{10,... | collective-permute-start | bytes 589832 | tf_op jit(solution)/shard_map/ppermute | solution.py:23
  25.1 10.0 %collective-permute-start.11 = (bf16[4,96,256]{2,1,0:T(8,128)(2,1)}, bf16[4,96,256]{2,1,0:T(8,128)(2,1)}, u32[]{:S(2)}, u32[]{:S(2)}) collective-permute-start(bf16[4,96,256]{2,1,0:T(8,128)(2,1)} %get-tuple-element.10), channel_id=1, source_target_pairs={{0,4},{1,5},{2,6},{3,7},{4,0},{5,1},{6,2},{7,3},{8,12},{9,13},{10,... | collective-permute-start | bytes 589832 | tf_op jit(solution)/shard_map/ppermute | solution.py:23
  25.6 9.5 %collective-permute-start.10 = (bf16[4,96,256]{2,1,0:T(8,128)(2,1)}, bf16[4,96,256]{2,1,0:T(8,128)(2,1)}, u32[]{:S(2)}, u32[]{:S(2)}) collective-permute-start(bf16[4,96,256]{2,1,0:T(8,128)(2,1)} %get-tuple-element.8), channel_id=1, source_target_pairs={{0,1},{1,0},{2,3},{3,2},{4,5},{5,4},{6,7},{7,6},{8,9},{9,8},{10,11... | collective-permute-start | bytes 589832 | tf_op jit(solution)/shard_map/ppermute | solution.py:23
  27.5 23.2 %collective-permute-start = (bf16[96,3072]{1,0:T(8,128)(2,1)}, bf16[96,3072]{1,0:T(8,128)(2,1)}, u32[]{:S(2)}, u32[]{:S(2)}) collective-permute-start(bf16[96,3072]{1,0:T(8,128)(2,1)} %dynamic-slice_bitcast_fusion), channel_id=1, source_target_pairs={{0,1},{1,0},{2,3},{3,2},{4,5},{5,4},{6,7},{7,6},{8,9},{9,8},{10,11... | collective-permute-start | bytes 1769480 | tf_op jit(solution)/shard_map/ppermute | solution.py:23
  37.9 15.5 %collective-permute-start.15 = (bf16[96,256]{1,0:T(8,128)(2,1)}, bf16[96,256]{1,0:T(8,128)(2,1)}, u32[]{:S(2)}, u32[]{:S(2)}) collective-permute-start(bf16[96,256]{1,0:T(8,128)(2,1)} %get-tuple-element.12), channel_id=1, source_target_pairs={{0,24},{1,25},{2,26},{3,27},{4,28},{5,29},{6,30},{7,31},{8,0},{9,1... | collective-permute-start | bytes 147464 | tf_op jit(solution)/shard_map/ppermute | solution.py:23
  41.5 13.4 %collective-permute-start.14 = (bf16[96,256]{1,0:T(8,128)(2,1)}, bf16[96,256]{1,0:T(8,128)(2,1)}, u32[]{:S(2)}, u32[]{:S(2)}) collective-permute-start(bf16[96,256]{1,0:T(8,128)(2,1)} %get-tuple-element.13), channel_id=1, source_target_pairs={{0,16},{1,17},{2,18},{3,19},{4,20},{5,21},{6,22},{7,23},{8,24},{9,... | collective-permute-start | bytes 147464 | tf_op jit(solution)/shard_map/ppermute | solution.py:23
  41.5 13.4 %collective-permute-start.13 = (bf16[96,256]{1,0:T(8,128)(2,1)}, bf16[96,256]{1,0:T(8,128)(2,1)}, u32[]{:S(2)}, u32[]{:S(2)}) collective-permute-start(bf16[96,256]{1,0:T(8,128)(2,1)} %get-tuple-element.11), channel_id=1, source_target_pairs={{0,8},{1,9},{2,10},{3,11},{4,12},{5,13},{6,14},{7,15},{8,16},{9,17... | collective-permute-start | bytes 147464 | tf_op jit(solution)/shard_map/ppermute | solution.py:23
  50.8 24.8 %collective-permute-start.1 = (bf16[96,3072]{1,0:T(8,128)(2,1)}, bf16[96,3072]{1,0:T(8,128)(2,1)S(1)}, u32[]{:S(2)}, u32[]{:S(2)}) collective-permute-start(bf16[96,3072]{1,0:T(8,128)(2,1)} %collective-permute-done), channel_id=1, source_target_pairs={{0,2},{1,3},{2,0},{3,1},{4,6},{5,7},{6,4},{7,5},{8,10},{9,11},{10,... | collective-permute-start | bytes 1769480 | tf_op jit(solution)/shard_map/ppermute | solution.py:23
  50.9 26.3 %collective-permute-start.2 = (bf16[96,3072]{1,0:T(8,128)(2,1)}, bf16[96,3072]{1,0:T(8,128)(2,1)S(1)}, u32[]{:S(2)}, u32[]{:S(2)}) collective-permute-start(bf16[96,3072]{1,0:T(8,128)(2,1)} %collective-permute-done), channel_id=1, source_target_pairs={{0,8},{1,9},{2,10},{3,11},{4,12},{5,13},{6,14},{7,15},{8,0},{9,1},... | collective-permute-start | bytes 1769480 | tf_op jit(solution)/shard_map/ppermute | solution.py:23
  53.4 24.4 %collective-permute-start.4 = (bf16[96,3072]{1,0:T(8,128)(2,1)}, bf16[96,3072]{1,0:T(8,128)(2,1)S(1)}, u32[]{:S(2)}, u32[]{:S(2)}) collective-permute-start(bf16[96,3072]{1,0:T(8,128)(2,1)} %collective-permute-done), channel_id=1, source_target_pairs={{0,4},{1,5},{2,6},{3,7},{4,0},{5,1},{6,2},{7,3},{8,12},{9,13},{10,... | collective-permute-start | bytes 1769480 | tf_op jit(solution)/shard_map/ppermute | solution.py:23
  56.8 12.9 %collective-permute-start.16 = (bf16[96,256]{1,0:T(8,128)(2,1)S(1)}, bf16[96,256]{1,0:T(8,128)(2,1)S(1)}, u32[]{:S(2)}, u32[]{:S(2)}) collective-permute-start(bf16[96,256]{1,0:T(8,128)(2,1)S(1)} %get-tuple-element.5), channel_id=1, source_target_pairs={{0,8},{1,9},{2,10},{3,11},{4,12},{5,13},{6,14},{7,15},{8,16},{9,17... | collective-permute-start | bytes 147464 | tf_op jit(solution)/shard_map/ppermute | solution.py:23
  58.6 13.2 %collective-permute-start.17 = (bf16[96,256]{1,0:T(8,128)(2,1)S(1)}, bf16[96,256]{1,0:T(8,128)(2,1)S(1)}, u32[]{:S(2)}, u32[]{:S(2)}) collective-permute-start(bf16[96,256]{1,0:T(8,128)(2,1)S(1)} %get-tuple-element.5), channel_id=1, source_target_pairs={{0,16},{1,17},{2,18},{3,19},{4,20},{5,21},{6,22},{7,23},{8,24},{9,... | collective-permute-start | bytes 147464 | tf_op jit(solution)/shard_map/ppermute | solution.py:23
  69.7 4.1 %collective-permute-start.18 = (bf16[96,256]{1,0:T(8,128)(2,1)S(1)}, bf16[96,256]{1,0:T(8,128)(2,1)S(1)}, u32[]{:S(2)}, u32[]{:S(2)}) collective-permute-start(bf16[96,256]{1,0:T(8,128)(2,1)S(1)} %get-tuple-element.5), channel_id=1, source_target_pairs={{0,24},{1,25},{2,26},{3,27},{4,28},{5,29},{6,30},{7,31},{8,0},{9,1... | collective-permute-start | bytes 147464 | tf_op jit(solution)/shard_map/ppermute | solution.py:23
  73.8 5.7 %collective-permute-start.19 = (bf16[4,96,256]{2,1,0:T(8,128)(2,1)S(1)}, bf16[4,96,256]{2,1,0:T(8,128)(2,1)S(1)}, u32[]{:S(2)}, u32[]{:S(2)}) collective-permute-start(bf16[4,96,256]{2,1,0:T(8,128)(2,1)S(1)} %bitcast_dynamic-update-slice_fusion.16), channel_id=1, source_target_pairs={{0,2},{1,3},{2,0},{3,1},{4,6},{5,7},{6,4},{7,5},{8,10},{9,11},{10,... | collective-permute-start | bytes 589832 | tf_op jit(solution)/shard_map/ppermute | solution.py:23
  73.8 7.3 %collective-permute-start.20 = (bf16[4,96,256]{2,1,0:T(8,128)(2,1)S(1)}, bf16[4,96,256]{2,1,0:T(8,128)(2,1)S(1)}, u32[]{:S(2)}, u32[]{:S(2)}) collective-permute-start(bf16[4,96,256]{2,1,0:T(8,128)(2,1)S(1)} %bitcast_dynamic-update-slice_fusion.16), channel_id=1, source_target_pairs={{0,1},{1,0},{2,3},{3,2},{4,5},{5,4},{6,7},{7,6},{8,9},{9,8},{10,11... | collective-permute-start | bytes 589832 | tf_op jit(solution)/shard_map/ppermute | solution.py:23
  75.6 17.6 %collective-permute-start.22 = (bf16[4,96,256]{2,1,0:T(8,128)(2,1)S(1)}, bf16[4,96,256]{2,1,0:T(8,128)(2,1)S(1)}, u32[]{:S(2)}, u32[]{:S(2)}) collective-permute-start(bf16[4,96,256]{2,1,0:T(8,128)(2,1)S(1)} %bitcast_dynamic-update-slice_fusion.16), channel_id=1, source_target_pairs={{0,4},{1,5},{2,6},{3,7},{4,0},{5,1},{6,2},{7,3},{8,12},{9,13},{10,... | collective-permute-start | bytes 589832 | tf_op jit(solution)/shard_map/ppermute | solution.py:23
  77.2 16.5 %collective-permute-start.24 = (bf16[4,96,256]{2,1,0:T(8,128)(2,1)S(1)}, bf16[4,96,256]{2,1,0:T(8,128)(2,1)S(1)}, u32[]{:S(2)}, u32[]{:S(2)}) collective-permute-start(bf16[4,96,256]{2,1,0:T(8,128)(2,1)S(1)} %bitcast_dynamic-update-slice_fusion.16), channel_id=1, source_target_pairs={{0,5},{1,4},{2,7},{3,6},{4,1},{5,0},{6,3},{7,2},{8,13},{9,12},{10,... | collective-permute-start | bytes 589832 | tf_op jit(solution)/shard_map/ppermute | solution.py:23
  77.9 15.3 %collective-permute-start.6 = (bf16[48,3072]{1,0:T(8,128)(2,1)S(1)}, bf16[48,3072]{1,0:T(8,128)(2,1)S(1)}, u32[]{:S(2)}, u32[]{:S(2)}) collective-permute-start(bf16[48,3072]{1,0:T(8,128)(2,1)S(1)} %slice.8), channel_id=1, source_target_pairs={{0,4},{1,5},{2,6},{3,7},{4,0},{5,1},{6,2},{7,3},{8,12},{9,13},{10,... | collective-permute-start | bytes 884744 | tf_op jit(solution)/shard_map/ppermute | solution.py:23
  79.5 14.4 %collective-permute-start.7 = (bf16[48,3072]{1,0:T(8,128)(2,1)S(1)}, bf16[48,3072]{1,0:T(8,128)(2,1)S(1)}, u32[]{:S(2)}, u32[]{:S(2)}) collective-permute-start(bf16[48,3072]{1,0:T(8,128)(2,1)S(1)} %slice.9), channel_id=1, source_target_pairs={{0,8},{1,9},{2,10},{3,11},{4,12},{5,13},{6,14},{7,15},{8,0},{9,1},... | collective-permute-start | bytes 884744 | tf_op jit(solution)/shard_map/ppermute | solution.py:23
  81.1 20.1 %collective-permute-start.3 = (bf16[96,3072]{1,0:T(8,128)(2,1)S(1)}, bf16[96,3072]{1,0:T(8,128)(2,1)S(1)}, u32[]{:S(2)}, u32[]{:S(2)}) collective-permute-start(bf16[96,3072]{1,0:T(8,128)(2,1)S(1)} %collective-permute-done.2), channel_id=1, source_target_pairs={{0,2},{1,3},{2,0},{3,1},{4,6},{5,7},{6,4},{7,5},{8,10},{9,11},{10,... | collective-permute-start | bytes 1769480 | tf_op jit(solution)/shard_map/ppermute | solution.py:23
  93.2 8.2 %collective-permute-start.5 = (bf16[96,3072]{1,0:T(8,128)(2,1)S(1)}, bf16[96,3072]{1,0:T(8,128)(2,1)S(1)}, u32[]{:S(2)}, u32[]{:S(2)}) collective-permute-start(bf16[96,3072]{1,0:T(8,128)(2,1)S(1)} %collective-permute-done.4), channel_id=1, source_target_pairs={{0,2},{1,3},{2,0},{3,1},{4,6},{5,7},{6,4},{7,5},{8,10},{9,11},{10,... | collective-permute-start | bytes 1769480 | tf_op jit(solution)/shard_map/ppermute | solution.py:23
  93.2 2.2 %collective-permute-start.21 = (bf16[4,96,256]{2,1,0:T(8,128)(2,1)S(1)}, bf16[4,96,256]{2,1,0:T(8,128)(2,1)S(1)}, u32[]{:S(2)}, u32[]{:S(2)}) collective-permute-start(bf16[4,96,256]{2,1,0:T(8,128)(2,1)S(1)} %collective-permute-done.20), channel_id=1, source_target_pairs={{0,2},{1,3},{2,0},{3,1},{4,6},{5,7},{6,4},{7,5},{8,10},{9,11},{10,... | collective-permute-start | bytes 589832 | tf_op jit(solution)/shard_map/ppermute | solution.py:23
  95.4 6.0 %collective-permute-start.8 = (bf16[96,3072]{1,0:T(8,128)(2,1)S(1)}, bf16[96,3072]{1,0:T(8,128)(2,1)S(1)}, u32[]{:S(2)}, u32[]{:S(2)}) collective-permute-start(bf16[96,3072]{1,0:T(8,128)(2,1)S(1)} %constant_dynamic-update-slice_fusion), channel_id=1, source_target_pairs={{0,2},{1,3},{2,0},{3,1},{4,6},{5,7},{6,4},{7,5},{8,10},{9,11},{10,... | collective-permute-start | bytes 1769480 | tf_op jit(solution)/shard_map/ppermute | solution.py:23
  (6 other events, 26.8 us)

commit v2 on v0

v2 whole, which is shorter than its diff:
```python
import jax
import jax.numpy as jnp
from jax import lax
from jax.experimental import pallas as pl
from jax.experimental.pallas import tpu as pltpu
from jax.sharding import PartitionSpec as P

AXES = ("dp", "fsdp")
F32, BF16 = jnp.float32, jnp.bfloat16
MIB = 1 << 20
VMEM = pl.BlockSpec(memory_space=pltpu.VMEM)
SMEM = pl.BlockSpec(memory_space=pltpu.SMEM)
ANY = pl.BlockSpec(memory_space=pl.ANY)


def shape(dims, dtype):
    return jax.ShapeDtypeStruct(dims, dtype)


def params(mib):
    return pltpu.CompilerParams(vmem_limit_bytes=mib * MIB)


def cost(flops, nbytes):
    return pl.CostEstimate(flops=int(flops), bytes_accessed=int(nbytes), transcendentals=0)


def place():
    d = lax.axis_index("dp")
    return d // 4, (d // 2) % 2, d % 2, lax.axis_index("fsdp")


def power(base, count):
    result, factor = F32(1.0), base
    for bit in range(31):
        result = jnp.where((count // (1 << bit)) % 2 == 1, result * F32(factor), result)
        factor = factor * factor
    return result


def plain(attn, cotangent, weight, projector, moment_one, moment_two, step_count):
    shard_rows = weight.shape[0]
    reduced = jnp.dot(attn, projector, preferred_element_type=F32).astype(BF16)
    grad_input = lax.dot_general(
        cotangent,
        lax.all_gather(weight, "fsdp", axis=0, tiled=True),
        (((1,), (1,)), ((), ())),
        preferred_element_type=F32,
    ).astype(BF16)
    projected = lax.psum_scatter(
        lax.dot_general(cotangent, reduced, (((0,), (0,)), ((), ())), preferred_element_type=F32),
        AXES,
        scatter_dimension=0,
        tiled=True,
    )
    first_moment = 0.9 * moment_one + 0.1 * projected
    second_moment = 0.999 * moment_two + 0.001 * projected * projected
    steps = step_count[0].astype(F32)
    first_hat = first_moment / (1.0 - jnp.power(F32(0.9), steps))
    second_hat = second_moment / (1.0 - jnp.power(F32(0.999), steps))
    low_step = (first_hat / (jnp.sqrt(second_hat) + 1e-08)).astype(BF16)
    my_projector = lax.dynamic_slice_in_dim(
        projector, lax.axis_index("fsdp") * shard_rows, shard_rows, 0
    )
    weight_step = 0.25 * lax.dot_general(
        my_projector,
        lax.all_gather(low_step, AXES, axis=0, tiled=True),
        (((1,), (1,)), ((), ())),
        preferred_element_type=F32,
    )
    return grad_input, weight_step, first_moment, second_moment


def solution(mesh):
    n_dp, n_y = mesh.shape["dp"], mesh.shape["fsdp"]
    n_z = n_dp // 4
    groups = 2 * n_z
    plane = [(dx, dy) for dx in range(2) for dy in range(n_y) if (dx, dy) != (0, 0)]

    def send(value, move):
        pairs = []
        for z in range(n_z):
            for x in range(2):
                for c in range(2):
                    for y in range(n_y):
                        tz, tx, tc, ty = move(z, x, c, y)
                        pairs.append(
                            (((z * 2 + x) * 2 + c) * n_y + y, ((tz * 2 + tx) * 2 + tc) * n_y + ty)
                        )
        return lax.ppermute(value, AXES, pairs)

    def to_core(value):
        return send(value, lambda z, x, c, y: (z, x, 1 - c, y))

    def to_plane(value, dx, dy):
        return send(value, lambda z, x, c, y: (z, x ^ dx, c, (y + dy) % n_y))

    def to_z(value, dz):
        return send(value, lambda z, x, c, y: ((z + dz) % n_z, x, c, y))

    def to_z_pair(value):
        return send(value, lambda z, x, c, y: (z ^ 1, x, c, y))

    def local_sums(attn, projector, cotangent):
        tokens, inner = attn.shape
        width, rank = cotangent.shape[1], projector.shape[1]
        rows = width // groups
        own = rows // (2 * n_y)

        def kernel(a_hbm, p_hbm, g_hbm, send_ref, keep_ref, a, p, g, red, part, sems):
            c = lax.axis_index("dp") % 2
            copy_a = pltpu.make_async_copy(a_hbm, a, sems.at[0])
            copy_p = pltpu.make_async_copy(p_hbm, p, sems.at[1])
            copy_a.start()
            copy_p.start()
            copies = []
            for k in range(groups):
                span = pl.ds(k * rows, rows)
                copies.append(pltpu.make_async_copy(g_hbm.at[:, span], g.at[k], sems.at[2 + k]))
                copies[-1].start()
            copy_a.wait()
            copy_p.wait()
            red[...] = jnp.dot(a[...], p[...], preferred_element_type=F32).astype(BF16)
            for k in range(groups):
                copies[k].wait()
                part[k % 2] = lax.dot_general(
                    g[k], red[...], (((0,), (0,)), ((), ())), preferred_element_type=F32
                )
                for y in range(n_y):
                    mine = pl.multiple_of(c * (n_y * own) + y * own, own)
                    theirs = pl.multiple_of((1 - c) * (n_y * own) + y * own, own)
                    keep_ref[k % 2, y, k // 2] = part[k % 2, pl.ds(mine, own), :]
                    send_ref[k % 2, y, k // 2] = part[k % 2, pl.ds(theirs, own), :].astype(BF16)

        dims = (2, n_y, n_z, own, rank)
        return pl.pallas_call(
            kernel,
            out_shape=(shape(dims, BF16), shape(dims, F32)),
            in_specs=[ANY, ANY, ANY],
            out_specs=(VMEM, VMEM),
            scratch_shapes=[
                pltpu.VMEM(attn.shape, BF16),
                pltpu.VMEM(projector.shape, BF16),
                pltpu.VMEM((groups, tokens, rows), BF16),
                pltpu.VMEM((tokens, rank), BF16),
                pltpu.VMEM((2, rows, rank), F32),
                pltpu.SemaphoreType.DMA((2 + groups,)),
            ],
            compiler_params=params(24),
            cost_estimate=cost(
                2 * tokens * rank * (inner + width), 2 * tokens * (inner + width) + 6 * width * rank
            ),
        )(attn, projector, cotangent)

    def core_sum(keep, got):
        slab = keep.shape[2:]

        def kernel(keep_ref, got_ref, own_ref, *send_refs):
            z, x, c, y = place()
            own_ref[...] = keep_ref[x, y] + got_ref[x, y].astype(F32)
            for (dx, dy), ref in zip(plane, send_refs):
                tx, ty = (x + dx) % 2, (y + dy) % n_y
                ref[...] = (keep_ref[tx, ty] + got_ref[tx, ty].astype(F32)).astype(BF16)

        return pl.pallas_call(
            kernel,
            out_shape=(shape(slab, F32),) + (shape(slab, BF16),) * len(plane),
            in_specs=[VMEM, VMEM],
            out_specs=(VMEM,) * (1 + len(plane)),
            compiler_params=params(12),
            cost_estimate=cost(keep.size, 8 * keep.size),
        )(keep, got)

    def plane_sum(own, got):
        slab = own.shape[1:]

        def kernel(own_ref, *refs):
            got_refs, out_ref, send_refs = refs[: len(got)], refs[len(got)], refs[len(got) + 1 :]
            z, x, c, y = place()
            for dz in range(n_z):
                tz = (z + dz) % n_z
                total = own_ref[tz]
                for ref in got_refs:
                    total = total + ref[tz].astype(F32)
                if dz == 0:
                    out_ref[...] = total
                else:
                    send_refs[dz - 1][...] = total.astype(BF16)

        return pl.pallas_call(
            kernel,
            out_shape=(shape(slab, F32),) + (shape(slab, BF16),) * (n_z - 1),
            in_specs=[VMEM] * (1 + len(got)),
            out_specs=(VMEM,) * n_z,
            compiler_params=params(8),
            cost_estimate=cost(4 * own.size, 10 * own.size),
        )(own, *got)

    def adam(own, got, moment_one, moment_two, step_count):
        def kernel(step_ref, own_ref, *refs):
            got_refs, (m1, m2, first_ref, second_ref, low_ref) = refs[: len(got)], refs[len(got) :]
            projected = own_ref[...]
            for ref in got_refs:
                projected = projected + ref[...].astype(F32)
            first = 0.9 * m1[...] + 0.1 * projected
            second = 0.999 * m2[...] + 0.001 * projected * projected
            first_ref[...] = first
            second_ref[...] = second
            count = step_ref[0]
            ones = jnp.ones(first.shape, F32)
            first_hat = first / ((1.0 - power(0.9, count)) * ones)
            second_hat = second / ((1.0 - power(0.999, count)) * ones)
            low_ref[...] = (first_hat / (jnp.sqrt(second_hat) + 1e-08)).astype(BF16)

        dims = own.shape
        return pl.pallas_call(
            kernel,
            out_shape=(shape(dims, F32), shape(dims, F32), shape(dims, BF16)),
            in_specs=[SMEM] + [VMEM] * (3 + len(got)),
            out_specs=(VMEM, VMEM, VMEM),
            compiler_params=params(4),
            cost_estimate=cost(20 * own.size, 24 * own.size),
        )(step_count, own, *got, moment_one, moment_two)

    def step_product(my_projector, blocks):
        rows, rank = my_projector.shape
        own = blocks[0][3].shape[1]
        span = 2 * n_y * own
        width = groups * span

        def kernel(p_ref, *refs):
            columns, (out_hbm, low, out, sems) = refs[: len(blocks)], refs[len(blocks) :]
            z, x, c, y = place()
            for (dc, dx, dy, _), ref in zip(blocks, columns):
                tc, tx, ty = (c + dc) % 2, (x + dx) % 2, (y + n_y - dy) % n_y
                for dz in range(n_z):
                    tz = (z + n_z - dz) % n_z
                    row = pl.multiple_of((tc * n_y + ty) * own, own)
                    low[tz * 2 + tx, pl.ds(row, own), :] = ref[dz]
            copies = []
            for k in range(groups):
                out[k] = 0.25 * lax.dot_general(
                    p_ref[...], low[k], (((1,), (1,)), ((), ())), preferred_element_type=F32
                )
                copies.append(
                    pltpu.make_async_copy(out.at[k], out_hbm.at[:, pl.ds(k * span, span)], sems.at[k])
                )
                copies[-1].start()
            for copy in copies:
                copy.wait()

        return pl.pallas_call(
            kernel,
            out_shape=shape((rows, width), F32),
            in_specs=[VMEM] * (1 + len(blocks)),
            out_specs=ANY,
            scratch_shapes=[
                pltpu.VMEM((groups, span, rank), BF16),
                pltpu.VMEM((groups, rows, span), F32),
                pltpu.SemaphoreType.DMA((groups,)),
            ],
            compiler_params=params(24),
            cost_estimate=cost(2 * rows * rank * width, 4 * rows * width),
        )(my_projector, *[block[3] for block in blocks])

    def input_product(cotangent, pieces, dy, into=None):
        tokens, width = cotangent.shape
        rows = sum(piece.shape[0] for _, piece in pieces)
        step = 256 if rows % 256 == 0 else 128
        chunks = rows // step

        def kernel(*refs):
            g_hbm, w_hbm = refs[0], refs[1 : 1 + len(pieces)]
            out_hbm, g, w, out, sems = refs[-5:]
            z, x, c, y = place()
            copy_g = pltpu.make_async_copy(g_hbm, g, sems.at[0])
            copy_g.start()
            copies = []
            for k, ((position, piece), ref) in enumerate(zip(pieces, w_hbm)):
                count = piece.shape[0]
                row = pl.multiple_of(position(z, x, c) * count, count)
                copies.append(pltpu.make_async_copy(ref, w.at[pl.ds(row, count)], sems.at[1 + k]))
                copies[-1].start()
            copy_g.wait()
            for copy in copies:
                copy.wait()
            outs = []
            base = ((y + n_y - dy) % n_y) * rows
            for k in range(chunks):
                out[k] = lax.dot_general(
                    g[...],
                    w[pl.ds(k * step, step), :],
                    (((1,), (1,)), ((), ())),
                    preferred_element_type=F32,
                ).astype(BF16)
                column = pl.multiple_of(base + k * step, step)
                outs.append(
                    pltpu.make_async_copy(
                        out.at[k], out_hbm.at[:, pl.ds(column, step)], sems.at[1 + len(pieces) + k]
                    )
                )
                outs[-1].start()
            for copy in outs:
                copy.wait()

        operands = [cotangent] + [piece for _, piece in pieces]
        aliases = {}
        if into is not None:
            operands.append(into)
            aliases = {len(operands) - 1: 0}
        return pl.pallas_call(
            kernel,
            out_shape=shape((tokens, rows * n_y), BF16),
            in_specs=[ANY] * len(operands),
            out_specs=ANY,
            input_output_aliases=aliases,
            scratch_shapes=[
                pltpu.VMEM(cotangent.shape, BF16),
                pltpu.VMEM((rows, width), BF16),
                pltpu.VMEM((chunks, tokens, step), BF16),
                pltpu.SemaphoreType.DMA((1 + len(pieces) + chunks,)),
            ],
            compiler_params=params(24),
            cost_estimate=cost(2 * tokens * rows * width, 2 * (tokens + rows) * width),
        )(*operands)

    def on_device(attn, cotangent, weight, projector, moment_one, moment_two, step_count):
        shard_rows, width = weight.shape
        own_rows = moment_one.shape[0]
        if n_y != 2 or own_rows % 16 or shard_rows % 128 or n_z % 2:
            return plain(attn, cotangent, weight, projector, moment_one, moment_two, step_count)
        z, x, c, y = place()
        q = (x * 2 + z % 2) * 2 + c

        own = to_plane(
            lax.dynamic_slice_in_dim(weight, q * (shard_rows // 8), shard_rows // 8, 0), 0, 1
        )
        over_x = to_plane(own, 1, 0)
        over_z = to_z_pair(own)
        over_xz = to_z_pair(over_x)
        pieces = []
        for dx, dz, piece in ((0, 0, own), (1, 0, over_x), (0, 1, over_z), (1, 1, over_xz)):
            for dc in range(2):
                position = lambda z, x, c, dx=dx, dz=dz, dc=dc: (
                    ((x + dx) % 2) * 2 + (z + dz) % 2
                ) * 2 + (c + dc) % 2
                pieces.append((position, to_core(piece) if dc else piece))

        outgoing, keep = local_sums(attn, projector, cotangent)
        sums = core_sum(keep, to_core(outgoing))
        got = [to_plane(part, dx, dy) for (dx, dy), part in zip(plane, sums[1:])]
        sums = plane_sum(sums[0], got)
        got = [to_z(part, dz) for dz, part in zip(range(1, n_z), sums[1:])]
        first_moment, second_moment, low_step = adam(
            sums[0], got, moment_one, moment_two, step_count
        )
        column = jnp.stack([low_step] + [to_z(low_step, dz) for dz in range(1, n_z)])
        blocks = [(0, 0, 0, column), (1, 0, 0, to_core(column))]
        for dx, dy in plane:
            got = to_plane(column, dx, dy)
            blocks += [(0, dx, dy, got), (1, dx, dy, to_core(got))]
        my_projector = lax.dynamic_slice_in_dim(projector, y * shard_rows, shard_rows, 0)
        weight_step = step_product(my_projector, blocks)

        grad_input = input_product(cotangent, [(lambda z, x, c: 0, weight)], 0)
        grad_input = input_product(cotangent, pieces, 1, grad_input)
        return grad_input, weight_step, first_moment, second_moment

    rows = P(("dp", "fsdp"), None)
    return jax.shard_map(
        on_device,
        mesh=mesh,
        in_specs=(rows, rows, P("fsdp", None), P(), rows, rows, P()),
        out_specs=(rows, P("fsdp", None), rows, rows),
        check_vma=False,
    )
```

time: 317 us -> 93.8 us (0.30)
  waiting for transfers between devices: 263 us -> 31 us
  starting transfers between devices: 0.12 us -> 25.3 us
  Pallas kernels: 0 us -> 23.6 us
  matrix products: 22.1 us -> 0 us
  between operations: 14.5 us -> 1.56 us
  local copies, waits for them, and re-layouts: 15.2 us -> 11.8 us
    all_gather x2 -> x0, waiting for transfers between devices: 162 us -> none  [the longest x1 112 us: on_device(): lax.all_gather(weight, 'fsdp', axis=0, tiled=True)]
    unnamed x4 -> x0, waiting for transfers between devices: 101 us -> none
    ppermute x0 -> x25, waiting for transfers between devices: none -> 31 us  [send(): return lax.ppermute(value, AXES, pairs)]
    ppermute x0 -> x25, starting transfers between devices: none -> 25.3 us  [send(): return lax.ppermute(value, AXES, pairs)]
    pallas_call x0 -> x7, Pallas kernels: none -> 23.6 us  [the longest x2 11.1 us: input_product(): pl.pallas_call(kernel, out_shape=shape((tokens, rows * n_y), BF16), in_sp...]
    dot_general x3 -> x0, matrix products: 22.1 us -> none  [the longest x1 9.16 us: on_device(): lax.dot_general(cotangent, lax.all_gather(weight, 'fsdp', axis=0, tiled=T...]
    unnamed x8 -> x34, local copies, waits for them, and re-layouts: 13.7 us -> 9.7 us
  transfers between devices with their start and end apart: 3 -> 25, of which waited for: 3 -> 13; matrix products, arithmetic and copies ran while one was open for 4% -> 1% of each run, Pallas kernels for 0% -> 18%
where the time goes in v2:
time: 93.8 us; the launch traced here: 93.4 us
  waiting for transfers between devices  31 us (33%)
  starting transfers between devices  25.3 us (27%)
  Pallas kernels  23.6 us (25%)
  local copies, waits for them, and re-layouts  11.8 us (13%)
  between operations  1.56 us (2%)
    ppermute x25, waiting for transfers between devices, send(): return lax.ppermute(value, AXES, pairs)  31 us
    ppermute x25, starting transfers between devices, send(): return lax.ppermute(value, AXES, pairs)  25.3 us
    pallas_call x2, Pallas kernels, input_product(): pl.pallas_call(kernel, out_shape=shape((tokens, rows * n_y), BF16), in_sp...  11.1 us
    unnamed x34, local copies, waits for them, and re-layouts  9.7 us
    pallas_call x1, Pallas kernels, local_sums(): pl.pallas_call(kernel, out_shape=(shape(dims, BF16), shape(dims, F32)), i...  6.16 us
    pallas_call x1, Pallas kernels, step_product(): pl.pallas_call(kernel, out_shape=shape((rows, width), F32), in_specs=[VME...  5.26 us
  transfers between devices with their start and end apart: 25, of which 13 were waited for; matrix products, arithmetic and copies ran while one was open for 1% of the time, Pallas kernels for 18%

profile of v2, /device:TPU:0, one launch (start us, length us, event | category | flops | bytes accessed | tf_op | source)
XLA Modules:
  0.0 93.4 jit_solution(12867556055473032652)
XLA Ops:
  1.8 3.0 %collective-permute-start = (bf16[96,3072]{1,0:T(8,128)(2,1)S(1)}, bf16[96,3072]{1,0:T(8,128)(2,1)}, u32[]{:S(2)}, u32[]{:S(2)}) collective-permute-start(bf16[96,3072]{1,0:T(8,128)(2,1)S(1)} %constant_dynamic-slice_fusion.1), channel_id=1, source_target_pairs={{0,1},{1,0},{2,3},{3,2},{4,5},{5,4},{6,7},{7,6},{8,9},{9,8},{10,11... | collective-permute-start | bytes 1769480 | tf_op jit(solution)/shard_map/ppermute | solution.py:90
  4.8 2.0 %copy-done = bf16[576,3072]{1,0:T(8,128)(2,1)S(1)} copy-done((bf16[576,3072]{1,0:T(8,128)(2,1)S(1)}, bf16[576,3072]{1,0:T(8,128)(2,1)}, u32[]{:S(2)}) %copy-start) | copy-done | bytes 3538968
  6.8 1.5 %copy-done.2 = bf16[576,1536]{1,0:T(8,128)(2,1)S(1)} copy-done((bf16[576,1536]{1,0:T(8,128)(2,1)S(1)}, bf16[576,1536]{1,0:T(8,128)(2,1)}, u32[]{:S(2)}) %copy-start.2) | copy-done | bytes 1769496
  9.5 6.2 %shard_map.104 = (bf16[2,2,4,96,256]{4,3,2,1,0:T(8,128)(2,1)S(1)}, f32[2,2,4,96,256]{4,3,2,1,0:T(8,128)S(1)}) custom-call(bf16[576,1536]{1,0:T(8,128)(2,1)S(1)} %copy-done.2, bf16[1536,256]{1,0:T(8,128)(2,1)S(1)} %copy-done.3, bf16[576,3072]{1,0:T(8,128)(2,1)S(1)} %copy-done), custom_call_target="tpu_custom_call" | custom-call | flops 1358954496 | bytes 10027008 | tf_op jit(solution)/shard_map/pallas_call | solution.py:136
  15.7 2.6 %collective-permute-done.refs_1_ = bf16[96,3072]{1,0:T(8,128)(2,1)} collective-permute-done((bf16[96,3072]{1,0:T(8,128)(2,1)S(1)}, bf16[96,3072]{1,0:T(8,128)(2,1)}, u32[]{:S(2)}, u32[]{:S(2)}) %collective-permute-start) | collective-permute-done | bytes 589856 | tf_op jit(solution)/shard_map/ppermute | solution.py:90
  18.3 1.7 %collective-permute-start.2 = (bf16[96,3072]{1,0:T(8,128)(2,1)}, bf16[96,3072]{1,0:T(8,128)(2,1)}, u32[]{:S(2)}, u32[]{:S(2)}) collective-permute-start(bf16[96,3072]{1,0:T(8,128)(2,1)} %collective-permute-done.refs_1_), channel_id=1, source_target_pairs={{0,4},{1,5},{2,6},{3,7},{4,0},{5,1},{6,2},{7,3},{8,12},{9,13},{10,... | collective-permute-start | bytes 1769480 | tf_op jit(solution)/shard_map/ppermute | solution.py:90
  20.0 1.6 %collective-permute-start.4 = (bf16[96,3072]{1,0:T(8,128)(2,1)}, bf16[96,3072]{1,0:T(8,128)(2,1)}, u32[]{:S(2)}, u32[]{:S(2)}) collective-permute-start(bf16[96,3072]{1,0:T(8,128)(2,1)} %collective-permute-done.refs_1_), channel_id=1, source_target_pairs={{0,8},{1,9},{2,10},{3,11},{4,12},{5,13},{6,14},{7,15},{8,0},{9,1},... | collective-permute-start | bytes 1769480 | tf_op jit(solution)/shard_map/ppermute | solution.py:90
  21.7 1.6 %collective-permute-start.9 = (bf16[4,96,256]{2,1,0:T(8,128)(2,1)S(1)}, bf16[4,96,256]{2,1,0:T(8,128)(2,1)S(1)}, u32[]{:S(2)}, u32[]{:S(2)}) collective-permute-start(bf16[4,96,256]{2,1,0:T(8,128)(2,1)S(1)} %get-tuple-element.20), channel_id=1, source_target_pairs={{0,1},{1,0},{2,3},{3,2},{4,5},{5,4},{6,7},{7,6},{8,9},{9,8},{10,11... | collective-permute-start | bytes 589832 | tf_op jit(solution)/shard_map/ppermute | solution.py:90
  25.3 9.6 %collective-permute-done.2.refs_3_ = bf16[96,3072]{1,0:T(8,128)(2,1)} collective-permute-done((bf16[96,3072]{1,0:T(8,128)(2,1)}, bf16[96,3072]{1,0:T(8,128)(2,1)}, u32[]{:S(2)}, u32[]{:S(2)}) %collective-permute-start.2) | collective-permute-done | bytes 589856 | tf_op jit(solution)/shard_map/ppermute | solution.py:90
  34.9 1.8 %collective-permute-start.6 = (bf16[96,3072]{1,0:T(8,128)(2,1)}, bf16[96,3072]{1,0:T(8,128)(2,1)}, u32[]{:S(2)}, u32[]{:S(2)}) collective-permute-start(bf16[96,3072]{1,0:T(8,128)(2,1)} %collective-permute-done.2.refs_3_), channel_id=1, source_target_pairs={{0,8},{1,9},{2,10},{3,11},{4,12},{5,13},{6,14},{7,15},{8,0},{9,1},... | collective-permute-start | bytes 1769480 | tf_op jit(solution)/shard_map/ppermute | solution.py:90
  36.7 2.3 %collective-permute-done.10.refs_1_ = bf16[4,96,256]{2,1,0:T(8,128)(2,1)S(1)} collective-permute-done((bf16[4,96,256]{2,1,0:T(8,128)(2,1)S(1)}, bf16[4,96,256]{2,1,0:T(8,128)(2,1)S(1)}, u32[]{:S(2)}, u32[]{:S(2)}) %collective-permute-start.10) | collective-permute-done | bytes 196640 | tf_op jit(solution)/shard_map/ppermute | solution.py:90
  39.0 3.3 %collective-permute-done.11.refs_2_ = bf16[4,96,256]{2,1,0:T(8,128)(2,1)S(1)} collective-permute-done((bf16[4,96,256]{2,1,0:T(8,128)(2,1)S(1)}, bf16[4,96,256]{2,1,0:T(8,128)(2,1)S(1)}, u32[]{:S(2)}, u32[]{:S(2)}) %collective-permute-start.11) | collective-permute-done | bytes 196640 | tf_op jit(solution)/shard_map/ppermute | solution.py:90
  42.4 1.6 %collective-permute-start.12 = (bf16[96,256]{1,0:T(8,128)(2,1)S(1)}, bf16[96,256]{1,0:T(8,128)(2,1)S(1)}, u32[]{:S(2)}, u32[]{:S(2)}) collective-permute-start(bf16[96,256]{1,0:T(8,128)(2,1)S(1)} %get-tuple-element.24), channel_id=1, source_target_pairs={{0,8},{1,9},{2,10},{3,11},{4,12},{5,13},{6,14},{7,15},{8,16},{9,17... | collective-permute-start | bytes 147464 | tf_op jit(solution)/shard_map/ppermute | solution.py:90
  44.0 2.6 %collective-permute-start.13 = (bf16[96,256]{1,0:T(8,128)(2,1)S(1)}, bf16[96,256]{1,0:T(8,128)(2,1)S(1)}, u32[]{:S(2)}, u32[]{:S(2)}) collective-permute-start(bf16[96,256]{1,0:T(8,128)(2,1)S(1)} %get-tuple-element.25), channel_id=1, source_target_pairs={{0,16},{1,17},{2,18},{3,19},{4,20},{5,21},{6,22},{7,23},{8,24},{9,... | collective-permute-start | bytes 147464 | tf_op jit(solution)/shard_map/ppermute | solution.py:90
  48.6 2.4 %collective-permute-done.12.refs_0_ = bf16[96,256]{1,0:T(8,128)(2,1)S(1)} collective-permute-done((bf16[96,256]{1,0:T(8,128)(2,1)S(1)}, bf16[96,256]{1,0:T(8,128)(2,1)S(1)}, u32[]{:S(2)}, u32[]{:S(2)}) %collective-permute-start.12) | collective-permute-done | bytes 49184 | tf_op jit(solution)/shard_map/ppermute | solution.py:90
  52.1 2.6 %collective-permute-start.17 = (bf16[96,256]{1,0:T(8,128)(2,1)S(1)}, bf16[96,256]{1,0:T(8,128)(2,1)S(1)}, u32[]{:S(2)}, u32[]{:S(2)}) collective-permute-start(bf16[96,256]{1,0:T(8,128)(2,1)S(1)} %get-tuple-element.27), channel_id=1, source_target_pairs={{0,24},{1,25},{2,26},{3,27},{4,28},{5,29},{6,30},{7,31},{8,0},{9,1... | collective-permute-start | bytes 147464 | tf_op jit(solution)/shard_map/ppermute | solution.py:90
  56.7 3.0 %collective-permute-done.16 = bf16[96,256]{1,0:T(8,128)(2,1)S(1)} collective-permute-done((bf16[96,256]{1,0:T(8,128)(2,1)S(1)}, bf16[96,256]{1,0:T(8,128)(2,1)S(1)}, u32[]{:S(2)}, u32[]{:S(2)}) %collective-permute-start.16) | collective-permute-done | bytes 49184 | tf_op jit(solution)/shard_map/ppermute | solution.py:90
  60.6 2.0 %collective-permute-start.23 = (bf16[4,96,256]{2,1,0:T(8,128)(2,1)S(1)}, bf16[4,96,256]{2,1,0:T(8,128)(2,1)S(1)}, u32[]{:S(2)}, u32[]{:S(2)}) collective-permute-start(bf16[4,96,256]{2,1,0:T(8,128)(2,1)S(1)} %pad_maximum_fusion.refs_0_), channel_id=1, source_target_pairs={{0,5},{1,4},{2,7},{3,6},{4,1},{5,0},{6,3},{7,2},{8,13},{9,12},{10,... | collective-permute-start | bytes 589832 | tf_op jit(solution)/shard_map/ppermute | solution.py:90
  64.9 2.4 %collective-permute-done.23.refs_6_ = bf16[4,96,256]{2,1,0:T(8,128)(2,1)S(1)} collective-permute-done((bf16[4,96,256]{2,1,0:T(8,128)(2,1)S(1)}, bf16[4,96,256]{2,1,0:T(8,128)(2,1)S(1)}, u32[]{:S(2)}, u32[]{:S(2)}) %collective-permute-start.23) | collective-permute-done | bytes 196640 | tf_op jit(solution)/shard_map/ppermute | solution.py:90
  72.9 1.6 %collective-permute-done.22.refs_5_ = bf16[4,96,256]{2,1,0:T(8,128)(2,1)} collective-permute-done((bf16[4,96,256]{2,1,0:T(8,128)(2,1)}, bf16[4,96,256]{2,1,0:T(8,128)(2,1)}, u32[]{:S(2)}, u32[]{:S(2)}) %collective-permute-start.22) | collective-permute-done | bytes 196640 | tf_op jit(solution)/shard_map/ppermute | solution.py:90
  74.6 2.3 %copy-done.16 = bf16[768,3072]{1,0:T(8,128)(2,1)S(1)} copy-done((bf16[768,3072]{1,0:T(8,128)(2,1)S(1)}, bf16[768,3072]{1,0:T(8,128)(2,1)}, u32[]{:S(2)}) %copy-start.16) | copy-done | bytes 4718616
  76.9 4.5 %shard_map.102.refs_9_ = bf16[576,1536]{1,0:T(8,128)(2,1)} custom-call(bf16[576,3072]{1,0:T(8,128)(2,1)S(1)} %copy-done.1, bf16[768,3072]{1,0:T(8,128)(2,1)S(1)} %copy-done.16), custom_call_target="tpu_custom_call" | custom-call | flops 2717908992 | bytes 8257536 | tf_op jit(solution)/shard_map/pallas_call | solution.py:311
  81.5 5.3 %shard_map.108 = f32[768,3072]{1,0:T(8,128)} custom-call(bf16[768,256]{1,0:T(8,128)(2,1)S(1)} %constant_dynamic-slice_fusion.p_ref, bf16[4,96,256]{2,1,0:T(8,128)(2,1)S(1)} %copy-done.5, bf16[4,96,256]{2,1,0:T(8,128)(2,1)S(1)} %copy-done.11, bf16[4,96,256]{2,1,0:T(8,128)(2,1)S(1)} %copy-done.9, bf16[4,96,256]{2,1,0:T(8,128)(2,1)S(1)} %collective-permute-done.20.refs_3_, ...), custom_call_target="tpu_custom_call" | custom-call | flops 1207959552 | bytes 9437184 | tf_op jit(solution)/shard_map/pallas_call | solution.py:252
  86.8 6.6 %shard_map.103 = bf16[576,1536]{1,0:T(8,128)(2,1)} custom-call(bf16[576,3072]{1,0:T(8,128)(2,1)S(1)} %copy-done.1, bf16[96,3072]{1,0:T(8,128)(2,1)} %collective-permute-done.refs_1_, bf16[96,3072]{1,0:T(8,128)(2,1)} %collective-permute-done.1.refs_2_, bf16[96,3072]{1,0:T(8,128)(2,1)} %collective-permute-done.2.refs_3_, ...), custom_call_target="tpu_custom_call", output_to_operand_aliasing={{}: (9, {})} | custom-call | flops 2717908992 | bytes 8257536 | tf_op jit(solution)/shard_map/pallas_call | solution.py:311
  (70 shorter events, 17.8 us)
Async XLA Ops:
  1.8 16.5 %collective-permute-start = (bf16[96,3072]{1,0:T(8,128)(2,1)S(1)}, bf16[96,3072]{1,0:T(8,128)(2,1)}, u32[]{:S(2)}, u32[]{:S(2)}) collective-permute-start(bf16[96,3072]{1,0:T(8,128)(2,1)S(1)} %constant_dynamic-slice_fusion.1), channel_id=1, source_target_pairs={{0,1},{1,0},{2,3},{3,2},{4,5},{5,4},{6,7},{7,6},{8,9},{9,8},{10,11... | collective-permute-start | bytes 1769480 | tf_op jit(solution)/shard_map/ppermute | solution.py:90
  15.6 5.9 %collective-permute-start.8 = (bf16[2,2,4,96,256]{4,3,2,1,0:T(8,128)(2,1)S(1)}, bf16[2,2,4,96,256]{4,3,2,1,0:T(8,128)(2,1)S(1)}, u32[]{:S(2)}, u32[]{:S(2)}) collective-permute-start(bf16[2,2,4,96,256]{4,3,2,1,0:T(8,128)(2,1)S(1)} %get-tuple-element.18), channel_id=1, source_target_pairs={{0,2},{1,3},{2,0},{3,1},{4,6},{5,7},{6,4},{7,5},{8,10},{9,11},{10,... | collective-permute-start | bytes 2359304 | tf_op jit(solution)/shard_map/ppermute | solution.py:90
  18.3 16.6 %collective-permute-start.2 = (bf16[96,3072]{1,0:T(8,128)(2,1)}, bf16[96,3072]{1,0:T(8,128)(2,1)}, u32[]{:S(2)}, u32[]{:S(2)}) collective-permute-start(bf16[96,3072]{1,0:T(8,128)(2,1)} %collective-permute-done.refs_1_), channel_id=1, source_target_pairs={{0,4},{1,5},{2,6},{3,7},{4,0},{5,1},{6,2},{7,3},{8,12},{9,13},{10,... | collective-permute-start | bytes 1769480 | tf_op jit(solution)/shard_map/ppermute | solution.py:90
  20.0 44.2 %collective-permute-start.4 = (bf16[96,3072]{1,0:T(8,128)(2,1)}, bf16[96,3072]{1,0:T(8,128)(2,1)}, u32[]{:S(2)}, u32[]{:S(2)}) collective-permute-start(bf16[96,3072]{1,0:T(8,128)(2,1)} %collective-permute-done.refs_1_), channel_id=1, source_target_pairs={{0,8},{1,9},{2,10},{3,11},{4,12},{5,13},{6,14},{7,15},{8,0},{9,1},... | collective-permute-start | bytes 1769480 | tf_op jit(solution)/shard_map/ppermute | solution.py:90
  21.7 15.0 %collective-permute-start.9 = (bf16[4,96,256]{2,1,0:T(8,128)(2,1)S(1)}, bf16[4,96,256]{2,1,0:T(8,128)(2,1)S(1)}, u32[]{:S(2)}, u32[]{:S(2)}) collective-permute-start(bf16[4,96,256]{2,1,0:T(8,128)(2,1)S(1)} %get-tuple-element.20), channel_id=1, source_target_pairs={{0,1},{1,0},{2,3},{3,2},{4,5},{5,4},{6,7},{7,6},{8,9},{9,8},{10,11... | collective-permute-start | bytes 589832 | tf_op jit(solution)/shard_map/ppermute | solution.py:90
  23.3 15.7 %collective-permute-start.10 = (bf16[4,96,256]{2,1,0:T(8,128)(2,1)S(1)}, bf16[4,96,256]{2,1,0:T(8,128)(2,1)S(1)}, u32[]{:S(2)}, u32[]{:S(2)}) collective-permute-start(bf16[4,96,256]{2,1,0:T(8,128)(2,1)S(1)} %get-tuple-element.21), channel_id=1, source_target_pairs={{0,4},{1,5},{2,6},{3,7},{4,0},{5,1},{6,2},{7,3},{8,12},{9,13},{10,... | collective-permute-start | bytes 589832 | tf_op jit(solution)/shard_map/ppermute | solution.py:90
  23.8 18.5 %collective-permute-start.11 = (bf16[4,96,256]{2,1,0:T(8,128)(2,1)S(1)}, bf16[4,96,256]{2,1,0:T(8,128)(2,1)S(1)}, u32[]{:S(2)}, u32[]{:S(2)}) collective-permute-start(bf16[4,96,256]{2,1,0:T(8,128)(2,1)S(1)} %get-tuple-element.22), channel_id=1, source_target_pairs={{0,5},{1,4},{2,7},{3,6},{4,1},{5,0},{6,3},{7,2},{8,13},{9,12},{10,... | collective-permute-start | bytes 589832 | tf_op jit(solution)/shard_map/ppermute | solution.py:90
  34.9 35.7 %collective-permute-start.6 = (bf16[96,3072]{1,0:T(8,128)(2,1)}, bf16[96,3072]{1,0:T(8,128)(2,1)}, u32[]{:S(2)}, u32[]{:S(2)}) collective-permute-start(bf16[96,3072]{1,0:T(8,128)(2,1)} %collective-permute-done.2.refs_3_), channel_id=1, source_target_pairs={{0,8},{1,9},{2,10},{3,11},{4,12},{5,13},{6,14},{7,15},{8,0},{9,1},... | collective-permute-start | bytes 1769480 | tf_op jit(solution)/shard_map/ppermute | solution.py:90
  42.4 8.6 %collective-permute-start.12 = (bf16[96,256]{1,0:T(8,128)(2,1)S(1)}, bf16[96,256]{1,0:T(8,128)(2,1)S(1)}, u32[]{:S(2)}, u32[]{:S(2)}) collective-permute-start(bf16[96,256]{1,0:T(8,128)(2,1)S(1)} %get-tuple-element.24), channel_id=1, source_target_pairs={{0,8},{1,9},{2,10},{3,11},{4,12},{5,13},{6,14},{7,15},{8,16},{9,17... | collective-permute-start | bytes 147464 | tf_op jit(solution)/shard_map/ppermute | solution.py:90
  44.0 7.0 %collective-permute-start.13 = (bf16[96,256]{1,0:T(8,128)(2,1)S(1)}, bf16[96,256]{1,0:T(8,128)(2,1)S(1)}, u32[]{:S(2)}, u32[]{:S(2)}) collective-permute-start(bf16[96,256]{1,0:T(8,128)(2,1)S(1)} %get-tuple-element.25), channel_id=1, source_target_pairs={{0,16},{1,17},{2,18},{3,19},{4,20},{5,21},{6,22},{7,23},{8,24},{9,... | collective-permute-start | bytes 147464 | tf_op jit(solution)/shard_map/ppermute | solution.py:90
  46.6 4.6 %collective-permute-start.14 = (bf16[96,256]{1,0:T(8,128)(2,1)S(1)}, bf16[96,256]{1,0:T(8,128)(2,1)S(1)}, u32[]{:S(2)}, u32[]{:S(2)}) collective-permute-start(bf16[96,256]{1,0:T(8,128)(2,1)S(1)} %get-tuple-element.26), channel_id=1, source_target_pairs={{0,24},{1,25},{2,26},{3,27},{4,28},{5,29},{6,30},{7,31},{8,0},{9,1... | collective-permute-start | bytes 147464 | tf_op jit(solution)/shard_map/ppermute | solution.py:90
  52.1 4.6 %collective-permute-start.17 = (bf16[96,256]{1,0:T(8,128)(2,1)S(1)}, bf16[96,256]{1,0:T(8,128)(2,1)S(1)}, u32[]{:S(2)}, u32[]{:S(2)}) collective-permute-start(bf16[96,256]{1,0:T(8,128)(2,1)S(1)} %get-tuple-element.27), channel_id=1, source_target_pairs={{0,24},{1,25},{2,26},{3,27},{4,28},{5,29},{6,30},{7,31},{8,0},{9,1... | collective-permute-start | bytes 147464 | tf_op jit(solution)/shard_map/ppermute | solution.py:90
  54.7 5.0 %collective-permute-start.16 = (bf16[96,256]{1,0:T(8,128)(2,1)S(1)}, bf16[96,256]{1,0:T(8,128)(2,1)S(1)}, u32[]{:S(2)}, u32[]{:S(2)}) collective-permute-start(bf16[96,256]{1,0:T(8,128)(2,1)S(1)} %get-tuple-element.27), channel_id=1, source_target_pairs={{0,16},{1,17},{2,18},{3,19},{4,20},{5,21},{6,22},{7,23},{8,24},{9,... | collective-permute-start | bytes 147464 | tf_op jit(solution)/shard_map/ppermute | solution.py:90
  54.7 5.9 %collective-permute-start.15 = (bf16[96,256]{1,0:T(8,128)(2,1)S(1)}, bf16[96,256]{1,0:T(8,128)(2,1)S(1)}, u32[]{:S(2)}, u32[]{:S(2)}) collective-permute-start(bf16[96,256]{1,0:T(8,128)(2,1)S(1)} %get-tuple-element.27), channel_id=1, source_target_pairs={{0,8},{1,9},{2,10},{3,11},{4,12},{5,13},{6,14},{7,15},{8,16},{9,17... | collective-permute-start | bytes 147464 | tf_op jit(solution)/shard_map/ppermute | solution.py:90
  60.6 6.7 %collective-permute-start.23 = (bf16[4,96,256]{2,1,0:T(8,128)(2,1)S(1)}, bf16[4,96,256]{2,1,0:T(8,128)(2,1)S(1)}, u32[]{:S(2)}, u32[]{:S(2)}) collective-permute-start(bf16[4,96,256]{2,1,0:T(8,128)(2,1)S(1)} %pad_maximum_fusion.refs_0_), channel_id=1, source_target_pairs={{0,5},{1,4},{2,7},{3,6},{4,1},{5,0},{6,3},{7,2},{8,13},{9,12},{10,... | collective-permute-start | bytes 589832 | tf_op jit(solution)/shard_map/ppermute | solution.py:90
  62.6 6.7 %collective-permute-start.21 = (bf16[4,96,256]{2,1,0:T(8,128)(2,1)S(1)}, bf16[4,96,256]{2,1,0:T(8,128)(2,1)}, u32[]{:S(2)}, u32[]{:S(2)}) collective-permute-start(bf16[4,96,256]{2,1,0:T(8,128)(2,1)S(1)} %pad_maximum_fusion.refs_0_), channel_id=1, source_target_pairs={{0,4},{1,5},{2,6},{3,7},{4,0},{5,1},{6,2},{7,3},{8,12},{9,13},{10,... | collective-permute-start | bytes 589832 | tf_op jit(solution)/shard_map/ppermute | solution.py:90
  63.4 6.0 %collective-permute-start.19 = (bf16[4,96,256]{2,1,0:T(8,128)(2,1)S(1)}, bf16[4,96,256]{2,1,0:T(8,128)(2,1)S(1)}, u32[]{:S(2)}, u32[]{:S(2)}) collective-permute-start(bf16[4,96,256]{2,1,0:T(8,128)(2,1)S(1)} %pad_maximum_fusion.refs_0_), channel_id=1, source_target_pairs={{0,1},{1,0},{2,3},{3,2},{4,5},{5,4},{6,7},{7,6},{8,9},{9,8},{10,11... | collective-permute-start | bytes 589832 | tf_op jit(solution)/shard_map/ppermute | solution.py:90
  64.2 5.6 %collective-permute-start.18 = (bf16[4,96,256]{2,1,0:T(8,128)(2,1)S(1)}, bf16[4,96,256]{2,1,0:T(8,128)(2,1)S(1)}, u32[]{:S(2)}, u32[]{:S(2)}) collective-permute-start(bf16[4,96,256]{2,1,0:T(8,128)(2,1)S(1)} %pad_maximum_fusion.refs_0_), channel_id=1, source_target_pairs={{0,2},{1,3},{2,0},{3,1},{4,6},{5,7},{6,4},{7,5},{8,10},{9,11},{10,... | collective-permute-start | bytes 589832 | tf_op jit(solution)/shard_map/ppermute | solution.py:90
  67.3 3.7 %collective-permute-start.24 = (bf16[4,96,256]{2,1,0:T(8,128)(2,1)S(1)}, bf16[4,96,256]{2,1,0:T(8,128)(2,1)S(1)}, u32[]{:S(2)}, u32[]{:S(2)}) collective-permute-start(bf16[4,96,256]{2,1,0:T(8,128)(2,1)S(1)} %collective-permute-done.23.refs_6_), channel_id=1, source_target_pairs={{0,2},{1,3},{2,0},{3,1},{4,6},{5,7},{6,4},{7,5},{8,10},{9,11},{10,... | collective-permute-start | bytes 589832 | tf_op jit(solution)/shard_map/ppermute | solution.py:90
  69.3 17.5 %collective-permute-start.1 = (bf16[96,3072]{1,0:T(8,128)(2,1)}, bf16[96,3072]{1,0:T(8,128)(2,1)}, u32[]{:S(2)}, u32[]{:S(2)}) collective-permute-start(bf16[96,3072]{1,0:T(8,128)(2,1)} %collective-permute-done.refs_1_), channel_id=1, source_target_pairs={{0,2},{1,3},{2,0},{3,1},{4,6},{5,7},{6,4},{7,5},{8,10},{9,11},{10,... | collective-permute-start | bytes 1769480 | tf_op jit(solution)/shard_map/ppermute | solution.py:90
  69.4 17.4 %collective-permute-start.3 = (bf16[96,3072]{1,0:T(8,128)(2,1)}, bf16[96,3072]{1,0:T(8,128)(2,1)}, u32[]{:S(2)}, u32[]{:S(2)}) collective-permute-start(bf16[96,3072]{1,0:T(8,128)(2,1)} %collective-permute-done.2.refs_3_), channel_id=1, source_target_pairs={{0,2},{1,3},{2,0},{3,1},{4,6},{5,7},{6,4},{7,5},{8,10},{9,11},{10,... | collective-permute-start | bytes 1769480 | tf_op jit(solution)/shard_map/ppermute | solution.py:90
  70.5 16.3 %collective-permute-start.5 = (bf16[96,3072]{1,0:T(8,128)(2,1)}, bf16[96,3072]{1,0:T(8,128)(2,1)}, u32[]{:S(2)}, u32[]{:S(2)}) collective-permute-start(bf16[96,3072]{1,0:T(8,128)(2,1)} %collective-permute-done.4.refs_5_), channel_id=1, source_target_pairs={{0,2},{1,3},{2,0},{3,1},{4,6},{5,7},{6,4},{7,5},{8,10},{9,11},{10,... | collective-permute-start | bytes 1769480 | tf_op jit(solution)/shard_map/ppermute | solution.py:90
  70.6 16.2 %collective-permute-start.7 = (bf16[96,3072]{1,0:T(8,128)(2,1)}, bf16[96,3072]{1,0:T(8,128)(2,1)}, u32[]{:S(2)}, u32[]{:S(2)}) collective-permute-start(bf16[96,3072]{1,0:T(8,128)(2,1)} %collective-permute-done.6.refs_7_), channel_id=1, source_target_pairs={{0,2},{1,3},{2,0},{3,1},{4,6},{5,7},{6,4},{7,5},{8,10},{9,11},{10,... | collective-permute-start | bytes 1769480 | tf_op jit(solution)/shard_map/ppermute | solution.py:90
  74.4 7.0 %collective-permute-start.20 = (bf16[4,96,256]{2,1,0:T(8,128)(2,1)}, bf16[4,96,256]{2,1,0:T(8,128)(2,1)S(1)}, u32[]{:S(2)}, u32[]{:S(2)}) collective-permute-start(bf16[4,96,256]{2,1,0:T(8,128)(2,1)} %copy-done.8), channel_id=1, source_target_pairs={{0,2},{1,3},{2,0},{3,1},{4,6},{5,7},{6,4},{7,5},{8,10},{9,11},{10,... | collective-permute-start | bytes 589832 | tf_op jit(solution)/shard_map/ppermute | solution.py:90
  (18 other events, 199.6 us)

commit v3 on v2

--- a/solution.py
+++ b/solution.py
@@ -11,6 +11,7 @@
 VMEM = pl.BlockSpec(memory_space=pltpu.VMEM)
 SMEM = pl.BlockSpec(memory_space=pltpu.SMEM)
 ANY = pl.BlockSpec(memory_space=pl.ANY)
+HBM = pl.BlockSpec(memory_space=pltpu.HBM)
 
 
 def shape(dims, dtype):
@@ -18,11 +19,11 @@
 
 
 def params(mib):
-    return pltpu.CompilerParams(vmem_limit_bytes=mib * MIB)
+    return pltpu.CompilerParams(vmem_limit_bytes=int(mib * MIB))
 
 
 def cost(flops, nbytes):
-    return pl.CostEstimate(flops=int(flops), bytes_accessed=int(nbytes), transcendentals=0)
+    return pl.CostEstimate(flops=0, bytes_accessed=0, transcendentals=0)
 
 
 def place():
@@ -136,7 +137,7 @@
         return pl.pallas_call(
             kernel,
             out_shape=(shape(dims, BF16), shape(dims, F32)),
-            in_specs=[ANY, ANY, ANY],
+            in_specs=[HBM, HBM, HBM],
             out_specs=(VMEM, VMEM),
             scratch_shapes=[
                 pltpu.VMEM(attn.shape, BF16),
@@ -146,7 +147,7 @@
                 pltpu.VMEM((2, rows, rank), F32),
                 pltpu.SemaphoreType.DMA((2 + groups,)),
             ],
-            compiler_params=params(24),
+            compiler_params=params(50),
             cost_estimate=cost(
                 2 * tokens * rank * (inner + width), 2 * tokens * (inner + width) + 6 * width * rank
             ),
@@ -171,11 +172,14 @@
             cost_estimate=cost(keep.size, 8 * keep.size),
         )(keep, got)
 
-    def plane_sum(own, got):
+    def plane_sum(own, got, parts, wait):
         slab = own.shape[1:]
+        rows, width = sum(part.shape[0] for part in parts), parts[0].shape[1]
 
         def kernel(own_ref, *refs):
-            got_refs, out_ref, send_refs = refs[: len(got)], refs[len(got)], refs[len(got) + 1 :]
+            got_refs, part_refs = refs[: len(got)], refs[len(got) : len(got) + len(parts)]
+            out_ref, send_refs = refs[-2 - n_z], refs[-1 - n_z : -2]
+            full_ref, half_ref = refs[-2:]
             z, x, c, y = place()
             for dz in range(n_z):
                 tz = (z + dz) % n_z
@@ -186,19 +190,30 @@
                     out_ref[...] = total
                 else:
                     send_refs[dz - 1][...] = total.astype(BF16)
-
-        return pl.pallas_call(
-            kernel,
-            out_shape=(shape(slab, F32),) + (shape(slab, BF16),) * (n_z - 1),
-            in_specs=[VMEM] * (1 + len(got)),
-            out_specs=(VMEM,) * n_z,
+            begin = 0
+            for ref in part_refs:
+                full_ref[begin : begin + ref.shape[0], :] = ref[...]
+                begin += ref.shape[0]
+            half_ref[...] = full_ref[: rows // 2, :]
+
+        return pl.pallas_call(
+            kernel,
+            out_shape=(shape(slab, F32),)
+            + (shape(slab, BF16),) * (n_z - 1)
+            + (shape((rows, width), BF16), shape((rows // 2, width), BF16)),
+            in_specs=[VMEM] * (1 + len(got) + len(parts)) + [ANY] * len(wait),
+            out_specs=(VMEM,) * (n_z + 2),
             compiler_params=params(8),
             cost_estimate=cost(4 * own.size, 10 * own.size),
-        )(own, *got)
-
-    def adam(own, got, moment_one, moment_two, step_count):
+        )(own, *got, *parts, *wait)
+
+    def adam(own, got, moment_one, moment_two, step_count, full, wait):
+        half = full.shape[0] // 2
+
         def kernel(step_ref, own_ref, *refs):
-            got_refs, (m1, m2, first_ref, second_ref, low_ref) = refs[: len(got)], refs[len(got) :]
+            got_refs, (m1, m2, full_ref, wait_ref) = refs[: len(got)], refs[len(got) : -4]
+            first_ref, second_ref, low_ref, half_ref = refs[-4:]
+            half_ref[...] = full_ref[half:, :]
             projected = own_ref[...]
             for ref in got_refs:
                 projected = projected + ref[...].astype(F32)
@@ -215,12 +230,17 @@
         dims = own.shape
         return pl.pallas_call(
             kernel,
-            out_shape=(shape(dims, F32), shape(dims, F32), shape(dims, BF16)),
-            in_specs=[SMEM] + [VMEM] * (3 + len(got)),
-            out_specs=(VMEM, VMEM, VMEM),
+            out_shape=(
+                shape(dims, F32),
+                shape(dims, F32),
+                shape(dims, BF16),
+                shape((half, full.shape[1]), BF16),
+            ),
+            in_specs=[SMEM] + [VMEM] * (4 + len(got)) + [ANY],
+            out_specs=(VMEM,) * 4,
             compiler_params=params(4),
             cost_estimate=cost(20 * own.size, 24 * own.size),
-        )(step_count, own, *got, moment_one, moment_two)
+        )(step_count, own, *got, moment_one, moment_two, full, wait)
 
     def step_product(my_projector, blocks):
         rows, rank = my_projector.shape
@@ -253,117 +273,203 @@
             kernel,
             out_shape=shape((rows, width), F32),
             in_specs=[VMEM] * (1 + len(blocks)),
-            out_specs=ANY,
+            out_specs=HBM,
             scratch_shapes=[
                 pltpu.VMEM((groups, span, rank), BF16),
                 pltpu.VMEM((groups, rows, span), F32),
                 pltpu.SemaphoreType.DMA((groups,)),
             ],
-            compiler_params=params(24),
+            compiler_params=params(16),
             cost_estimate=cost(2 * rows * rank * width, 4 * rows * width),
         )(my_projector, *[block[3] for block in blocks])
 
-    def input_product(cotangent, pieces, dy, into=None):
+    def own_product(cotangent, weight, wait):
+        tokens, width = cotangent.shape
+        rows = weight.shape[0]
+        step = 256
+        chunks = rows // step
+
+        def kernel(g_hbm, w_hbm, wait_ref, out_hbm, done_ref, g, w, out, sems):
+            y = lax.axis_index("fsdp")
+            copy_g = pltpu.make_async_copy(g_hbm, g, sems.at[0])
+            copy_g.start()
+            copies = []
+            for k in range(chunks):
+                copies.append(
+                    pltpu.make_async_copy(
+                        w_hbm.at[pl.ds(k * step, step), :], w.at[k], sems.at[1 + k]
+                    )
+                )
+                copies[-1].start()
+            done_ref[...] = jnp.zeros_like(done_ref)
+            copy_g.wait()
+            outs = []
+            for k in range(chunks):
+                copies[k].wait()
+                out[k] = lax.dot_general(
+                    g[...], w[k], (((1,), (1,)), ((), ())), preferred_element_type=F32
+                ).astype(BF16)
+                column = pl.multiple_of(y * rows + k * step, step)
+                outs.append(
+                    pltpu.make_async_copy(
+                        out.at[k], out_hbm.at[:, pl.ds(column, step)], sems.at[1 + chunks + k]
+                    )
+                )
+                outs[-1].start()
+            for copy in outs:
+                copy.wait()
+
+        return pl.pallas_call(
+            kernel,
+            out_shape=(shape((tokens, rows * n_y), BF16), shape((8, 128), F32)),
+            in_specs=[HBM, HBM, ANY],
+            out_specs=(HBM, VMEM),
+            scratch_shapes=[
+                pltpu.VMEM((tokens, width), BF16),
+                pltpu.VMEM((chunks, step, width), BF16),
+                pltpu.VMEM((chunks, tokens, step), BF16),
+                pltpu.SemaphoreType.DMA((1 + 2 * chunks,)),
+            ],
+            compiler_params=params(50),
+            cost_estimate=cost(2 * tokens * rows * width, 2 * (tokens + rows) * width),
+        )(cotangent, weight, wait)
+
+    def stack(values, *wait):
+        def kernel(*refs):
+            for k in range(len(values)):
+                refs[-1][k] = refs[k][...]
+
+        return pl.pallas_call(
+            kernel,
+            out_shape=shape((len(values),) + values[0].shape, values[0].dtype),
+            in_specs=[VMEM] * len(values) + [ANY] * len(wait),
+            out_specs=VMEM,
+            compiler_params=params(4),
+            cost_estimate=cost(0, 2 * values[0].size),
+        )(*values, *wait)
+
+    def relay(value, *wait):
+        def kernel(ref, *refs):
+            refs[-1][...] = ref[...]
+
+        return pl.pallas_call(
+            kernel,
+            out_shape=shape(value.shape, value.dtype),
+            in_specs=[VMEM] + [ANY] * len(wait),
+            out_specs=VMEM,
+            compiler_params=params(4),
+            cost_estimate=cost(0, 2 * value.size),
+        )(value, *wait)
+
+    def other_product(cotangent, pieces, into):
         tokens, width = cotangent.shape
         rows = sum(piece.shape[0] for _, piece in pieces)
         step = 256 if rows % 256 == 0 else 128
         chunks = rows // step
 
-        def kernel(*refs):
-            g_hbm, w_hbm = refs[0], refs[1 : 1 + len(pieces)]
-            out_hbm, g, w, out, sems = refs[-5:]
+        def kernel(g_ref, *refs):
+            w_refs = refs[: len(pieces)]
+            out_hbm, w, out, sems = refs[-4:]
             z, x, c, y = place()
-            copy_g = pltpu.make_async_copy(g_hbm, g, sems.at[0])
-            copy_g.start()
             copies = []
-            for k, ((position, piece), ref) in enumerate(zip(pieces, w_hbm)):
+            for k, ((first, piece), ref) in enumerate(zip(pieces, w_refs)):
                 count = piece.shape[0]
-                row = pl.multiple_of(position(z, x, c) * count, count)
-                copies.append(pltpu.make_async_copy(ref, w.at[pl.ds(row, count)], sems.at[1 + k]))
+                row = pl.multiple_of(first(z, x, c), 16)
+                copies.append(pltpu.make_async_copy(ref, w.at[pl.ds(row, count)], sems.at[k]))
                 copies[-1].start()
-            copy_g.wait()
             for copy in copies:
                 copy.wait()
             outs = []
-            base = ((y + n_y - dy) % n_y) * rows
             for k in range(chunks):
                 out[k] = lax.dot_general(
-                    g[...],
+                    g_ref[...],
                     w[pl.ds(k * step, step), :],
                     (((1,), (1,)), ((), ())),
                     preferred_element_type=F32,
                 ).astype(BF16)
-                column = pl.multiple_of(base + k * step, step)
+                column = pl.multiple_of((1 - y) * rows + k * step, step)
                 outs.append(
                     pltpu.make_async_copy(
-                        out.at[k], out_hbm.at[:, pl.ds(column, step)], sems.at[1 + len(pieces) + k]
+                        out.at[k], out_hbm.at[:, pl.ds(column, step)], sems.at[len(pieces) + k]
                     )
                 )
                 outs[-1].start()
             for copy in outs:
                 copy.wait()
 
-        operands = [cotangent] + [piece for _, piece in pieces]
-        aliases = {}
-        if into is not None:
-            operands.append(into)
-            aliases = {len(operands) - 1: 0}
-        return pl.pallas_call(
-            kernel,
-            out_shape=shape((tokens, rows * n_y), BF16),
-            in_specs=[ANY] * len(operands),
-            out_specs=ANY,
-            input_output_aliases=aliases,
+        return pl.pallas_call(
+            kernel,
+            out_shape=shape(into.shape, BF16),
+            in_specs=[VMEM] + [ANY] * len(pieces) + [HBM],
+            out_specs=HBM,
+            input_output_aliases={1 + len(pieces): 0},
             scratch_shapes=[
-                pltpu.VMEM(cotangent.shape, BF16),
                 pltpu.VMEM((rows, width), BF16),
                 pltpu.VMEM((chunks, tokens, step), BF16),
-                pltpu.SemaphoreType.DMA((1 + len(pieces) + chunks,)),
+                pltpu.SemaphoreType.DMA((len(pieces) + chunks,)),
             ],
-            compiler_params=params(24),
+            compiler_params=params(8),
             cost_estimate=cost(2 * tokens * rows * width, 2 * (tokens + rows) * width),
-        )(*operands)
+        )(cotangent, *[piece for _, piece in pieces], into)
 
     def on_device(attn, cotangent, weight, projector, moment_one, moment_two, step_count):
         shard_rows, width = weight.shape
         own_rows = moment_one.shape[0]
-        if n_y != 2 or own_rows % 16 or shard_rows % 128 or n_z % 2:
+        if n_y != 2 or own_rows % 16 or shard_rows % 384 or n_z % 2:
             return plain(attn, cotangent, weight, projector, moment_one, moment_two, step_count)
         z, x, c, y = place()
         q = (x * 2 + z % 2) * 2 + c
 
-        own = to_plane(
-            lax.dynamic_slice_in_dim(weight, q * (shard_rows // 8), shard_rows // 8, 0), 0, 1
+        eighth = shard_rows // 8
+        cut = eighth // 48 * 16
+        cuts = ((0, cut), (cut, eighth - cut))
+
+        def mine(part):
+            begin, count = cuts[part]
+            return lax.dynamic_slice_in_dim(weight, q * eighth + begin, count, 0)
+
+        outgoing, keep = local_sums(attn, projector, cotangent)
+        over_y = [to_plane(mine(0), 0, 1)]
+        over_y.append(to_plane(relay(mine(1), over_y[0]), 0, 1))
+        sums = core_sum(keep, to_core(relay(outgoing, over_y[0])))
+        over_z = [to_z_pair(over_y[0])]
+
+        got = [to_plane(part, dx, dy) for (dx, dy), part in zip(plane, sums[1:])]
+        grad_input, done = own_product(cotangent, weight, sums[1])
+        over_y[1] = relay(over_y[1], done)
+        over_z.append(to_z_pair(over_y[1]))
+        sums = plane_sum(sums[0], got, over_y, [over_z[0]])
+        own, half = sums[n_z:]
+
+        over_x = [to_plane(half, 1, 0)]
+        got = [to_z(part, dz) for dz, part in zip(range(1, n_z), sums[1:n_z])]
+        first_moment, second_moment, low_step, half = adam(
+            sums[0], got, moment_one, moment_two, step_count, own, over_x[0]
         )
-        over_x = to_plane(own, 1, 0)
-        over_z = to_z_pair(own)
-        over_xz = to_z_pair(over_x)
-        pieces = []
-        for dx, dz, piece in ((0, 0, own), (1, 0, over_x), (0, 1, over_z), (1, 1, over_xz)):
-            for dc in range(2):
-                position = lambda z, x, c, dx=dx, dz=dz, dc=dc: (
-                    ((x + dx) % 2) * 2 + (z + dz) % 2
-                ) * 2 + (c + dc) % 2
-                pieces.append((position, to_core(piece) if dc else piece))
-
-        outgoing, keep = local_sums(attn, projector, cotangent)
-        sums = core_sum(keep, to_core(outgoing))
-        got = [to_plane(part, dx, dy) for (dx, dy), part in zip(plane, sums[1:])]
-        sums = plane_sum(sums[0], got)
-        got = [to_z(part, dz) for dz, part in zip(range(1, n_z), sums[1:])]
-        first_moment, second_moment, low_step = adam(
-            sums[0], got, moment_one, moment_two, step_count
+        over_x.append(to_plane(half, 1, 0))
+        over_xz = [to_z_pair(part) for part in over_x]
+        column = stack(
+            [low_step] + [to_z(low_step, dz) for dz in range(1, n_z)], over_z[1], over_x[1]
         )
-        column = jnp.stack([low_step] + [to_z(low_step, dz) for dz in range(1, n_z)])
+
         blocks = [(0, 0, 0, column), (1, 0, 0, to_core(column))]
         for dx, dy in plane:
             got = to_plane(column, dx, dy)
             blocks += [(0, dx, dy, got), (1, dx, dy, to_core(got))]
+        pieces = []
+        for dx, dz, parts in ((0, 0, [own]), (1, 0, over_x), (0, 1, over_z), (1, 1, over_xz)):
+            begin = 0
+            for part in parts:
+                for dc in range(2):
+                    row = lambda z, x, c, dx=dx, dz=dz, dc=dc, begin=begin: (
+                        (((x + dx) % 2) * 2 + (z + dz) % 2) * 2 + (c + dc) % 2
+                    ) * eighth + begin
+                    pieces.append((row, to_core(part) if dc else part))
+                begin += part.shape[0]
         my_projector = lax.dynamic_slice_in_dim(projector, y * shard_rows, shard_rows, 0)
         weight_step = step_product(my_projector, blocks)
 
-        grad_input = input_product(cotangent, [(lambda z, x, c: 0, weight)], 0)
-        grad_input = input_product(cotangent, pieces, 1, grad_input)
+        grad_input = other_product(cotangent, pieces, grad_input)
         return grad_input, weight_step, first_moment, second_moment
 
     rows = P(("dp", "fsdp"), None)

time: 93.8 us -> 108 us (1.15)
  local copies, waits for them, and re-layouts: 11.8 us -> 21.4 us
  Pallas kernels: 23.6 us -> 31 us
  waiting for transfers between devices: 31 us -> 24.9 us
  starting transfers between devices: 25.3 us -> 28.1 us
    unnamed x34 -> x60, local copies, waits for them, and re-layouts: 9.7 us -> 18 us
    ppermute x25 -> x32, waiting for transfers between devices: 31 us -> 24.9 us  [send(): return lax.ppermute(value, AXES, pairs)]
    pallas_call x2 -> x6, Pallas kernels: 11.1 us -> 14.9 us  [the longest x1 7.7 us: own_product(): pl.pallas_call(kernel, out_shape=(shape((tokens, rows * n_y), BF16), shap...]
    ppermute x25 -> x32, starting transfers between devices: 25.3 us -> 28.1 us  [send(): return lax.ppermute(value, AXES, pairs)]
    pallas_call x1, Pallas kernels: 0.09 us -> 1.85 us  [plane_sum(): pl.pallas_call(kernel, out_shape=(shape(slab, F32),) + (shape(slab, BF16)...]
    dynamic_slice x1 -> x2, local copies, waits for them, and re-layouts: 1.11 us -> 2.37 us  [mine(): return lax.dynamic_slice_in_dim(weight, q * eighth + begin, count, 0)]
    pallas_call x1, Pallas kernels: 0.88 us -> 2.04 us  [adam(): pl.pallas_call(kernel, out_shape=(shape(dims, F32), shape(dims, F32), sha...]
    pallas_call x1, Pallas kernels: 0.13 us -> 1.26 us  [core_sum(): pl.pallas_call(kernel, out_shape=(shape(slab, F32),) + (shape(slab, BF16)...]
  transfers between devices with their start and end apart: 25 -> 32, of which waited for: 13 -> 8; matrix products, arithmetic and copies ran while one was open for 1% -> 2% of each run, Pallas kernels for 18% -> 21%
where the time goes in v3:
time: 108 us; the launch traced here: 107 us
  Pallas kernels  31 us (29%)
  starting transfers between devices  28.1 us (26%)
  waiting for transfers between devices  24.9 us (23%)
  local copies, waits for them, and re-layouts  21.4 us (20%)
  between operations  1.77 us (2%)
    ppermute x32, starting transfers between devices, send(): return lax.ppermute(value, AXES, pairs)  28.1 us
    ppermute x32, waiting for transfers between devices, send(): return lax.ppermute(value, AXES, pairs)  24.9 us
    unnamed x60, local copies, waits for them, and re-layouts  18 us
    pallas_call x1, Pallas kernels, own_product(): pl.pallas_call(kernel, out_shape=(shape((tokens, rows * n_y), BF16), shap...  7.7 us
    pallas_call x1, Pallas kernels, local_sums(): pl.pallas_call(kernel, out_shape=(shape(dims, BF16), shape(dims, F32)), i...  6.72 us
    pallas_call x1, Pallas kernels, other_product(): pl.pallas_call(kernel, out_shape=shape(into.shape, BF16), in_specs=[VMEM]...  6.18 us
    pallas_call x1, Pallas kernels, step_product(): pl.pallas_call(kernel, out_shape=shape((rows, width), F32), in_specs=[VME...  4.23 us
    dynamic_slice x2, local copies, waits for them, and re-layouts, mine(): return lax.dynamic_slice_in_dim(weight, q * eighth + begin, count, 0)  2.37 us
  transfers between devices with their start and end apart: 32, of which 8 were waited for; matrix products, arithmetic and copies ran while one was open for 2% of the time, Pallas kernels for 21%

profile of v3, /device:TPU:0, one launch (start us, length us, event | category | flops | bytes accessed | tf_op | source)
XLA Modules:
  0.0 107.1 jit_solution(15554186212420662510)
XLA Ops:
  1.6 3.0 %collective-permute-start = (bf16[32,3072]{1,0:T(8,128)(2,1)S(1)}, bf16[32,3072]{1,0:T(8,128)(2,1)}, u32[]{:S(2)}, u32[]{:S(2)}) collective-permute-start(bf16[32,3072]{1,0:T(8,128)(2,1)S(1)} %constant_dynamic-slice_fusion.2), channel_id=1, source_target_pairs={{0,1},{1,0},{2,3},{3,2},{4,5},{5,4},{6,7},{7,6},{8,9},{9,8},{10,11... | collective-permute-start | bytes 589832 | tf_op jit(solution)/shard_map/ppermute | solution.py:91
  5.8 6.7 %shard_map.102 = (bf16[2,2,4,96,256]{4,3,2,1,0:T(8,128)(2,1)S(1)}, f32[2,2,4,96,256]{4,3,2,1,0:T(8,128)S(1)}) custom-call(bf16[576,1536]{1,0:T(8,128)(2,1)} %a_hbm.1, bf16[1536,256]{1,0:T(8,128)(2,1)S(1)} %copy-done.1, bf16[576,3072]{1,0:T(8,128)(2,1)} %g_ref.1), custom_call_target="tpu_custom_call" | custom-call | tf_op jit(solution)/shard_map/pallas_call | solution.py:137
  16.2 2.1 %collective-permute-start.6 = (bf16[32,3072]{1,0:T(8,128)(2,1)}, bf16[32,3072]{1,0:T(8,128)(2,1)S(1)}, u32[]{:S(2)}, u32[]{:S(2)}) collective-permute-start(bf16[32,3072]{1,0:T(8,128)(2,1)} %collective-permute-done.refs_0_.refs_3_), channel_id=1, source_target_pairs={{0,8},{1,9},{2,10},{3,11},{4,12},{5,13},{6,14},{7,15},{8,0},{9,1},... | collective-permute-start | bytes 589832 | tf_op jit(solution)/shard_map/ppermute | solution.py:91
  20.9 1.6 %collective-permute-start.3 = (bf16[4,96,256]{2,1,0:T(8,128)(2,1)S(1)}, bf16[4,96,256]{2,1,0:T(8,128)(2,1)S(1)}, u32[]{:S(2)}, u32[]{:S(2)}) collective-permute-start(bf16[4,96,256]{2,1,0:T(8,128)(2,1)S(1)} %get-tuple-element.26), channel_id=1, source_target_pairs={{0,4},{1,5},{2,6},{3,7},{4,0},{5,1},{6,2},{7,3},{8,12},{9,13},{10,... | collective-permute-start | bytes 589832 | tf_op jit(solution)/shard_map/ppermute | solution.py:91
  22.5 1.5 %collective-permute-start.4 = (bf16[4,96,256]{2,1,0:T(8,128)(2,1)S(1)}, bf16[4,96,256]{2,1,0:T(8,128)(2,1)S(1)}, u32[]{:S(2)}, u32[]{:S(2)}) collective-permute-start(bf16[4,96,256]{2,1,0:T(8,128)(2,1)S(1)} %get-tuple-element.27), channel_id=1, source_target_pairs={{0,5},{1,4},{2,7},{3,6},{4,1},{5,0},{6,3},{7,2},{8,13},{9,12},{10,... | collective-permute-start | bytes 589832 | tf_op jit(solution)/shard_map/ppermute | solution.py:91
  24.5 7.7 %shard_map.106 = (bf16[576,1536]{1,0:T(8,128)(2,1)}, f32[8,128]{1,0:T(8,128)S(1)}) custom-call(bf16[576,3072]{1,0:T(8,128)(2,1)S(1)} %copy-done, bf16[768,3072]{1,0:T(8,128)(2,1)} %w_hbm.1, bf16[4,96,256]{2,1,0:T(8,128)(2,1)S(1)} %get-tuple-element.25.wait_ref), custom_call_target="tpu_custom_call" | custom-call | tf_op jit(solution)/shard_map/pallas_call | solution.py:322
  32.6 3.1 %collective-permute-done.2.refs_0_ = bf16[4,96,256]{2,1,0:T(8,128)(2,1)S(1)} collective-permute-done((bf16[4,96,256]{2,1,0:T(8,128)(2,1)S(1)}, bf16[4,96,256]{2,1,0:T(8,128)(2,1)S(1)}, u32[]{:S(2)}, u32[]{:S(2)}) %collective-permute-start.2) | collective-permute-done | bytes 196640 | tf_op jit(solution)/shard_map/ppermute | solution.py:91
  35.7 1.8 %shard_map.108 = (f32[96,256]{1,0:T(8,128)S(1)}, bf16[96,256]{1,0:T(8,128)(2,1)S(1)}, bf16[96,256]{1,0:T(8,128)(2,1)S(1)}, bf16[96,256]{1,0:T(8,128)(2,1)S(1)}, ...) custom-call(f32[4,96,256]{2,1,0:T(8,128)S(1)} %get-tuple-element.24.own_ref, ...), custom_call_target="tpu_custom_call" | custom-call | tf_op jit(solution)/shard_map/pallas_call | solution.py:199
  37.6 1.5 %collective-permute-start.8 = (bf16[48,3072]{1,0:T(8,128)(2,1)S(1)}, bf16[48,3072]{1,0:T(8,128)(2,1)S(1)}, u32[]{:S(2)}, u32[]{:S(2)}) collective-permute-start(bf16[48,3072]{1,0:T(8,128)(2,1)S(1)} %get-tuple-element.30), channel_id=1, source_target_pairs={{0,4},{1,5},{2,6},{3,7},{4,0},{5,1},{6,2},{7,3},{8,12},{9,13},{10,... | collective-permute-start | bytes 884744 | tf_op jit(solution)/shard_map/ppermute | solution.py:91
  39.0 1.6 %collective-permute-start.16 = (bf16[64,3072]{1,0:T(8,128)(2,1)S(1)}, bf16[64,3072]{1,0:T(8,128)(2,1)}, u32[]{:S(2)}, u32[]{:S(2)}) collective-permute-start(bf16[64,3072]{1,0:T(8,128)(2,1)S(1)} %shard_map.107.refs_4_), channel_id=1, source_target_pairs={{0,8},{1,9},{2,10},{3,11},{4,12},{5,13},{6,14},{7,15},{8,0},{9,1},... | collective-permute-start | bytes 1179656 | tf_op jit(solution)/shard_map/ppermute | solution.py:91
  41.1 2.6 %collective-permute-start.11 = (bf16[96,256]{1,0:T(8,128)(2,1)S(1)}, bf16[96,256]{1,0:T(8,128)(2,1)S(1)}, u32[]{:S(2)}, u32[]{:S(2)}) collective-permute-start(bf16[96,256]{1,0:T(8,128)(2,1)S(1)} %get-tuple-element.33), channel_id=1, source_target_pairs={{0,16},{1,17},{2,18},{3,19},{4,20},{5,21},{6,22},{7,23},{8,24},{9,... | collective-permute-start | bytes 147464 | tf_op jit(solution)/shard_map/ppermute | solution.py:91
  43.7 2.5 %collective-permute-start.12 = (bf16[96,256]{1,0:T(8,128)(2,1)S(1)}, bf16[96,256]{1,0:T(8,128)(2,1)S(1)}, u32[]{:S(2)}, u32[]{:S(2)}) collective-permute-start(bf16[96,256]{1,0:T(8,128)(2,1)S(1)} %get-tuple-element.34), channel_id=1, source_target_pairs={{0,24},{1,25},{2,26},{3,27},{4,28},{5,29},{6,30},{7,31},{8,0},{9,1... | collective-permute-start | bytes 147464 | tf_op jit(solution)/shard_map/ppermute | solution.py:91
  46.8 6.4 %collective-permute-done.10.refs_0_ = bf16[96,256]{1,0:T(8,128)(2,1)S(1)} collective-permute-done((bf16[96,256]{1,0:T(8,128)(2,1)S(1)}, bf16[96,256]{1,0:T(8,128)(2,1)S(1)}, u32[]{:S(2)}, u32[]{:S(2)}) %collective-permute-start.10) | collective-permute-done | bytes 49184 | tf_op jit(solution)/shard_map/ppermute | solution.py:91
  53.2 2.0 %shard_map.109 = (f32[96,256]{1,0:T(8,128)}, f32[96,256]{1,0:T(8,128)}, bf16[96,256]{1,0:T(8,128)(2,1)S(1)}, bf16[48,3072]{1,0:T(8,128)(2,1)S(1)}) custom-call(s32[1]{0:T(128)S(6)} %copy.13.step_ref, f32[96,256]{1,0:T(8,128)S(1)} %get-tuple-element.31.own_ref, bf16[96,256]{1,0:T(8,128)(2,1)S(1)} %collective-permute-done.10.refs_0_, ...), custom_call_target="tpu_custom_call" | custom-call | tf_op jit(solution)/shard_map/pallas_call | solution.py:231
  56.9 2.0 %collective-permute-start.24 = (bf16[96,256]{1,0:T(8,128)(2,1)S(1)}, bf16[96,256]{1,0:T(8,128)(2,1)S(1)}, u32[]{:S(2)}, u32[]{:S(2)}) collective-permute-start(bf16[96,256]{1,0:T(8,128)(2,1)S(1)} %get-tuple-element.37.refs_0_), channel_id=1, source_target_pairs={{0,24},{1,25},{2,26},{3,27},{4,28},{5,29},{6,30},{7,31},{8,0},{9,1... | collective-permute-start | bytes 147464 | tf_op jit(solution)/shard_map/ppermute | solution.py:91
  59.3 5.3 %collective-permute-done.24.refs_3_ = bf16[96,256]{1,0:T(8,128)(2,1)S(1)} collective-permute-done((bf16[96,256]{1,0:T(8,128)(2,1)S(1)}, bf16[96,256]{1,0:T(8,128)(2,1)S(1)}, u32[]{:S(2)}, u32[]{:S(2)}) %collective-permute-start.24) | collective-permute-done | bytes 49184 | tf_op jit(solution)/shard_map/ppermute | solution.py:91
  64.6 1.7 %collective-permute-start.22 = (bf16[96,256]{1,0:T(8,128)(2,1)S(1)}, bf16[96,256]{1,0:T(8,128)(2,1)S(1)}, u32[]{:S(2)}, u32[]{:S(2)}) collective-permute-start(bf16[96,256]{1,0:T(8,128)(2,1)S(1)} %get-tuple-element.37.refs_0_), channel_id=1, source_target_pairs={{0,8},{1,9},{2,10},{3,11},{4,12},{5,13},{6,14},{7,15},{8,16},{9,17... | collective-permute-start | bytes 147464 | tf_op jit(solution)/shard_map/ppermute | solution.py:91
  66.3 4.3 %collective-permute-done.22.refs_1_ = bf16[96,256]{1,0:T(8,128)(2,1)S(1)} collective-permute-done((bf16[96,256]{1,0:T(8,128)(2,1)S(1)}, bf16[96,256]{1,0:T(8,128)(2,1)S(1)}, u32[]{:S(2)}, u32[]{:S(2)}) %collective-permute-start.22) | collective-permute-done | bytes 49184 | tf_op jit(solution)/shard_map/ppermute | solution.py:91
  70.6 1.5 %collective-permute-start.30 = (bf16[4,96,256]{2,1,0:T(8,128)(2,1)S(1)}, bf16[4,96,256]{2,1,0:T(8,128)(2,1)S(1)}, u32[]{:S(2)}, u32[]{:S(2)}) collective-permute-start(bf16[4,96,256]{2,1,0:T(8,128)(2,1)S(1)} %shard_map.111.refs_0_), channel_id=1, source_target_pairs={{0,5},{1,4},{2,7},{3,6},{4,1},{5,0},{6,3},{7,2},{8,13},{9,12},{10,... | collective-permute-start | bytes 589832 | tf_op jit(solution)/shard_map/ppermute | solution.py:91
  73.4 1.5 %collective-permute-start.26 = (bf16[4,96,256]{2,1,0:T(8,128)(2,1)S(1)}, bf16[4,96,256]{2,1,0:T(8,128)(2,1)S(1)}, u32[]{:S(2)}, u32[]{:S(2)}) collective-permute-start(bf16[4,96,256]{2,1,0:T(8,128)(2,1)S(1)} %shard_map.111.refs_0_), channel_id=1, source_target_pairs={{0,1},{1,0},{2,3},{3,2},{4,5},{5,4},{6,7},{7,6},{8,9},{9,8},{10,11... | collective-permute-start | bytes 589832 | tf_op jit(solution)/shard_map/ppermute | solution.py:91
  76.3 3.1 %collective-permute-done.30.refs_6_ = bf16[4,96,256]{2,1,0:T(8,128)(2,1)S(1)} collective-permute-done((bf16[4,96,256]{2,1,0:T(8,128)(2,1)S(1)}, bf16[4,96,256]{2,1,0:T(8,128)(2,1)S(1)}, u32[]{:S(2)}, u32[]{:S(2)}) %collective-permute-start.30) | collective-permute-done | bytes 196640 | tf_op jit(solution)/shard_map/ppermute | solution.py:91
  79.4 2.0 %collective-permute-done.28.refs_4_ = bf16[4,96,256]{2,1,0:T(8,128)(2,1)S(1)} collective-permute-done((bf16[4,96,256]{2,1,0:T(8,128)(2,1)S(1)}, bf16[4,96,256]{2,1,0:T(8,128)(2,1)S(1)}, u32[]{:S(2)}, u32[]{:S(2)}) %collective-permute-start.28) | collective-permute-done | bytes 196640 | tf_op jit(solution)/shard_map/ppermute | solution.py:91
  96.4 4.2 %shard_map.112 = f32[768,3072]{1,0:T(8,128)} custom-call(bf16[768,256]{1,0:T(8,128)(2,1)S(1)} %constant_dynamic-slice_fusion.p_ref, bf16[4,96,256]{2,1,0:T(8,128)(2,1)S(1)} %copy-done.9, bf16[4,96,256]{2,1,0:T(8,128)(2,1)S(1)} %copy-done.21, bf16[4,96,256]{2,1,0:T(8,128)(2,1)S(1)} %copy-done.19, bf16[4,96,256]{2,1,0:T(8,128)(2,1)S(1)} %copy-done.27, ...), custom_call_target="tpu_custom_call" | custom-call | tf_op jit(solution)/shard_map/pallas_call | solution.py:272
  100.8 6.2 %shard_map.110 = bf16[576,1536]{1,0:T(8,128)(2,1)} custom-call(bf16[576,3072]{1,0:T(8,128)(2,1)S(1)} %copy-done, bf16[96,3072]{1,0:T(8,128)(2,1)} %get-tuple-element.29.refs_5_.refs_0_, bf16[96,3072]{1,0:T(8,128)(2,1)} %collective-permute-done.7.refs_1_, bf16[48,3072]{1,0:T(8,128)(2,1)S(1)} %copy-done.5, ...), custom_call_target="tpu_custom_call", output_to_operand_aliasing={{}: (15, {})} | custom-call | tf_op jit(solution)/shard_map/pallas_call | solution.py:400
  (114 shorter events, 29.5 us)
Async XLA Ops:
  1.6 12.0 %collective-permute-start = (bf16[32,3072]{1,0:T(8,128)(2,1)S(1)}, bf16[32,3072]{1,0:T(8,128)(2,1)}, u32[]{:S(2)}, u32[]{:S(2)}) collective-permute-start(bf16[32,3072]{1,0:T(8,128)(2,1)S(1)} %constant_dynamic-slice_fusion.2), channel_id=1, source_target_pairs={{0,1},{1,0},{2,3},{3,2},{4,5},{5,4},{6,7},{7,6},{8,9},{9,8},{10,11... | collective-permute-start | bytes 589832 | tf_op jit(solution)/shard_map/ppermute | solution.py:91
  16.1 16.1 %collective-permute-start.5 = (bf16[64,3072]{1,0:T(8,128)(2,1)S(1)}, bf16[64,3072]{1,0:T(8,128)(2,1)S(1)}, u32[]{:S(2)}, u32[]{:S(2)}) collective-permute-start(bf16[64,3072]{1,0:T(8,128)(2,1)S(1)} %shard_map.105), channel_id=1, source_target_pairs={{0,1},{1,0},{2,3},{3,2},{4,5},{5,4},{6,7},{7,6},{8,9},{9,8},{10,11... | collective-permute-start | bytes 1179656 | tf_op jit(solution)/shard_map/ppermute | solution.py:91
  16.2 16.1 %collective-permute-start.6 = (bf16[32,3072]{1,0:T(8,128)(2,1)}, bf16[32,3072]{1,0:T(8,128)(2,1)S(1)}, u32[]{:S(2)}, u32[]{:S(2)}) collective-permute-start(bf16[32,3072]{1,0:T(8,128)(2,1)} %collective-permute-done.refs_0_.refs_3_), channel_id=1, source_target_pairs={{0,8},{1,9},{2,10},{3,11},{4,12},{5,13},{6,14},{7,15},{8,0},{9,1},... | collective-permute-start | bytes 589832 | tf_op jit(solution)/shard_map/ppermute | solution.py:91
  20.9 11.3 %collective-permute-start.3 = (bf16[4,96,256]{2,1,0:T(8,128)(2,1)S(1)}, bf16[4,96,256]{2,1,0:T(8,128)(2,1)S(1)}, u32[]{:S(2)}, u32[]{:S(2)}) collective-permute-start(bf16[4,96,256]{2,1,0:T(8,128)(2,1)S(1)} %get-tuple-element.26), channel_id=1, source_target_pairs={{0,4},{1,5},{2,6},{3,7},{4,0},{5,1},{6,2},{7,3},{8,12},{9,13},{10,... | collective-permute-start | bytes 589832 | tf_op jit(solution)/shard_map/ppermute | solution.py:91
  22.5 10.1 %collective-permute-start.4 = (bf16[4,96,256]{2,1,0:T(8,128)(2,1)S(1)}, bf16[4,96,256]{2,1,0:T(8,128)(2,1)S(1)}, u32[]{:S(2)}, u32[]{:S(2)}) collective-permute-start(bf16[4,96,256]{2,1,0:T(8,128)(2,1)S(1)} %get-tuple-element.27), channel_id=1, source_target_pairs={{0,5},{1,4},{2,7},{3,6},{4,1},{5,0},{6,3},{7,2},{8,13},{9,12},{10,... | collective-permute-start | bytes 589832 | tf_op jit(solution)/shard_map/ppermute | solution.py:91
  24.0 11.7 %collective-permute-start.2 = (bf16[4,96,256]{2,1,0:T(8,128)(2,1)S(1)}, bf16[4,96,256]{2,1,0:T(8,128)(2,1)S(1)}, u32[]{:S(2)}, u32[]{:S(2)}) collective-permute-start(bf16[4,96,256]{2,1,0:T(8,128)(2,1)S(1)} %get-tuple-element.25.wait_ref), channel_id=1, source_target_pairs={{0,1},{1,0},{2,3},{3,2},{4,5},{5,4},{6,7},{7,6},{8,9},{9,8},{10,11... | collective-permute-start | bytes 589832 | tf_op jit(solution)/shard_map/ppermute | solution.py:91
  37.6 15.6 %collective-permute-start.8 = (bf16[48,3072]{1,0:T(8,128)(2,1)S(1)}, bf16[48,3072]{1,0:T(8,128)(2,1)S(1)}, u32[]{:S(2)}, u32[]{:S(2)}) collective-permute-start(bf16[48,3072]{1,0:T(8,128)(2,1)S(1)} %get-tuple-element.30), channel_id=1, source_target_pairs={{0,4},{1,5},{2,6},{3,7},{4,0},{5,1},{6,2},{7,3},{8,12},{9,13},{10,... | collective-permute-start | bytes 884744 | tf_op jit(solution)/shard_map/ppermute | solution.py:91
  39.0 19.8 %collective-permute-start.16 = (bf16[64,3072]{1,0:T(8,128)(2,1)S(1)}, bf16[64,3072]{1,0:T(8,128)(2,1)}, u32[]{:S(2)}, u32[]{:S(2)}) collective-permute-start(bf16[64,3072]{1,0:T(8,128)(2,1)S(1)} %shard_map.107.refs_4_), channel_id=1, source_target_pairs={{0,8},{1,9},{2,10},{3,11},{4,12},{5,13},{6,14},{7,15},{8,0},{9,1},... | collective-permute-start | bytes 1179656 | tf_op jit(solution)/shard_map/ppermute | solution.py:91
  40.6 12.6 %collective-permute-start.10 = (bf16[96,256]{1,0:T(8,128)(2,1)S(1)}, bf16[96,256]{1,0:T(8,128)(2,1)S(1)}, u32[]{:S(2)}, u32[]{:S(2)}) collective-permute-start(bf16[96,256]{1,0:T(8,128)(2,1)S(1)} %get-tuple-element.32), channel_id=1, source_target_pairs={{0,8},{1,9},{2,10},{3,11},{4,12},{5,13},{6,14},{7,15},{8,16},{9,17... | collective-permute-start | bytes 147464 | tf_op jit(solution)/shard_map/ppermute | solution.py:91
  41.1 12.1 %collective-permute-start.11 = (bf16[96,256]{1,0:T(8,128)(2,1)S(1)}, bf16[96,256]{1,0:T(8,128)(2,1)S(1)}, u32[]{:S(2)}, u32[]{:S(2)}) collective-permute-start(bf16[96,256]{1,0:T(8,128)(2,1)S(1)} %get-tuple-element.33), channel_id=1, source_target_pairs={{0,16},{1,17},{2,18},{3,19},{4,20},{5,21},{6,22},{7,23},{8,24},{9,... | collective-permute-start | bytes 147464 | tf_op jit(solution)/shard_map/ppermute | solution.py:91
  43.7 9.5 %collective-permute-start.12 = (bf16[96,256]{1,0:T(8,128)(2,1)S(1)}, bf16[96,256]{1,0:T(8,128)(2,1)S(1)}, u32[]{:S(2)}, u32[]{:S(2)}) collective-permute-start(bf16[96,256]{1,0:T(8,128)(2,1)S(1)} %get-tuple-element.34), channel_id=1, source_target_pairs={{0,24},{1,25},{2,26},{3,27},{4,28},{5,29},{6,30},{7,31},{8,0},{9,1... | collective-permute-start | bytes 147464 | tf_op jit(solution)/shard_map/ppermute | solution.py:91
  55.3 15.3 %collective-permute-start.13 = (bf16[48,3072]{1,0:T(8,128)(2,1)S(1)}, bf16[48,3072]{1,0:T(8,128)(2,1)}, u32[]{:S(2)}, u32[]{:S(2)}) collective-permute-start(bf16[48,3072]{1,0:T(8,128)(2,1)S(1)} %get-tuple-element.35), channel_id=1, source_target_pairs={{0,4},{1,5},{2,6},{3,7},{4,0},{5,1},{6,2},{7,3},{8,12},{9,13},{10,... | collective-permute-start | bytes 884744 | tf_op jit(solution)/shard_map/ppermute | solution.py:91
  55.8 17.5 %collective-permute-start.18 = (bf16[48,3072]{1,0:T(8,128)(2,1)S(1)}, bf16[48,3072]{1,0:T(8,128)(2,1)}, u32[]{:S(2)}, u32[]{:S(2)}) collective-permute-start(bf16[48,3072]{1,0:T(8,128)(2,1)S(1)} %collective-permute-done.8.refs_6_.refs_2_), channel_id=1, source_target_pairs={{0,8},{1,9},{2,10},{3,11},{4,12},{5,13},{6,14},{7,15},{8,0},{9,1},... | collective-permute-start | bytes 884744 | tf_op jit(solution)/shard_map/ppermute | solution.py:91
  56.9 18.0 %collective-permute-start.9 = (bf16[48,3072]{1,0:T(8,128)(2,1)S(1)}, bf16[48,3072]{1,0:T(8,128)(2,1)S(1)}, u32[]{:S(2)}, u32[]{:S(2)}) collective-permute-start(bf16[48,3072]{1,0:T(8,128)(2,1)S(1)} %collective-permute-done.8.refs_6_.refs_2_), channel_id=1, source_target_pairs={{0,2},{1,3},{2,0},{3,1},{4,6},{5,7},{6,4},{7,5},{8,10},{9,11},{10,... | collective-permute-start | bytes 884744 | tf_op jit(solution)/shard_map/ppermute | solution.py:91
  64.6 8.0 %collective-permute-start.15 = (bf16[32,3072]{1,0:T(8,128)(2,1)S(1)}, bf16[32,3072]{1,0:T(8,128)(2,1)S(1)}, u32[]{:S(2)}, u32[]{:S(2)}) collective-permute-start(bf16[32,3072]{1,0:T(8,128)(2,1)S(1)} %collective-permute-done.6.refs_5_.refs_6_), channel_id=1, source_target_pairs={{0,2},{1,3},{2,0},{3,1},{4,6},{5,7},{6,4},{7,5},{8,10},{9,11},{10,... | collective-permute-start | bytes 589832 | tf_op jit(solution)/shard_map/ppermute | solution.py:91
  70.6 8.8 %collective-permute-start.30 = (bf16[4,96,256]{2,1,0:T(8,128)(2,1)S(1)}, bf16[4,96,256]{2,1,0:T(8,128)(2,1)S(1)}, u32[]{:S(2)}, u32[]{:S(2)}) collective-permute-start(bf16[4,96,256]{2,1,0:T(8,128)(2,1)S(1)} %shard_map.111.refs_0_), channel_id=1, source_target_pairs={{0,5},{1,4},{2,7},{3,6},{4,1},{5,0},{6,3},{7,2},{8,13},{9,12},{10,... | collective-permute-start | bytes 589832 | tf_op jit(solution)/shard_map/ppermute | solution.py:91
  72.1 9.3 %collective-permute-start.28 = (bf16[4,96,256]{2,1,0:T(8,128)(2,1)S(1)}, bf16[4,96,256]{2,1,0:T(8,128)(2,1)S(1)}, u32[]{:S(2)}, u32[]{:S(2)}) collective-permute-start(bf16[4,96,256]{2,1,0:T(8,128)(2,1)S(1)} %shard_map.111.refs_0_), channel_id=1, source_target_pairs={{0,4},{1,5},{2,6},{3,7},{4,0},{5,1},{6,2},{7,3},{8,12},{9,13},{10,... | collective-permute-start | bytes 589832 | tf_op jit(solution)/shard_map/ppermute | solution.py:91
  73.3 11.6 %collective-permute-start.20 = (bf16[48,3072]{1,0:T(8,128)(2,1)}, bf16[48,3072]{1,0:T(8,128)(2,1)}, u32[]{:S(2)}, u32[]{:S(2)}) collective-permute-start(bf16[48,3072]{1,0:T(8,128)(2,1)} %collective-permute-done.13.refs_4_.refs_5_), channel_id=1, source_target_pairs={{0,8},{1,9},{2,10},{3,11},{4,12},{5,13},{6,14},{7,15},{8,0},{9,1},... | collective-permute-start | bytes 884744 | tf_op jit(solution)/shard_map/ppermute | solution.py:91
  73.4 9.0 %collective-permute-start.26 = (bf16[4,96,256]{2,1,0:T(8,128)(2,1)S(1)}, bf16[4,96,256]{2,1,0:T(8,128)(2,1)S(1)}, u32[]{:S(2)}, u32[]{:S(2)}) collective-permute-start(bf16[4,96,256]{2,1,0:T(8,128)(2,1)S(1)} %shard_map.111.refs_0_), channel_id=1, source_target_pairs={{0,1},{1,0},{2,3},{3,2},{4,5},{5,4},{6,7},{7,6},{8,9},{9,8},{10,11... | collective-permute-start | bytes 589832 | tf_op jit(solution)/shard_map/ppermute | solution.py:91
  79.4 21.3 %collective-permute-start.7 = (bf16[96,3072]{1,0:T(8,128)(2,1)}, bf16[96,3072]{1,0:T(8,128)(2,1)}, u32[]{:S(2)}, u32[]{:S(2)}) collective-permute-start(bf16[96,3072]{1,0:T(8,128)(2,1)} %get-tuple-element.29.refs_5_.refs_0_), channel_id=1, source_target_pairs={{0,2},{1,3},{2,0},{3,1},{4,6},{5,7},{6,4},{7,5},{8,10},{9,11},{10,... | collective-permute-start | bytes 1769480 | tf_op jit(solution)/shard_map/ppermute | solution.py:91
  84.9 15.8 %collective-permute-start.17 = (bf16[64,3072]{1,0:T(8,128)(2,1)}, bf16[64,3072]{1,0:T(8,128)(2,1)}, u32[]{:S(2)}, u32[]{:S(2)}) collective-permute-start(bf16[64,3072]{1,0:T(8,128)(2,1)} %collective-permute-done.16.refs_8_.refs_4_), channel_id=1, source_target_pairs={{0,2},{1,3},{2,0},{3,1},{4,6},{5,7},{6,4},{7,5},{8,10},{9,11},{10,... | collective-permute-start | bytes 1179656 | tf_op jit(solution)/shard_map/ppermute | solution.py:91
  85.8 14.9 %collective-permute-start.14 = (bf16[48,3072]{1,0:T(8,128)(2,1)}, bf16[48,3072]{1,0:T(8,128)(2,1)}, u32[]{:S(2)}, u32[]{:S(2)}) collective-permute-start(bf16[48,3072]{1,0:T(8,128)(2,1)} %collective-permute-done.13.refs_4_.refs_5_), channel_id=1, source_target_pairs={{0,2},{1,3},{2,0},{3,1},{4,6},{5,7},{6,4},{7,5},{8,10},{9,11},{10,... | collective-permute-start | bytes 884744 | tf_op jit(solution)/shard_map/ppermute | solution.py:91
  86.8 13.9 %collective-permute-start.19 = (bf16[48,3072]{1,0:T(8,128)(2,1)}, bf16[48,3072]{1,0:T(8,128)(2,1)}, u32[]{:S(2)}, u32[]{:S(2)}) collective-permute-start(bf16[48,3072]{1,0:T(8,128)(2,1)} %collective-permute-done.18.refs_10_), channel_id=1, source_target_pairs={{0,2},{1,3},{2,0},{3,1},{4,6},{5,7},{6,4},{7,5},{8,10},{9,11},{10,... | collective-permute-start | bytes 884744 | tf_op jit(solution)/shard_map/ppermute | solution.py:91
  87.7 13.0 %collective-permute-start.21 = (bf16[48,3072]{1,0:T(8,128)(2,1)}, bf16[48,3072]{1,0:T(8,128)(2,1)}, u32[]{:S(2)}, u32[]{:S(2)}) collective-permute-start(bf16[48,3072]{1,0:T(8,128)(2,1)} %collective-permute-done.20.refs_12_), channel_id=1, source_target_pairs={{0,2},{1,3},{2,0},{3,1},{4,6},{5,7},{6,4},{7,5},{8,10},{9,11},{10,... | collective-permute-start | bytes 884744 | tf_op jit(solution)/shard_map/ppermute | solution.py:91
  (38 other events, 194.2 us)

commit v4 on v3

--- a/solution.py
+++ b/solution.py
@@ -102,25 +102,52 @@
     def to_z_pair(value):
         return send(value, lambda z, x, c, y: (z ^ 1, x, c, y))
 
+    def cut(weight, projector):
+        rows, width = weight.shape
+        eighth = rows // 8
+
+        def kernel(w_hbm, p_hbm, first_ref, second_ref, p_ref, sems):
+            z, x, c, y = place()
+            row = pl.multiple_of(((x * 2 + z % 2) * 2 + c) * eighth, eighth)
+            copies = [
+                pltpu.make_async_copy(w_hbm.at[pl.ds(row, eighth // 2)], first_ref, sems.at[0]),
+                pltpu.make_async_copy(
+                    w_hbm.at[pl.ds(row + eighth // 2, eighth // 2)], second_ref, sems.at[1]
+                ),
+                pltpu.make_async_copy(p_hbm, p_ref, sems.at[2]),
+            ]
+            for copy in copies:
+                copy.start()
+            for copy in copies:
+                copy.wait()
+
+        half = shape((eighth // 2, width), BF16)
+        return pl.pallas_call(
+            kernel,
+            out_shape=(half, half, shape(projector.shape, BF16)),
+            in_specs=[HBM, HBM],
+            out_specs=(VMEM,) * 3,
+            scratch_shapes=[pltpu.SemaphoreType.DMA((3,))],
+            compiler_params=params(54),
+            cost_estimate=cost(0, 0),
+        )(weight, projector)
+
     def local_sums(attn, projector, cotangent):
         tokens, inner = attn.shape
         width, rank = cotangent.shape[1], projector.shape[1]
         rows = width // groups
         own = rows // (2 * n_y)
 
-        def kernel(a_hbm, p_hbm, g_hbm, send_ref, keep_ref, a, p, g, red, part, sems):
+        def kernel(a_hbm, p, g_hbm, send_ref, keep_ref, a, g, red, part, sems):
             c = lax.axis_index("dp") % 2
             copy_a = pltpu.make_async_copy(a_hbm, a, sems.at[0])
-            copy_p = pltpu.make_async_copy(p_hbm, p, sems.at[1])
             copy_a.start()
-            copy_p.start()
             copies = []
             for k in range(groups):
                 span = pl.ds(k * rows, rows)
-                copies.append(pltpu.make_async_copy(g_hbm.at[:, span], g.at[k], sems.at[2 + k]))
+                copies.append(pltpu.make_async_copy(g_hbm.at[:, span], g.at[k], sems.at[1 + k]))
                 copies[-1].start()
             copy_a.wait()
-            copy_p.wait()
             red[...] = jnp.dot(a[...], p[...], preferred_element_type=F32).astype(BF16)
             for k in range(groups):
                 copies[k].wait()
@@ -137,15 +164,14 @@
         return pl.pallas_call(
             kernel,
             out_shape=(shape(dims, BF16), shape(dims, F32)),
-            in_specs=[HBM, HBM, HBM],
+            in_specs=[HBM, VMEM, HBM],
             out_specs=(VMEM, VMEM),
             scratch_shapes=[
                 pltpu.VMEM(attn.shape, BF16),
-                pltpu.VMEM(projector.shape, BF16),
                 pltpu.VMEM((groups, tokens, rows), BF16),
                 pltpu.VMEM((tokens, rank), BF16),
                 pltpu.VMEM((2, rows, rank), F32),
-                pltpu.SemaphoreType.DMA((2 + groups,)),
+                pltpu.SemaphoreType.DMA((1 + groups,)),
             ],
             compiler_params=params(50),
             cost_estimate=cost(
@@ -178,8 +204,7 @@
 
         def kernel(own_ref, *refs):
             got_refs, part_refs = refs[: len(got)], refs[len(got) : len(got) + len(parts)]
-            out_ref, send_refs = refs[-2 - n_z], refs[-1 - n_z : -2]
-            full_ref, half_ref = refs[-2:]
+            out_ref, send_refs, full_ref = refs[-1 - n_z], refs[-n_z:-1], refs[-1]
             z, x, c, y = place()
             for dz in range(n_z):
                 tz = (z + dz) % n_z
@@ -194,26 +219,21 @@
             for ref in part_refs:
                 full_ref[begin : begin + ref.shape[0], :] = ref[...]
                 begin += ref.shape[0]
-            half_ref[...] = full_ref[: rows // 2, :]
 
         return pl.pallas_call(
             kernel,
             out_shape=(shape(slab, F32),)
             + (shape(slab, BF16),) * (n_z - 1)
-            + (shape((rows, width), BF16), shape((rows // 2, width), BF16)),
+            + (shape((rows, width), BF16),),
             in_specs=[VMEM] * (1 + len(got) + len(parts)) + [ANY] * len(wait),
-            out_specs=(VMEM,) * (n_z + 2),
+            out_specs=(VMEM,) * (n_z + 1),
             compiler_params=params(8),
             cost_estimate=cost(4 * own.size, 10 * own.size),
         )(own, *got, *parts, *wait)
 
-    def adam(own, got, moment_one, moment_two, step_count, full, wait):
-        half = full.shape[0] // 2
-
+    def adam(own, got, moment_one, moment_two, step_count):
         def kernel(step_ref, own_ref, *refs):
-            got_refs, (m1, m2, full_ref, wait_ref) = refs[: len(got)], refs[len(got) : -4]
-            first_ref, second_ref, low_ref, half_ref = refs[-4:]
-            half_ref[...] = full_ref[half:, :]
+            got_refs, (m1, m2, first_ref, second_ref, low_ref) = refs[: len(got)], refs[len(got) :]
             projected = own_ref[...]
             for ref in got_refs:
                 projected = projected + ref[...].astype(F32)
@@ -234,16 +254,15 @@
                 shape(dims, F32),
                 shape(dims, F32),
                 shape(dims, BF16),
-                shape((half, full.shape[1]), BF16),
             ),
-            in_specs=[SMEM] + [VMEM] * (4 + len(got)) + [ANY],
-            out_specs=(VMEM,) * 4,
+            in_specs=[SMEM] + [VMEM] * (3 + len(got)),
+            out_specs=(VMEM,) * 3,
             compiler_params=params(4),
             cost_estimate=cost(20 * own.size, 24 * own.size),
-        )(step_count, own, *got, moment_one, moment_two, full, wait)
-
-    def step_product(my_projector, blocks):
-        rows, rank = my_projector.shape
+        )(step_count, own, *got, moment_one, moment_two)
+
+    def step_product(projector, rows, blocks):
+        rank = projector.shape[1]
         own = blocks[0][3].shape[1]
         span = 2 * n_y * own
         width = groups * span
@@ -260,7 +279,10 @@
             copies = []
             for k in range(groups):
                 out[k] = 0.25 * lax.dot_general(
-                    p_ref[...], low[k], (((1,), (1,)), ((), ())), preferred_element_type=F32
+                    p_ref[pl.ds(pl.multiple_of(y * rows, 16), rows), :],
+                    low[k],
+                    (((1,), (1,)), ((), ())),
+                    preferred_element_type=F32,
                 )
                 copies.append(
                     pltpu.make_async_copy(out.at[k], out_hbm.at[:, pl.ds(k * span, span)], sems.at[k])
@@ -281,28 +303,25 @@
             ],
             compiler_params=params(16),
             cost_estimate=cost(2 * rows * rank * width, 4 * rows * width),
-        )(my_projector, *[block[3] for block in blocks])
-
-    def own_product(cotangent, weight, wait):
+        )(projector, *[block[3] for block in blocks])
+
+    def own_product(cotangent, weight, *wait):
         tokens, width = cotangent.shape
         rows = weight.shape[0]
         step = 256
         chunks = rows // step
 
-        def kernel(g_hbm, w_hbm, wait_ref, out_hbm, done_ref, g, w, out, sems):
+        def kernel(g, w_hbm, wait_ref, plane_ref, out_hbm, done_ref, w, out, sems):
             y = lax.axis_index("fsdp")
-            copy_g = pltpu.make_async_copy(g_hbm, g, sems.at[0])
-            copy_g.start()
             copies = []
             for k in range(chunks):
                 copies.append(
                     pltpu.make_async_copy(
-                        w_hbm.at[pl.ds(k * step, step), :], w.at[k], sems.at[1 + k]
+                        w_hbm.at[pl.ds(k * step, step), :], w.at[k], sems.at[k]
                     )
                 )
                 copies[-1].start()
             done_ref[...] = jnp.zeros_like(done_ref)
-            copy_g.wait()
             outs = []
             for k in range(chunks):
                 copies[k].wait()
@@ -312,7 +331,7 @@
                 column = pl.multiple_of(y * rows + k * step, step)
                 outs.append(
                     pltpu.make_async_copy(
-                        out.at[k], out_hbm.at[:, pl.ds(column, step)], sems.at[1 + chunks + k]
+                        out.at[k], out_hbm.at[:, pl.ds(column, step)], sems.at[chunks + k]
                     )
                 )
                 outs[-1].start()
@@ -322,31 +341,35 @@
         return pl.pallas_call(
             kernel,
             out_shape=(shape((tokens, rows * n_y), BF16), shape((8, 128), F32)),
-            in_specs=[HBM, HBM, ANY],
+            in_specs=[VMEM, HBM, ANY, ANY],
             out_specs=(HBM, VMEM),
             scratch_shapes=[
-                pltpu.VMEM((tokens, width), BF16),
                 pltpu.VMEM((chunks, step, width), BF16),
                 pltpu.VMEM((chunks, tokens, step), BF16),
-                pltpu.SemaphoreType.DMA((1 + 2 * chunks,)),
+                pltpu.SemaphoreType.DMA((2 * chunks,)),
             ],
-            compiler_params=params(50),
+            compiler_params=params(10),
             cost_estimate=cost(2 * tokens * rows * width, 2 * (tokens + rows) * width),
-        )(cotangent, weight, wait)
-
-    def stack(values, *wait):
+        )(cotangent, weight, *wait)
+
+    def stack(values, piece, *wait):
         def kernel(*refs):
+            out_ref, piece_ref = refs[-2:]
             for k in range(len(values)):
-                refs[-1][k] = refs[k][...]
-
-        return pl.pallas_call(
-            kernel,
-            out_shape=shape((len(values),) + values[0].shape, values[0].dtype),
-            in_specs=[VMEM] * len(values) + [ANY] * len(wait),
-            out_specs=VMEM,
+                out_ref[k] = refs[k][...]
+            piece_ref[...] = refs[len(values)][...]
+
+        return pl.pallas_call(
+            kernel,
+            out_shape=(
+                shape((len(values),) + values[0].shape, values[0].dtype),
+                shape(piece.shape, piece.dtype),
+            ),
+            in_specs=[VMEM] * (len(values) + 1) + [ANY] * len(wait),
+            out_specs=(VMEM, VMEM),
             compiler_params=params(4),
             cost_estimate=cost(0, 2 * values[0].size),
-        )(*values, *wait)
+        )(*values, piece, *wait)
 
     def relay(value, *wait):
         def kernel(ref, *refs):
@@ -417,47 +440,34 @@
         own_rows = moment_one.shape[0]
         if n_y != 2 or own_rows % 16 or shard_rows % 384 or n_z % 2:
             return plain(attn, cotangent, weight, projector, moment_one, moment_two, step_count)
-        z, x, c, y = place()
-        q = (x * 2 + z % 2) * 2 + c
-
         eighth = shard_rows // 8
-        cut = eighth // 48 * 16
-        cuts = ((0, cut), (cut, eighth - cut))
-
-        def mine(part):
-            begin, count = cuts[part]
-            return lax.dynamic_slice_in_dim(weight, q * eighth + begin, count, 0)
-
-        outgoing, keep = local_sums(attn, projector, cotangent)
-        over_y = [to_plane(mine(0), 0, 1)]
-        over_y.append(to_plane(relay(mine(1), over_y[0]), 0, 1))
+        first, second, own_projector = cut(weight, projector)
+        over_y = [to_plane(first, 0, 1)]
+        outgoing, keep = local_sums(attn, own_projector, cotangent)
+        over_y.append(to_plane(relay(second, over_y[0]), 0, 1))
         sums = core_sum(keep, to_core(relay(outgoing, over_y[0])))
-        over_z = [to_z_pair(over_y[0])]
-
         got = [to_plane(part, dx, dy) for (dx, dy), part in zip(plane, sums[1:])]
-        grad_input, done = own_product(cotangent, weight, sums[1])
-        over_y[1] = relay(over_y[1], done)
-        over_z.append(to_z_pair(over_y[1]))
-        sums = plane_sum(sums[0], got, over_y, [over_z[0]])
-        own, half = sums[n_z:]
-
-        over_x = [to_plane(half, 1, 0)]
+        over_z = [to_z_pair(part) for part in over_y]
+        grad_input, done = own_product(cotangent, weight, over_y[1], sums[1])
+        sums = plane_sum(sums[0], got, over_y, [done] + over_z)
+        own = sums[n_z]
+
+        over_x = to_plane(own, 1, 0)
         got = [to_z(part, dz) for dz, part in zip(range(1, n_z), sums[1:n_z])]
-        first_moment, second_moment, low_step, half = adam(
-            sums[0], got, moment_one, moment_two, step_count, own, over_x[0]
+        first_moment, second_moment, low_step = adam(
+            sums[0], got, moment_one, moment_two, step_count
         )
-        over_x.append(to_plane(half, 1, 0))
-        over_xz = [to_z_pair(part) for part in over_x]
-        column = stack(
-            [low_step] + [to_z(low_step, dz) for dz in range(1, n_z)], over_z[1], over_x[1]
+        column, over_x = stack(
+            [low_step] + [to_z(low_step, dz) for dz in range(1, n_z)], over_x
         )
+        over_xz = to_z_pair(over_x)
 
         blocks = [(0, 0, 0, column), (1, 0, 0, to_core(column))]
         for dx, dy in plane:
             got = to_plane(column, dx, dy)
             blocks += [(0, dx, dy, got), (1, dx, dy, to_core(got))]
         pieces = []
-        for dx, dz, parts in ((0, 0, [own]), (1, 0, over_x), (0, 1, over_z), (1, 1, over_xz)):
+        for dx, dz, parts in ((0, 0, [own]), (1, 0, [over_x]), (0, 1, over_z), (1, 1, [over_xz])):
             begin = 0
             for part in parts:
                 for dc in range(2):
@@ -466,9 +476,7 @@
                     ) * eighth + begin
                     pieces.append((row, to_core(part) if dc else part))
                 begin += part.shape[0]
-        my_projector = lax.dynamic_slice_in_dim(projector, y * shard_rows, shard_rows, 0)
-        weight_step = step_product(my_projector, blocks)
-
+        weight_step = step_product(own_projector, shard_rows, blocks)
         grad_input = other_product(cotangent, pieces, grad_input)
         return grad_input, weight_step, first_moment, second_moment
 

time: 108 us -> 80.6 us (0.75)
  local copies, waits for them, and re-layouts: 21.4 us -> 1.96 us
  Pallas kernels: 31 us -> 26 us
  waiting for transfers between devices: 24.9 us -> 23.7 us
  starting transfers between devices: 28.1 us -> 27 us
    unnamed x60 -> x14, local copies, waits for them, and re-layouts: 18 us -> 1.96 us
    dynamic_slice x3 -> x0, local copies, waits for them, and re-layouts: 3.4 us -> none  [the longest x2 2.37 us: mine(): return lax.dynamic_slice_in_dim(weight, q * eighth + begin, count, 0)]
    pallas_call x1 -> x2, Pallas kernels: 0.01 us -> 2.54 us  [the longest x1 2.49 us: cut(): pl.pallas_call(kernel, out_shape=(half, half, shape(projector.shape, BF16...]
    pallas_call x1, Pallas kernels: 1.85 us -> 0.1 us  [plane_sum(): pl.pallas_call(kernel, out_shape=(shape(slab, F32),) + (shape(slab, BF16)...]
    pallas_call x1, Pallas kernels: 7.7 us -> 6.22 us  [own_product(): pl.pallas_call(kernel, out_shape=(shape((tokens, rows * n_y), BF16), shap...]
    pallas_call x1, Pallas kernels: 6.18 us -> 4.98 us  [other_product(): pl.pallas_call(kernel, out_shape=shape(into.shape, BF16), in_specs=[VMEM]...]
    ppermute x32 -> x28, waiting for transfers between devices: 24.9 us -> 23.7 us  [send(): return lax.ppermute(value, AXES, pairs)]
    pallas_call x1, Pallas kernels: 2.04 us -> 0.88 us  [adam(): pl.pallas_call(kernel, out_shape=(shape(dims, F32), shape(dims, F32), sha...]
  transfers between devices with their start and end apart: 32 -> 28, of which waited for: 8 -> 13; matrix products, arithmetic and copies ran while one was open for 2% -> 0% of each run, Pallas kernels for 21% -> 23%
where the time goes in v4:
time: 80.6 us; the launch traced here: 80.4 us
  starting transfers between devices  27 us (33%)
  Pallas kernels  26 us (32%)
  waiting for transfers between devices  23.7 us (29%)
  local copies, waits for them, and re-layouts  1.96 us (2%)
  between operations  1.66 us (2%)
    ppermute x28, starting transfers between devices, send(): return lax.ppermute(value, AXES, pairs)  27 us
    ppermute x28, waiting for transfers between devices, send(): return lax.ppermute(value, AXES, pairs)  23.7 us
    pallas_call x1, Pallas kernels, local_sums(): pl.pallas_call(kernel, out_shape=(shape(dims, BF16), shape(dims, F32)), i...  6.86 us
    pallas_call x1, Pallas kernels, own_product(): pl.pallas_call(kernel, out_shape=(shape((tokens, rows * n_y), BF16), shap...  6.22 us
    pallas_call x1, Pallas kernels, other_product(): pl.pallas_call(kernel, out_shape=shape(into.shape, BF16), in_specs=[VMEM]...  4.98 us
    pallas_call x1, Pallas kernels, step_product(): pl.pallas_call(kernel, out_shape=shape((rows, width), F32), in_specs=[VME...  4.23 us
    pallas_call x1, Pallas kernels, cut(): pl.pallas_call(kernel, out_shape=(half, half, shape(projector.shape, BF16...  2.49 us
    unnamed x14, local copies, waits for them, and re-layouts  1.96 us
  transfers between devices with their start and end apart: 28, of which 13 were waited for; matrix products, arithmetic and copies ran while one was open for 0% of the time, Pallas kernels for 23%

profile of v4, /device:TPU:0, one launch (start us, length us, event | category | flops | bytes accessed | tf_op | source)
XLA Modules:
  0.0 80.4 jit_solution(4588849329299545413)
XLA Ops:
  0.6 2.5 %shard_map.102 = (bf16[48,3072]{1,0:T(8,128)(2,1)}, bf16[48,3072]{1,0:T(8,128)(2,1)}, bf16[1536,256]{1,0:T(8,128)(2,1)}) custom-call(bf16[768,3072]{1,0:T(8,128)(2,1)} %w_hbm.3, bf16[1536,256]{1,0:T(8,128)(2,1)} %p_hbm.1), custom_call_target="tpu_custom_call" | custom-call | tf_op jit(solution)/shard_map/pallas_call | solution.py:125
  3.1 3.0 %collective-permute-start = (bf16[48,3072]{1,0:T(8,128)(2,1)}, bf16[48,3072]{1,0:T(8,128)(2,1)S(1)}, u32[]{:S(2)}, u32[]{:S(2)}) collective-permute-start(bf16[48,3072]{1,0:T(8,128)(2,1)} %get-tuple-element.28), channel_id=1, source_target_pairs={{0,1},{1,0},{2,3},{3,2},{4,5},{5,4},{6,7},{7,6},{8,9},{9,8},{10,11... | collective-permute-start | bytes 884744 | tf_op jit(solution)/shard_map/ppermute | solution.py:91
  6.2 1.1 %copy-done.1 = bf16[1536,256]{1,0:T(8,128)(2,1)S(1)} copy-done((bf16[1536,256]{1,0:T(8,128)(2,1)S(1)}, bf16[1536,256]{1,0:T(8,128)(2,1)}, u32[]{:S(2)}) %copy-start.1) | copy-done | bytes 786456
  7.3 6.9 %shard_map.103 = (bf16[2,2,4,96,256]{4,3,2,1,0:T(8,128)(2,1)S(1)}, f32[2,2,4,96,256]{4,3,2,1,0:T(8,128)S(1)}) custom-call(bf16[576,1536]{1,0:T(8,128)(2,1)} %a_hbm.1, bf16[1536,256]{1,0:T(8,128)(2,1)S(1)} %copy-done.1, bf16[576,3072]{1,0:T(8,128)(2,1)} %g_ref.1), custom_call_target="tpu_custom_call" | custom-call | tf_op jit(solution)/shard_map/pallas_call | solution.py:164
  15.4 1.9 %collective-permute-start.6 = (bf16[48,3072]{1,0:T(8,128)(2,1)S(1)}, bf16[48,3072]{1,0:T(8,128)(2,1)S(1)}, u32[]{:S(2)}, u32[]{:S(2)}) collective-permute-start(bf16[48,3072]{1,0:T(8,128)(2,1)S(1)} %collective-permute-done.refs_0_.refs_3_), channel_id=1, source_target_pairs={{0,8},{1,9},{2,10},{3,11},{4,12},{5,13},{6,14},{7,15},{8,0},{9,1},... | collective-permute-start | bytes 884744 | tf_op jit(solution)/shard_map/ppermute | solution.py:91
  17.3 6.5 %collective-permute-done.5.wait_ref.refs_4_ = bf16[48,3072]{1,0:T(8,128)(2,1)S(1)} collective-permute-done((bf16[48,3072]{1,0:T(8,128)(2,1)S(1)}, bf16[48,3072]{1,0:T(8,128)(2,1)S(1)}, u32[]{:S(2)}, u32[]{:S(2)}) %collective-permute-start.5) | collective-permute-done | bytes 294944 | tf_op jit(solution)/shard_map/ppermute | solution.py:91
  23.9 1.6 %collective-permute-start.7 = (bf16[48,3072]{1,0:T(8,128)(2,1)S(1)}, bf16[48,3072]{1,0:T(8,128)(2,1)S(1)}, u32[]{:S(2)}, u32[]{:S(2)}) collective-permute-start(bf16[48,3072]{1,0:T(8,128)(2,1)S(1)} %collective-permute-done.5.wait_ref.refs_4_), channel_id=1, source_target_pairs={{0,8},{1,9},{2,10},{3,11},{4,12},{5,13},{6,14},{7,15},{8,0},{9,1},... | collective-permute-start | bytes 884744 | tf_op jit(solution)/shard_map/ppermute | solution.py:91
  25.6 1.6 %collective-permute-start.3 = (bf16[4,96,256]{2,1,0:T(8,128)(2,1)S(1)}, bf16[4,96,256]{2,1,0:T(8,128)(2,1)S(1)}, u32[]{:S(2)}, u32[]{:S(2)}) collective-permute-start(bf16[4,96,256]{2,1,0:T(8,128)(2,1)S(1)} %get-tuple-element.31), channel_id=1, source_target_pairs={{0,4},{1,5},{2,6},{3,7},{4,0},{5,1},{6,2},{7,3},{8,12},{9,13},{10,... | collective-permute-start | bytes 589832 | tf_op jit(solution)/shard_map/ppermute | solution.py:91
  29.1 6.2 %shard_map.107 = (bf16[576,1536]{1,0:T(8,128)(2,1)}, f32[8,128]{1,0:T(8,128)S(1)}) custom-call(bf16[576,3072]{1,0:T(8,128)(2,1)S(1)} %copy-done, bf16[768,3072]{1,0:T(8,128)(2,1)S(1)} %bitcast.1, bf16[48,3072]{1,0:T(8,128)(2,1)S(1)} %collective-permute-done.5.wait_ref.refs_4_, bf16[4,96,256]{2,1,0:T(8,128)(2,1)S(1)} %get-tuple-element.30.plane_ref), custom_call_target="tpu_custom_call" | custom-call | tf_op jit(solution)/shard_map/pallas_call | solution.py:341
  36.1 1.4 %collective-permute-done.2.refs_0_ = bf16[4,96,256]{2,1,0:T(8,128)(2,1)S(1)} collective-permute-done((bf16[4,96,256]{2,1,0:T(8,128)(2,1)S(1)}, bf16[4,96,256]{2,1,0:T(8,128)(2,1)S(1)}, u32[]{:S(2)}, u32[]{:S(2)}) %collective-permute-start.2) | collective-permute-done | bytes 196640 | tf_op jit(solution)/shard_map/ppermute | solution.py:91
  37.6 1.6 %collective-permute-start.15 = (bf16[96,3072]{1,0:T(8,128)(2,1)S(1)}, bf16[96,3072]{1,0:T(8,128)(2,1)S(1)}, u32[]{:S(2)}, u32[]{:S(2)}) collective-permute-start(bf16[96,3072]{1,0:T(8,128)(2,1)S(1)} %get-tuple-element.35.refs_0_), channel_id=1, source_target_pairs={{0,4},{1,5},{2,6},{3,7},{4,0},{5,1},{6,2},{7,3},{8,12},{9,13},{10,... | collective-permute-start | bytes 1769480 | tf_op jit(solution)/shard_map/ppermute | solution.py:91
  39.6 2.6 %collective-permute-start.10 = (bf16[96,256]{1,0:T(8,128)(2,1)S(1)}, bf16[96,256]{1,0:T(8,128)(2,1)S(1)}, u32[]{:S(2)}, u32[]{:S(2)}) collective-permute-start(bf16[96,256]{1,0:T(8,128)(2,1)S(1)} %get-tuple-element.38), channel_id=1, source_target_pairs={{0,16},{1,17},{2,18},{3,19},{4,20},{5,21},{6,22},{7,23},{8,24},{9,... | collective-permute-start | bytes 147464 | tf_op jit(solution)/shard_map/ppermute | solution.py:91
  42.2 2.5 %collective-permute-start.11 = (bf16[96,256]{1,0:T(8,128)(2,1)S(1)}, bf16[96,256]{1,0:T(8,128)(2,1)S(1)}, u32[]{:S(2)}, u32[]{:S(2)}) collective-permute-start(bf16[96,256]{1,0:T(8,128)(2,1)S(1)} %get-tuple-element.39), channel_id=1, source_target_pairs={{0,24},{1,25},{2,26},{3,27},{4,28},{5,29},{6,30},{7,31},{8,0},{9,1... | collective-permute-start | bytes 147464 | tf_op jit(solution)/shard_map/ppermute | solution.py:91
  47.3 4.2 %collective-permute-start.14 = (bf16[96,256]{1,0:T(8,128)(2,1)S(1)}, bf16[96,256]{1,0:T(8,128)(2,1)S(1)}, u32[]{:S(2)}, u32[]{:S(2)}) collective-permute-start(bf16[96,256]{1,0:T(8,128)(2,1)S(1)} %get-tuple-element.40.refs_0_), channel_id=1, source_target_pairs={{0,24},{1,25},{2,26},{3,27},{4,28},{5,29},{6,30},{7,31},{8,0},{9,1... | collective-permute-start | bytes 147464 | tf_op jit(solution)/shard_map/ppermute | solution.py:91
  52.1 1.6 %collective-permute-done.14.refs_3_ = bf16[96,256]{1,0:T(8,128)(2,1)S(1)} collective-permute-done((bf16[96,256]{1,0:T(8,128)(2,1)S(1)}, bf16[96,256]{1,0:T(8,128)(2,1)S(1)}, u32[]{:S(2)}, u32[]{:S(2)}) %collective-permute-start.14) | collective-permute-done | bytes 49184 | tf_op jit(solution)/shard_map/ppermute | solution.py:91
  53.7 2.9 %collective-permute-done.13.refs_2_ = bf16[96,256]{1,0:T(8,128)(2,1)S(1)} collective-permute-done((bf16[96,256]{1,0:T(8,128)(2,1)S(1)}, bf16[96,256]{1,0:T(8,128)(2,1)S(1)}, u32[]{:S(2)}, u32[]{:S(2)}) %collective-permute-start.13) | collective-permute-done | bytes 49184 | tf_op jit(solution)/shard_map/ppermute | solution.py:91
  56.6 1.4 %collective-permute-done.12.refs_1_ = bf16[96,256]{1,0:T(8,128)(2,1)S(1)} collective-permute-done((bf16[96,256]{1,0:T(8,128)(2,1)S(1)}, bf16[96,256]{1,0:T(8,128)(2,1)S(1)}, u32[]{:S(2)}, u32[]{:S(2)}) %collective-permute-start.12) | collective-permute-done | bytes 49184 | tf_op jit(solution)/shard_map/ppermute | solution.py:91
  59.2 1.5 %collective-permute-start.24 = (bf16[4,96,256]{2,1,0:T(8,128)(2,1)S(1)}, bf16[4,96,256]{2,1,0:T(8,128)(2,1)S(1)}, u32[]{:S(2)}, u32[]{:S(2)}) collective-permute-start(bf16[4,96,256]{2,1,0:T(8,128)(2,1)S(1)} %get-tuple-element.43.refs_0_), channel_id=1, source_target_pairs={{0,4},{1,5},{2,6},{3,7},{4,0},{5,1},{6,2},{7,3},{8,12},{9,13},{10,... | collective-permute-start | bytes 589832 | tf_op jit(solution)/shard_map/ppermute | solution.py:91
  60.7 1.2 %collective-permute-start.22 = (bf16[4,96,256]{2,1,0:T(8,128)(2,1)S(1)}, bf16[4,96,256]{2,1,0:T(8,128)(2,1)S(1)}, u32[]{:S(2)}, u32[]{:S(2)}) collective-permute-start(bf16[4,96,256]{2,1,0:T(8,128)(2,1)S(1)} %get-tuple-element.43.refs_0_), channel_id=1, source_target_pairs={{0,1},{1,0},{2,3},{3,2},{4,5},{5,4},{6,7},{7,6},{8,9},{9,8},{10,11... | collective-permute-start | bytes 589832 | tf_op jit(solution)/shard_map/ppermute | solution.py:91
  61.9 3.2 %collective-permute-done.26.refs_6_ = bf16[4,96,256]{2,1,0:T(8,128)(2,1)S(1)} collective-permute-done((bf16[4,96,256]{2,1,0:T(8,128)(2,1)S(1)}, bf16[4,96,256]{2,1,0:T(8,128)(2,1)S(1)}, u32[]{:S(2)}, u32[]{:S(2)}) %collective-permute-start.26) | collective-permute-done | bytes 196640 | tf_op jit(solution)/shard_map/ppermute | solution.py:91
  65.0 1.4 %collective-permute-done.24.refs_4_ = bf16[4,96,256]{2,1,0:T(8,128)(2,1)S(1)} collective-permute-done((bf16[4,96,256]{2,1,0:T(8,128)(2,1)S(1)}, bf16[4,96,256]{2,1,0:T(8,128)(2,1)S(1)}, u32[]{:S(2)}, u32[]{:S(2)}) %collective-permute-start.24) | collective-permute-done | bytes 196640 | tf_op jit(solution)/shard_map/ppermute | solution.py:91
  68.6 1.8 %collective-permute-done.25.refs_5_ = bf16[4,96,256]{2,1,0:T(8,128)(2,1)S(1)} collective-permute-done((bf16[4,96,256]{2,1,0:T(8,128)(2,1)S(1)}, bf16[4,96,256]{2,1,0:T(8,128)(2,1)S(1)}, u32[]{:S(2)}, u32[]{:S(2)}) %collective-permute-start.25) | collective-permute-done | bytes 196640 | tf_op jit(solution)/shard_map/ppermute | solution.py:91
  70.9 4.2 %shard_map.112 = f32[768,3072]{1,0:T(8,128)} custom-call(bf16[1536,256]{1,0:T(8,128)(2,1)S(1)} %copy-done.1, bf16[4,96,256]{2,1,0:T(8,128)(2,1)S(1)} %get-tuple-element.43.refs_0_, bf16[4,96,256]{2,1,0:T(8,128)(2,1)S(1)} %collective-permute-done.21.refs_1_, bf16[4,96,256]{2,1,0:T(8,128)(2,1)S(1)} %collective-permute-done.22.refs_2_, ...), custom_call_target="tpu_custom_call" | custom-call | tf_op jit(solution)/shard_map/pallas_call | solution.py:294
  75.2 5.0 %shard_map.111 = bf16[576,1536]{1,0:T(8,128)(2,1)} custom-call(bf16[576,3072]{1,0:T(8,128)(2,1)S(1)} %copy-done, bf16[96,3072]{1,0:T(8,128)(2,1)S(1)} %get-tuple-element.35.refs_0_, bf16[96,3072]{1,0:T(8,128)(2,1)S(1)} %collective-permute-done.8.refs_1_, bf16[96,3072]{1,0:T(8,128)(2,1)S(1)} %get-tuple-element.41.refs_2_, ...), custom_call_target="tpu_custom_call", output_to_operand_aliasing={{}: (11, {})} | custom-call | tf_op jit(solution)/shard_map/pallas_call | solution.py:423
  (58 shorter events, 10.9 us)
Async XLA Ops:
  3.1 11.1 %collective-permute-start = (bf16[48,3072]{1,0:T(8,128)(2,1)}, bf16[48,3072]{1,0:T(8,128)(2,1)S(1)}, u32[]{:S(2)}, u32[]{:S(2)}) collective-permute-start(bf16[48,3072]{1,0:T(8,128)(2,1)} %get-tuple-element.28), channel_id=1, source_target_pairs={{0,1},{1,0},{2,3},{3,2},{4,5},{5,4},{6,7},{7,6},{8,9},{9,8},{10,11... | collective-permute-start | bytes 884744 | tf_op jit(solution)/shard_map/ppermute | solution.py:91
  14.3 11.2 %collective-permute-start.1 = (bf16[2,2,4,96,256]{4,3,2,1,0:T(8,128)(2,1)S(1)}, bf16[2,2,4,96,256]{4,3,2,1,0:T(8,128)(2,1)S(1)}, u32[]{:S(2)}, u32[]{:S(2)}) collective-permute-start(bf16[2,2,4,96,256]{4,3,2,1,0:T(8,128)(2,1)S(1)} %shard_map.104), channel_id=1, source_target_pairs={{0,2},{1,3},{2,0},{3,1},{4,6},{5,7},{6,4},{7,5},{8,10},{9,11},{10,... | collective-permute-start | bytes 2359304 | tf_op jit(solution)/shard_map/ppermute | solution.py:91
  15.2 8.7 %collective-permute-start.5 = (bf16[48,3072]{1,0:T(8,128)(2,1)S(1)}, bf16[48,3072]{1,0:T(8,128)(2,1)S(1)}, u32[]{:S(2)}, u32[]{:S(2)}) collective-permute-start(bf16[48,3072]{1,0:T(8,128)(2,1)S(1)} %shard_map.106), channel_id=1, source_target_pairs={{0,1},{1,0},{2,3},{3,2},{4,5},{5,4},{6,7},{7,6},{8,9},{9,8},{10,11... | collective-permute-start | bytes 884744 | tf_op jit(solution)/shard_map/ppermute | solution.py:91
  15.4 20.0 %collective-permute-start.6 = (bf16[48,3072]{1,0:T(8,128)(2,1)S(1)}, bf16[48,3072]{1,0:T(8,128)(2,1)S(1)}, u32[]{:S(2)}, u32[]{:S(2)}) collective-permute-start(bf16[48,3072]{1,0:T(8,128)(2,1)S(1)} %collective-permute-done.refs_0_.refs_3_), channel_id=1, source_target_pairs={{0,8},{1,9},{2,10},{3,11},{4,12},{5,13},{6,14},{7,15},{8,0},{9,1},... | collective-permute-start | bytes 884744 | tf_op jit(solution)/shard_map/ppermute | solution.py:91
  23.9 11.6 %collective-permute-start.7 = (bf16[48,3072]{1,0:T(8,128)(2,1)S(1)}, bf16[48,3072]{1,0:T(8,128)(2,1)S(1)}, u32[]{:S(2)}, u32[]{:S(2)}) collective-permute-start(bf16[48,3072]{1,0:T(8,128)(2,1)S(1)} %collective-permute-done.5.wait_ref.refs_4_), channel_id=1, source_target_pairs={{0,8},{1,9},{2,10},{3,11},{4,12},{5,13},{6,14},{7,15},{8,0},{9,1},... | collective-permute-start | bytes 884744 | tf_op jit(solution)/shard_map/ppermute | solution.py:91
  25.6 9.8 %collective-permute-start.3 = (bf16[4,96,256]{2,1,0:T(8,128)(2,1)S(1)}, bf16[4,96,256]{2,1,0:T(8,128)(2,1)S(1)}, u32[]{:S(2)}, u32[]{:S(2)}) collective-permute-start(bf16[4,96,256]{2,1,0:T(8,128)(2,1)S(1)} %get-tuple-element.31), channel_id=1, source_target_pairs={{0,4},{1,5},{2,6},{3,7},{4,0},{5,1},{6,2},{7,3},{8,12},{9,13},{10,... | collective-permute-start | bytes 589832 | tf_op jit(solution)/shard_map/ppermute | solution.py:91
  27.1 9.0 %collective-permute-start.4 = (bf16[4,96,256]{2,1,0:T(8,128)(2,1)S(1)}, bf16[4,96,256]{2,1,0:T(8,128)(2,1)S(1)}, u32[]{:S(2)}, u32[]{:S(2)}) collective-permute-start(bf16[4,96,256]{2,1,0:T(8,128)(2,1)S(1)} %get-tuple-element.32), channel_id=1, source_target_pairs={{0,5},{1,4},{2,7},{3,6},{4,1},{5,0},{6,3},{7,2},{8,13},{9,12},{10,... | collective-permute-start | bytes 589832 | tf_op jit(solution)/shard_map/ppermute | solution.py:91
  28.0 9.5 %collective-permute-start.2 = (bf16[4,96,256]{2,1,0:T(8,128)(2,1)S(1)}, bf16[4,96,256]{2,1,0:T(8,128)(2,1)S(1)}, u32[]{:S(2)}, u32[]{:S(2)}) collective-permute-start(bf16[4,96,256]{2,1,0:T(8,128)(2,1)S(1)} %get-tuple-element.30.plane_ref), channel_id=1, source_target_pairs={{0,1},{1,0},{2,3},{3,2},{4,5},{5,4},{6,7},{7,6},{8,9},{9,8},{10,11... | collective-permute-start | bytes 589832 | tf_op jit(solution)/shard_map/ppermute | solution.py:91
  37.6 20.4 %collective-permute-start.15 = (bf16[96,3072]{1,0:T(8,128)(2,1)S(1)}, bf16[96,3072]{1,0:T(8,128)(2,1)S(1)}, u32[]{:S(2)}, u32[]{:S(2)}) collective-permute-start(bf16[96,3072]{1,0:T(8,128)(2,1)S(1)} %get-tuple-element.35.refs_0_), channel_id=1, source_target_pairs={{0,4},{1,5},{2,6},{3,7},{4,0},{5,1},{6,2},{7,3},{8,12},{9,13},{10,... | collective-permute-start | bytes 1769480 | tf_op jit(solution)/shard_map/ppermute | solution.py:91
  39.1 6.2 %collective-permute-start.9 = (bf16[96,256]{1,0:T(8,128)(2,1)S(1)}, bf16[96,256]{1,0:T(8,128)(2,1)S(1)}, u32[]{:S(2)}, u32[]{:S(2)}) collective-permute-start(bf16[96,256]{1,0:T(8,128)(2,1)S(1)} %get-tuple-element.37), channel_id=1, source_target_pairs={{0,8},{1,9},{2,10},{3,11},{4,12},{5,13},{6,14},{7,15},{8,16},{9,17... | collective-permute-start | bytes 147464 | tf_op jit(solution)/shard_map/ppermute | solution.py:91
  39.6 5.7 %collective-permute-start.10 = (bf16[96,256]{1,0:T(8,128)(2,1)S(1)}, bf16[96,256]{1,0:T(8,128)(2,1)S(1)}, u32[]{:S(2)}, u32[]{:S(2)}) collective-permute-start(bf16[96,256]{1,0:T(8,128)(2,1)S(1)} %get-tuple-element.38), channel_id=1, source_target_pairs={{0,16},{1,17},{2,18},{3,19},{4,20},{5,21},{6,22},{7,23},{8,24},{9,... | collective-permute-start | bytes 147464 | tf_op jit(solution)/shard_map/ppermute | solution.py:91
  47.3 6.4 %collective-permute-start.14 = (bf16[96,256]{1,0:T(8,128)(2,1)S(1)}, bf16[96,256]{1,0:T(8,128)(2,1)S(1)}, u32[]{:S(2)}, u32[]{:S(2)}) collective-permute-start(bf16[96,256]{1,0:T(8,128)(2,1)S(1)} %get-tuple-element.40.refs_0_), channel_id=1, source_target_pairs={{0,24},{1,25},{2,26},{3,27},{4,28},{5,29},{6,30},{7,31},{8,0},{9,1... | collective-permute-start | bytes 147464 | tf_op jit(solution)/shard_map/ppermute | solution.py:91
  51.5 5.1 %collective-permute-start.13 = (bf16[96,256]{1,0:T(8,128)(2,1)S(1)}, bf16[96,256]{1,0:T(8,128)(2,1)S(1)}, u32[]{:S(2)}, u32[]{:S(2)}) collective-permute-start(bf16[96,256]{1,0:T(8,128)(2,1)S(1)} %get-tuple-element.40.refs_0_), channel_id=1, source_target_pairs={{0,16},{1,17},{2,18},{3,19},{4,20},{5,21},{6,22},{7,23},{8,24},{9,... | collective-permute-start | bytes 147464 | tf_op jit(solution)/shard_map/ppermute | solution.py:91
  51.5 6.5 %collective-permute-start.12 = (bf16[96,256]{1,0:T(8,128)(2,1)S(1)}, bf16[96,256]{1,0:T(8,128)(2,1)S(1)}, u32[]{:S(2)}, u32[]{:S(2)}) collective-permute-start(bf16[96,256]{1,0:T(8,128)(2,1)S(1)} %get-tuple-element.40.refs_0_), channel_id=1, source_target_pairs={{0,8},{1,9},{2,10},{3,11},{4,12},{5,13},{6,14},{7,15},{8,16},{9,17... | collective-permute-start | bytes 147464 | tf_op jit(solution)/shard_map/ppermute | solution.py:91
  58.1 9.9 %collective-permute-start.19 = (bf16[96,3072]{1,0:T(8,128)(2,1)S(1)}, bf16[96,3072]{1,0:T(8,128)(2,1)S(1)}, u32[]{:S(2)}, u32[]{:S(2)}) collective-permute-start(bf16[96,3072]{1,0:T(8,128)(2,1)S(1)} %get-tuple-element.41.refs_2_), channel_id=1, source_target_pairs={{0,8},{1,9},{2,10},{3,11},{4,12},{5,13},{6,14},{7,15},{8,0},{9,1},... | collective-permute-start | bytes 1769480 | tf_op jit(solution)/shard_map/ppermute | solution.py:91
  58.4 6.6 %collective-permute-start.26 = (bf16[4,96,256]{2,1,0:T(8,128)(2,1)S(1)}, bf16[4,96,256]{2,1,0:T(8,128)(2,1)S(1)}, u32[]{:S(2)}, u32[]{:S(2)}) collective-permute-start(bf16[4,96,256]{2,1,0:T(8,128)(2,1)S(1)} %get-tuple-element.43.refs_0_), channel_id=1, source_target_pairs={{0,5},{1,4},{2,7},{3,6},{4,1},{5,0},{6,3},{7,2},{8,13},{9,12},{10,... | collective-permute-start | bytes 589832 | tf_op jit(solution)/shard_map/ppermute | solution.py:91
  59.2 7.3 %collective-permute-start.24 = (bf16[4,96,256]{2,1,0:T(8,128)(2,1)S(1)}, bf16[4,96,256]{2,1,0:T(8,128)(2,1)S(1)}, u32[]{:S(2)}, u32[]{:S(2)}) collective-permute-start(bf16[4,96,256]{2,1,0:T(8,128)(2,1)S(1)} %get-tuple-element.43.refs_0_), channel_id=1, source_target_pairs={{0,4},{1,5},{2,6},{3,7},{4,0},{5,1},{6,2},{7,3},{8,12},{9,13},{10,... | collective-permute-start | bytes 589832 | tf_op jit(solution)/shard_map/ppermute | solution.py:91
  60.7 6.4 %collective-permute-start.22 = (bf16[4,96,256]{2,1,0:T(8,128)(2,1)S(1)}, bf16[4,96,256]{2,1,0:T(8,128)(2,1)S(1)}, u32[]{:S(2)}, u32[]{:S(2)}) collective-permute-start(bf16[4,96,256]{2,1,0:T(8,128)(2,1)S(1)} %get-tuple-element.43.refs_0_), channel_id=1, source_target_pairs={{0,1},{1,0},{2,3},{3,2},{4,5},{5,4},{6,7},{7,6},{8,9},{9,8},{10,11... | collective-permute-start | bytes 589832 | tf_op jit(solution)/shard_map/ppermute | solution.py:91
  61.9 6.1 %collective-permute-start.21 = (bf16[4,96,256]{2,1,0:T(8,128)(2,1)S(1)}, bf16[4,96,256]{2,1,0:T(8,128)(2,1)S(1)}, u32[]{:S(2)}, u32[]{:S(2)}) collective-permute-start(bf16[4,96,256]{2,1,0:T(8,128)(2,1)S(1)} %get-tuple-element.43.refs_0_), channel_id=1, source_target_pairs={{0,2},{1,3},{2,0},{3,1},{4,6},{5,7},{6,4},{7,5},{8,10},{9,11},{10,... | collective-permute-start | bytes 589832 | tf_op jit(solution)/shard_map/ppermute | solution.py:91
  66.4 8.7 %collective-permute-start.8 = (bf16[96,3072]{1,0:T(8,128)(2,1)S(1)}, bf16[96,3072]{1,0:T(8,128)(2,1)S(1)}, u32[]{:S(2)}, u32[]{:S(2)}) collective-permute-start(bf16[96,3072]{1,0:T(8,128)(2,1)S(1)} %get-tuple-element.35.refs_0_), channel_id=1, source_target_pairs={{0,2},{1,3},{2,0},{3,1},{4,6},{5,7},{6,4},{7,5},{8,10},{9,11},{10,... | collective-permute-start | bytes 1769480 | tf_op jit(solution)/shard_map/ppermute | solution.py:91
  67.1 8.1 %collective-permute-start.16 = (bf16[96,3072]{1,0:T(8,128)(2,1)S(1)}, bf16[96,3072]{1,0:T(8,128)(2,1)S(1)}, u32[]{:S(2)}, u32[]{:S(2)}) collective-permute-start(bf16[96,3072]{1,0:T(8,128)(2,1)S(1)} %get-tuple-element.41.refs_2_), channel_id=1, source_target_pairs={{0,2},{1,3},{2,0},{3,1},{4,6},{5,7},{6,4},{7,5},{8,10},{9,11},{10,... | collective-permute-start | bytes 1769480 | tf_op jit(solution)/shard_map/ppermute | solution.py:91
  68.0 7.2 %collective-permute-start.20 = (bf16[96,3072]{1,0:T(8,128)(2,1)S(1)}, bf16[96,3072]{1,0:T(8,128)(2,1)S(1)}, u32[]{:S(2)}, u32[]{:S(2)}) collective-permute-start(bf16[96,3072]{1,0:T(8,128)(2,1)S(1)} %collective-permute-done.19.refs_8_), channel_id=1, source_target_pairs={{0,2},{1,3},{2,0},{3,1},{4,6},{5,7},{6,4},{7,5},{8,10},{9,11},{10,... | collective-permute-start | bytes 1769480 | tf_op jit(solution)/shard_map/ppermute | solution.py:91
  70.4 4.8 %collective-permute-start.17 = (bf16[48,3072]{1,0:T(8,128)(2,1)S(1)}, bf16[48,3072]{1,0:T(8,128)(2,1)S(1)}, u32[]{:S(2)}, u32[]{:S(2)}) collective-permute-start(bf16[48,3072]{1,0:T(8,128)(2,1)S(1)} %collective-permute-done.6.refs_6_.refs_4_), channel_id=1, source_target_pairs={{0,2},{1,3},{2,0},{3,1},{4,6},{5,7},{6,4},{7,5},{8,10},{9,11},{10,... | collective-permute-start | bytes 884744 | tf_op jit(solution)/shard_map/ppermute | solution.py:91
  70.7 4.5 %collective-permute-start.18 = (bf16[48,3072]{1,0:T(8,128)(2,1)S(1)}, bf16[48,3072]{1,0:T(8,128)(2,1)S(1)}, u32[]{:S(2)}, u32[]{:S(2)}) collective-permute-start(bf16[48,3072]{1,0:T(8,128)(2,1)S(1)} %collective-permute-done.7.refs_7_.refs_6_), channel_id=1, source_target_pairs={{0,2},{1,3},{2,0},{3,1},{4,6},{5,7},{6,4},{7,5},{8,10},{9,11},{10,... | collective-permute-start | bytes 884744 | tf_op jit(solution)/shard_map/ppermute | solution.py:91
  (11 other events, 101.7 us)

commit v5 on v4

--- a/solution.py
+++ b/solution.py
@@ -105,14 +105,15 @@
     def cut(weight, projector):
         rows, width = weight.shape
         eighth = rows // 8
+        large = eighth // 48 * 32
 
         def kernel(w_hbm, p_hbm, first_ref, second_ref, p_ref, sems):
             z, x, c, y = place()
             row = pl.multiple_of(((x * 2 + z % 2) * 2 + c) * eighth, eighth)
             copies = [
-                pltpu.make_async_copy(w_hbm.at[pl.ds(row, eighth // 2)], first_ref, sems.at[0]),
+                pltpu.make_async_copy(w_hbm.at[pl.ds(row, large)], first_ref, sems.at[0]),
                 pltpu.make_async_copy(
-                    w_hbm.at[pl.ds(row + eighth // 2, eighth // 2)], second_ref, sems.at[1]
+                    w_hbm.at[pl.ds(row + large, eighth - large)], second_ref, sems.at[1]
                 ),
                 pltpu.make_async_copy(p_hbm, p_ref, sems.at[2]),
             ]
@@ -121,14 +122,14 @@
             for copy in copies:
                 copy.wait()
 
-        half = shape((eighth // 2, width), BF16)
-        return pl.pallas_call(
-            kernel,
-            out_shape=(half, half, shape(projector.shape, BF16)),
+        parts = (shape((large, width), BF16), shape((eighth - large, width), BF16))
+        return pl.pallas_call(
+            kernel,
+            out_shape=parts + (shape(projector.shape, BF16),),
             in_specs=[HBM, HBM],
             out_specs=(VMEM,) * 3,
             scratch_shapes=[pltpu.SemaphoreType.DMA((3,))],
-            compiler_params=params(54),
+            compiler_params=params(52.5),
             cost_estimate=cost(0, 0),
         )(weight, projector)
 
@@ -305,21 +306,19 @@
             cost_estimate=cost(2 * rows * rank * width, 4 * rows * width),
         )(projector, *[block[3] for block in blocks])
 
-    def own_product(cotangent, weight, *wait):
+    def own_product(cotangent, weight, begin, chunks, into, *wait):
         tokens, width = cotangent.shape
         rows = weight.shape[0]
         step = 256
-        chunks = rows // step
-
-        def kernel(g, w_hbm, wait_ref, plane_ref, out_hbm, done_ref, w, out, sems):
+        operands = [cotangent, weight] + ([] if into is None else [into])
+
+        def kernel(g, w_hbm, *refs):
+            out_hbm, done_ref, w, out, sems = refs[-5:]
             y = lax.axis_index("fsdp")
             copies = []
             for k in range(chunks):
-                copies.append(
-                    pltpu.make_async_copy(
-                        w_hbm.at[pl.ds(k * step, step), :], w.at[k], sems.at[k]
-                    )
-                )
+                span = pl.ds((begin + k) * step, step)
+                copies.append(pltpu.make_async_copy(w_hbm.at[span, :], w.at[k], sems.at[k]))
                 copies[-1].start()
             done_ref[...] = jnp.zeros_like(done_ref)
             outs = []
@@ -328,7 +327,7 @@
                 out[k] = lax.dot_general(
                     g[...], w[k], (((1,), (1,)), ((), ())), preferred_element_type=F32
                 ).astype(BF16)
-                column = pl.multiple_of(y * rows + k * step, step)
+                column = pl.multiple_of(y * rows + (begin + k) * step, step)
                 outs.append(
                     pltpu.make_async_copy(
                         out.at[k], out_hbm.at[:, pl.ds(column, step)], sems.at[chunks + k]
@@ -341,8 +340,9 @@
         return pl.pallas_call(
             kernel,
             out_shape=(shape((tokens, rows * n_y), BF16), shape((8, 128), F32)),
-            in_specs=[VMEM, HBM, ANY, ANY],
+            in_specs=[VMEM] + [HBM] * (len(operands) - 1) + [ANY] * len(wait),
             out_specs=(HBM, VMEM),
+            input_output_aliases={} if into is None else {2: 0},
             scratch_shapes=[
                 pltpu.VMEM((chunks, step, width), BF16),
                 pltpu.VMEM((chunks, tokens, step), BF16),
@@ -350,7 +350,7 @@
             ],
             compiler_params=params(10),
             cost_estimate=cost(2 * tokens * rows * width, 2 * (tokens + rows) * width),
-        )(cotangent, weight, *wait)
+        )(*operands, *wait)
 
     def stack(values, piece, *wait):
         def kernel(*refs):
@@ -438,7 +438,7 @@
     def on_device(attn, cotangent, weight, projector, moment_one, moment_two, step_count):
         shard_rows, width = weight.shape
         own_rows = moment_one.shape[0]
-        if n_y != 2 or own_rows % 16 or shard_rows % 384 or n_z % 2:
+        if n_y != 2 or own_rows % 16 or shard_rows % 768 or n_z % 2:
             return plain(attn, cotangent, weight, projector, moment_one, moment_two, step_count)
         eighth = shard_rows // 8
         first, second, own_projector = cut(weight, projector)
@@ -447,8 +447,11 @@
         over_y.append(to_plane(relay(second, over_y[0]), 0, 1))
         sums = core_sum(keep, to_core(relay(outgoing, over_y[0])))
         got = [to_plane(part, dx, dy) for (dx, dy), part in zip(plane, sums[1:])]
+        over_y[1] = relay(over_y[1], sums[1])
         over_z = [to_z_pair(part) for part in over_y]
-        grad_input, done = own_product(cotangent, weight, over_y[1], sums[1])
+        grad_input, done = own_product(
+            cotangent, weight, 0, shard_rows // 256, None, over_y[1]
+        )
         sums = plane_sum(sums[0], got, over_y, [done] + over_z)
         own = sums[n_z]
 

time: 80.6 us -> 79.2 us (0.983)
  local copies, waits for them, and re-layouts: 1.96 us -> 0.03 us
  starting transfers between devices: 27 us -> 27.9 us
    unnamed x14 -> x10, local copies, waits for them, and re-layouts: 1.96 us -> 0.03 us
    pallas_call x1, Pallas kernels: 2.49 us -> 1.45 us  [cut(): pl.pallas_call(kernel, out_shape=parts + (shape(projector.shape, BF16),),...]
    ppermute x28, starting transfers between devices: 27 us -> 27.9 us  [send(): return lax.ppermute(value, AXES, pairs)]
  transfers between devices with their start and end apart: 28 -> 28, of which waited for: 13 -> 14; matrix products, arithmetic and copies ran while one was open for 0% -> 0% of each run, Pallas kernels for 23% -> 23%
where the time goes in v5:
time: 79.2 us; the launch traced here: 79.1 us
  starting transfers between devices  27.9 us (35%)
  Pallas kernels  25.6 us (32%)
  waiting for transfers between devices  23.9 us (30%)
  between operations  1.65 us (2%)
    ppermute x28, starting transfers between devices, send(): return lax.ppermute(value, AXES, pairs)  27.9 us
    ppermute x28, waiting for transfers between devices, send(): return lax.ppermute(value, AXES, pairs)  23.9 us
    pallas_call x1, Pallas kernels, local_sums(): pl.pallas_call(kernel, out_shape=(shape(dims, BF16), shape(dims, F32)), i...  6.86 us
    pallas_call x1, Pallas kernels, own_product(): pl.pallas_call(kernel, out_shape=(shape((tokens, rows * n_y), BF16), shap...  6.21 us
    pallas_call x1, Pallas kernels, other_product(): pl.pallas_call(kernel, out_shape=shape(into.shape, BF16), in_specs=[VMEM]...  5.59 us
    pallas_call x1, Pallas kernels, step_product(): pl.pallas_call(kernel, out_shape=shape((rows, width), F32), in_specs=[VME...  4.23 us
  transfers between devices with their start and end apart: 28, of which 14 were waited for; matrix products, arithmetic and copies ran while one was open for 0% of the time, Pallas kernels for 23%

profile of v5, /device:TPU:0, one launch (start us, length us, event | category | flops | bytes accessed | tf_op | source)
XLA Modules:
  0.0 79.1 jit_solution(18345375579698713332)
XLA Ops:
  0.6 1.5 %shard_map.102 = (bf16[64,3072]{1,0:T(8,128)(2,1)S(1)}, bf16[32,3072]{1,0:T(8,128)(2,1)S(1)}, bf16[1536,256]{1,0:T(8,128)(2,1)S(1)}) custom-call(bf16[768,3072]{1,0:T(8,128)(2,1)} %w_hbm.3, bf16[1536,256]{1,0:T(8,128)(2,1)} %p_hbm.1), custom_call_target="tpu_custom_call" | custom-call | tf_op jit(solution)/shard_map/pallas_call | solution.py:126
  2.1 3.0 %collective-permute-start = (bf16[64,3072]{1,0:T(8,128)(2,1)S(1)}, bf16[64,3072]{1,0:T(8,128)(2,1)S(1)}, u32[]{:S(2)}, u32[]{:S(2)}) collective-permute-start(bf16[64,3072]{1,0:T(8,128)(2,1)S(1)} %get-tuple-element.28), channel_id=1, source_target_pairs={{0,1},{1,0},{2,3},{3,2},{4,5},{5,4},{6,7},{7,6},{8,9},{9,8},{10,11... | collective-permute-start | bytes 1179656 | tf_op jit(solution)/shard_map/ppermute | solution.py:91
  5.1 6.9 %shard_map.103 = (bf16[2,2,4,96,256]{4,3,2,1,0:T(8,128)(2,1)S(1)}, f32[2,2,4,96,256]{4,3,2,1,0:T(8,128)S(1)}) custom-call(bf16[576,1536]{1,0:T(8,128)(2,1)} %a_hbm.1, bf16[1536,256]{1,0:T(8,128)(2,1)S(1)} %get-tuple-element.25.p.p_ref, bf16[576,3072]{1,0:T(8,128)(2,1)} %g_ref.1), custom_call_target="tpu_custom_call" | custom-call | tf_op jit(solution)/shard_map/pallas_call | solution.py:165
  12.0 2.2 %collective-permute-done.refs_0_.refs_3_ = bf16[64,3072]{1,0:T(8,128)(2,1)S(1)} collective-permute-done((bf16[64,3072]{1,0:T(8,128)(2,1)S(1)}, bf16[64,3072]{1,0:T(8,128)(2,1)S(1)}, u32[]{:S(2)}, u32[]{:S(2)}) %collective-permute-start) | collective-permute-done | bytes 393248 | tf_op jit(solution)/shard_map/ppermute | solution.py:91
  14.4 1.8 %collective-permute-start.5 = (bf16[32,3072]{1,0:T(8,128)(2,1)S(1)}, bf16[32,3072]{1,0:T(8,128)(2,1)S(1)}, u32[]{:S(2)}, u32[]{:S(2)}) collective-permute-start(bf16[32,3072]{1,0:T(8,128)(2,1)S(1)} %shard_map.106), channel_id=1, source_target_pairs={{0,1},{1,0},{2,3},{3,2},{4,5},{5,4},{6,7},{7,6},{8,9},{9,8},{10,11... | collective-permute-start | bytes 589832 | tf_op jit(solution)/shard_map/ppermute | solution.py:91
  16.2 1.6 %collective-permute-start.6 = (bf16[64,3072]{1,0:T(8,128)(2,1)S(1)}, bf16[64,3072]{1,0:T(8,128)(2,1)S(1)}, u32[]{:S(2)}, u32[]{:S(2)}) collective-permute-start(bf16[64,3072]{1,0:T(8,128)(2,1)S(1)} %collective-permute-done.refs_0_.refs_3_), channel_id=1, source_target_pairs={{0,8},{1,9},{2,10},{3,11},{4,12},{5,13},{6,14},{7,15},{8,0},{9,1},... | collective-permute-start | bytes 1179656 | tf_op jit(solution)/shard_map/ppermute | solution.py:91
  17.9 1.6 %collective-permute-start.3 = (bf16[4,96,256]{2,1,0:T(8,128)(2,1)S(1)}, bf16[4,96,256]{2,1,0:T(8,128)(2,1)S(1)}, u32[]{:S(2)}, u32[]{:S(2)}) collective-permute-start(bf16[4,96,256]{2,1,0:T(8,128)(2,1)S(1)} %get-tuple-element.31), channel_id=1, source_target_pairs={{0,4},{1,5},{2,6},{3,7},{4,0},{5,1},{6,2},{7,3},{8,12},{9,13},{10,... | collective-permute-start | bytes 589832 | tf_op jit(solution)/shard_map/ppermute | solution.py:91
  20.1 1.7 %collective-permute-done.5.ref = bf16[32,3072]{1,0:T(8,128)(2,1)S(1)} collective-permute-done((bf16[32,3072]{1,0:T(8,128)(2,1)S(1)}, bf16[32,3072]{1,0:T(8,128)(2,1)S(1)}, u32[]{:S(2)}, u32[]{:S(2)}) %collective-permute-start.5) | collective-permute-done | bytes 196640 | tf_op jit(solution)/shard_map/ppermute | solution.py:91
  21.8 1.9 %collective-permute-start.7 = (bf16[32,3072]{1,0:T(8,128)(2,1)S(1)}, bf16[32,3072]{1,0:T(8,128)(2,1)S(1)}, u32[]{:S(2)}, u32[]{:S(2)}) collective-permute-start(bf16[32,3072]{1,0:T(8,128)(2,1)S(1)} %shard_map.107.refs_0_.refs_4_), channel_id=1, source_target_pairs={{0,8},{1,9},{2,10},{3,11},{4,12},{5,13},{6,14},{7,15},{8,0},{9,1},... | collective-permute-start | bytes 589832 | tf_op jit(solution)/shard_map/ppermute | solution.py:91
  23.7 1.5 %collective-permute-start.2 = (bf16[4,96,256]{2,1,0:T(8,128)(2,1)S(1)}, bf16[4,96,256]{2,1,0:T(8,128)(2,1)S(1)}, u32[]{:S(2)}, u32[]{:S(2)}) collective-permute-start(bf16[4,96,256]{2,1,0:T(8,128)(2,1)S(1)} %get-tuple-element.30.refs_0_), channel_id=1, source_target_pairs={{0,1},{1,0},{2,3},{3,2},{4,5},{5,4},{6,7},{7,6},{8,9},{9,8},{10,11... | collective-permute-start | bytes 589832 | tf_op jit(solution)/shard_map/ppermute | solution.py:91
  25.2 6.2 %shard_map.108 = (bf16[576,1536]{1,0:T(8,128)(2,1)}, f32[8,128]{1,0:T(8,128)S(1)}) custom-call(bf16[576,3072]{1,0:T(8,128)(2,1)S(1)} %copy-done, bf16[768,3072]{1,0:T(8,128)(2,1)S(1)} %bitcast.1, bf16[32,3072]{1,0:T(8,128)(2,1)S(1)} %shard_map.107.refs_0_.refs_4_), custom_call_target="tpu_custom_call" | custom-call | tf_op jit(solution)/shard_map/pallas_call | solution.py:340
  31.7 1.7 %collective-permute-done.2.refs_0_ = bf16[4,96,256]{2,1,0:T(8,128)(2,1)S(1)} collective-permute-done((bf16[4,96,256]{2,1,0:T(8,128)(2,1)S(1)}, bf16[4,96,256]{2,1,0:T(8,128)(2,1)S(1)}, u32[]{:S(2)}, u32[]{:S(2)}) %collective-permute-start.2) | collective-permute-done | bytes 196640 | tf_op jit(solution)/shard_map/ppermute | solution.py:91
  33.5 1.6 %collective-permute-start.15 = (bf16[96,3072]{1,0:T(8,128)(2,1)S(1)}, bf16[96,3072]{1,0:T(8,128)(2,1)S(1)}, u32[]{:S(2)}, u32[]{:S(2)}) collective-permute-start(bf16[96,3072]{1,0:T(8,128)(2,1)S(1)} %get-tuple-element.35.refs_0_), channel_id=1, source_target_pairs={{0,4},{1,5},{2,6},{3,7},{4,0},{5,1},{6,2},{7,3},{8,12},{9,13},{10,... | collective-permute-start | bytes 1769480 | tf_op jit(solution)/shard_map/ppermute | solution.py:91
  36.0 2.6 %collective-permute-start.10 = (bf16[96,256]{1,0:T(8,128)(2,1)S(1)}, bf16[96,256]{1,0:T(8,128)(2,1)S(1)}, u32[]{:S(2)}, u32[]{:S(2)}) collective-permute-start(bf16[96,256]{1,0:T(8,128)(2,1)S(1)} %get-tuple-element.38), channel_id=1, source_target_pairs={{0,16},{1,17},{2,18},{3,19},{4,20},{5,21},{6,22},{7,23},{8,24},{9,... | collective-permute-start | bytes 147464 | tf_op jit(solution)/shard_map/ppermute | solution.py:91
  38.6 1.9 %collective-permute-start.11 = (bf16[96,256]{1,0:T(8,128)(2,1)S(1)}, bf16[96,256]{1,0:T(8,128)(2,1)S(1)}, u32[]{:S(2)}, u32[]{:S(2)}) collective-permute-start(bf16[96,256]{1,0:T(8,128)(2,1)S(1)} %get-tuple-element.39), channel_id=1, source_target_pairs={{0,24},{1,25},{2,26},{3,27},{4,28},{5,29},{6,30},{7,31},{8,0},{9,1... | collective-permute-start | bytes 147464 | tf_op jit(solution)/shard_map/ppermute | solution.py:91
  41.4 1.6 %collective-permute-done.10.refs_1_ = bf16[96,256]{1,0:T(8,128)(2,1)S(1)} collective-permute-done((bf16[96,256]{1,0:T(8,128)(2,1)S(1)}, bf16[96,256]{1,0:T(8,128)(2,1)S(1)}, u32[]{:S(2)}, u32[]{:S(2)}) %collective-permute-start.10) | collective-permute-done | bytes 49184 | tf_op jit(solution)/shard_map/ppermute | solution.py:91
  43.9 3.4 %collective-permute-start.14 = (bf16[96,256]{1,0:T(8,128)(2,1)S(1)}, bf16[96,256]{1,0:T(8,128)(2,1)S(1)}, u32[]{:S(2)}, u32[]{:S(2)}) collective-permute-start(bf16[96,256]{1,0:T(8,128)(2,1)S(1)} %get-tuple-element.40.refs_0_), channel_id=1, source_target_pairs={{0,24},{1,25},{2,26},{3,27},{4,28},{5,29},{6,30},{7,31},{8,0},{9,1... | collective-permute-start | bytes 147464 | tf_op jit(solution)/shard_map/ppermute | solution.py:91
  49.1 3.2 %collective-permute-done.13.refs_2_ = bf16[96,256]{1,0:T(8,128)(2,1)S(1)} collective-permute-done((bf16[96,256]{1,0:T(8,128)(2,1)S(1)}, bf16[96,256]{1,0:T(8,128)(2,1)S(1)}, u32[]{:S(2)}, u32[]{:S(2)}) %collective-permute-start.13) | collective-permute-done | bytes 49184 | tf_op jit(solution)/shard_map/ppermute | solution.py:91
  54.6 1.5 %collective-permute-start.24 = (bf16[4,96,256]{2,1,0:T(8,128)(2,1)S(1)}, bf16[4,96,256]{2,1,0:T(8,128)(2,1)S(1)}, u32[]{:S(2)}, u32[]{:S(2)}) collective-permute-start(bf16[4,96,256]{2,1,0:T(8,128)(2,1)S(1)} %get-tuple-element.43.refs_0_), channel_id=1, source_target_pairs={{0,4},{1,5},{2,6},{3,7},{4,0},{5,1},{6,2},{7,3},{8,12},{9,13},{10,... | collective-permute-start | bytes 589832 | tf_op jit(solution)/shard_map/ppermute | solution.py:91
  56.9 3.9 %collective-permute-done.26.refs_6_ = bf16[4,96,256]{2,1,0:T(8,128)(2,1)S(1)} collective-permute-done((bf16[4,96,256]{2,1,0:T(8,128)(2,1)S(1)}, bf16[4,96,256]{2,1,0:T(8,128)(2,1)S(1)}, u32[]{:S(2)}, u32[]{:S(2)}) %collective-permute-start.26) | collective-permute-done | bytes 196640 | tf_op jit(solution)/shard_map/ppermute | solution.py:91
  63.3 2.7 %collective-permute-done.19.refs_8_ = bf16[96,3072]{1,0:T(8,128)(2,1)S(1)} collective-permute-done((bf16[96,3072]{1,0:T(8,128)(2,1)S(1)}, bf16[96,3072]{1,0:T(8,128)(2,1)S(1)}, u32[]{:S(2)}, u32[]{:S(2)}) %collective-permute-start.19) | collective-permute-done | bytes 589856 | tf_op jit(solution)/shard_map/ppermute | solution.py:91
  66.7 2.3 %collective-permute-done.23.refs_3_ = bf16[4,96,256]{2,1,0:T(8,128)(2,1)S(1)} collective-permute-done((bf16[4,96,256]{2,1,0:T(8,128)(2,1)S(1)}, bf16[4,96,256]{2,1,0:T(8,128)(2,1)S(1)}, u32[]{:S(2)}, u32[]{:S(2)}) %collective-permute-start.23) | collective-permute-done | bytes 196640 | tf_op jit(solution)/shard_map/ppermute | solution.py:91
  69.1 4.2 %shard_map.113 = f32[768,3072]{1,0:T(8,128)} custom-call(bf16[1536,256]{1,0:T(8,128)(2,1)S(1)} %get-tuple-element.25.p.p_ref, bf16[4,96,256]{2,1,0:T(8,128)(2,1)S(1)} %get-tuple-element.43.refs_0_, bf16[4,96,256]{2,1,0:T(8,128)(2,1)S(1)} %collective-permute-done.21.refs_1_, bf16[4,96,256]{2,1,0:T(8,128)(2,1)S(1)} %collective-permute-done.22.refs_2_, ...), custom_call_target="tpu_custom_call" | custom-call | tf_op jit(solution)/shard_map/pallas_call | solution.py:295
  73.3 5.6 %shard_map.112 = bf16[576,1536]{1,0:T(8,128)(2,1)} custom-call(bf16[576,3072]{1,0:T(8,128)(2,1)S(1)} %copy-done, bf16[96,3072]{1,0:T(8,128)(2,1)S(1)} %get-tuple-element.35.refs_0_, bf16[96,3072]{1,0:T(8,128)(2,1)S(1)} %collective-permute-done.8.refs_1_, bf16[96,3072]{1,0:T(8,128)(2,1)S(1)} %get-tuple-element.41.refs_2_, ...), custom_call_target="tpu_custom_call", output_to_operand_aliasing={{}: (11, {})} | custom-call | tf_op jit(solution)/shard_map/pallas_call | solution.py:423
  (55 shorter events, 11.4 us)
Async XLA Ops:
  2.1 12.1 %collective-permute-start = (bf16[64,3072]{1,0:T(8,128)(2,1)S(1)}, bf16[64,3072]{1,0:T(8,128)(2,1)S(1)}, u32[]{:S(2)}, u32[]{:S(2)}) collective-permute-start(bf16[64,3072]{1,0:T(8,128)(2,1)S(1)} %get-tuple-element.28), channel_id=1, source_target_pairs={{0,1},{1,0},{2,3},{3,2},{4,5},{5,4},{6,7},{7,6},{8,9},{9,8},{10,11... | collective-permute-start | bytes 1179656 | tf_op jit(solution)/shard_map/ppermute | solution.py:91
  14.4 7.4 %collective-permute-start.5 = (bf16[32,3072]{1,0:T(8,128)(2,1)S(1)}, bf16[32,3072]{1,0:T(8,128)(2,1)S(1)}, u32[]{:S(2)}, u32[]{:S(2)}) collective-permute-start(bf16[32,3072]{1,0:T(8,128)(2,1)S(1)} %shard_map.106), channel_id=1, source_target_pairs={{0,1},{1,0},{2,3},{3,2},{4,5},{5,4},{6,7},{7,6},{8,9},{9,8},{10,11... | collective-permute-start | bytes 589832 | tf_op jit(solution)/shard_map/ppermute | solution.py:91
  16.2 15.2 %collective-permute-start.6 = (bf16[64,3072]{1,0:T(8,128)(2,1)S(1)}, bf16[64,3072]{1,0:T(8,128)(2,1)S(1)}, u32[]{:S(2)}, u32[]{:S(2)}) collective-permute-start(bf16[64,3072]{1,0:T(8,128)(2,1)S(1)} %collective-permute-done.refs_0_.refs_3_), channel_id=1, source_target_pairs={{0,8},{1,9},{2,10},{3,11},{4,12},{5,13},{6,14},{7,15},{8,0},{9,1},... | collective-permute-start | bytes 1179656 | tf_op jit(solution)/shard_map/ppermute | solution.py:91
  17.9 13.5 %collective-permute-start.3 = (bf16[4,96,256]{2,1,0:T(8,128)(2,1)S(1)}, bf16[4,96,256]{2,1,0:T(8,128)(2,1)S(1)}, u32[]{:S(2)}, u32[]{:S(2)}) collective-permute-start(bf16[4,96,256]{2,1,0:T(8,128)(2,1)S(1)} %get-tuple-element.31), channel_id=1, source_target_pairs={{0,4},{1,5},{2,6},{3,7},{4,0},{5,1},{6,2},{7,3},{8,12},{9,13},{10,... | collective-permute-start | bytes 589832 | tf_op jit(solution)/shard_map/ppermute | solution.py:91
  19.5 12.0 %collective-permute-start.4 = (bf16[4,96,256]{2,1,0:T(8,128)(2,1)S(1)}, bf16[4,96,256]{2,1,0:T(8,128)(2,1)S(1)}, u32[]{:S(2)}, u32[]{:S(2)}) collective-permute-start(bf16[4,96,256]{2,1,0:T(8,128)(2,1)S(1)} %get-tuple-element.32), channel_id=1, source_target_pairs={{0,5},{1,4},{2,7},{3,6},{4,1},{5,0},{6,3},{7,2},{8,13},{9,12},{10,... | collective-permute-start | bytes 589832 | tf_op jit(solution)/shard_map/ppermute | solution.py:91
  21.8 9.9 %collective-permute-start.7 = (bf16[32,3072]{1,0:T(8,128)(2,1)S(1)}, bf16[32,3072]{1,0:T(8,128)(2,1)S(1)}, u32[]{:S(2)}, u32[]{:S(2)}) collective-permute-start(bf16[32,3072]{1,0:T(8,128)(2,1)S(1)} %shard_map.107.refs_0_.refs_4_), channel_id=1, source_target_pairs={{0,8},{1,9},{2,10},{3,11},{4,12},{5,13},{6,14},{7,15},{8,0},{9,1},... | collective-permute-start | bytes 589832 | tf_op jit(solution)/shard_map/ppermute | solution.py:91
  23.7 9.7 %collective-permute-start.2 = (bf16[4,96,256]{2,1,0:T(8,128)(2,1)S(1)}, bf16[4,96,256]{2,1,0:T(8,128)(2,1)S(1)}, u32[]{:S(2)}, u32[]{:S(2)}) collective-permute-start(bf16[4,96,256]{2,1,0:T(8,128)(2,1)S(1)} %get-tuple-element.30.refs_0_), channel_id=1, source_target_pairs={{0,1},{1,0},{2,3},{3,2},{4,5},{5,4},{6,7},{7,6},{8,9},{9,8},{10,11... | collective-permute-start | bytes 589832 | tf_op jit(solution)/shard_map/ppermute | solution.py:91
  33.5 19.7 %collective-permute-start.15 = (bf16[96,3072]{1,0:T(8,128)(2,1)S(1)}, bf16[96,3072]{1,0:T(8,128)(2,1)S(1)}, u32[]{:S(2)}, u32[]{:S(2)}) collective-permute-start(bf16[96,3072]{1,0:T(8,128)(2,1)S(1)} %get-tuple-element.35.refs_0_), channel_id=1, source_target_pairs={{0,4},{1,5},{2,6},{3,7},{4,0},{5,1},{6,2},{7,3},{8,12},{9,13},{10,... | collective-permute-start | bytes 1769480 | tf_op jit(solution)/shard_map/ppermute | solution.py:91
  35.0 6.4 %collective-permute-start.9 = (bf16[96,256]{1,0:T(8,128)(2,1)S(1)}, bf16[96,256]{1,0:T(8,128)(2,1)S(1)}, u32[]{:S(2)}, u32[]{:S(2)}) collective-permute-start(bf16[96,256]{1,0:T(8,128)(2,1)S(1)} %get-tuple-element.37), channel_id=1, source_target_pairs={{0,8},{1,9},{2,10},{3,11},{4,12},{5,13},{6,14},{7,15},{8,16},{9,17... | collective-permute-start | bytes 147464 | tf_op jit(solution)/shard_map/ppermute | solution.py:91
  36.0 7.0 %collective-permute-start.10 = (bf16[96,256]{1,0:T(8,128)(2,1)S(1)}, bf16[96,256]{1,0:T(8,128)(2,1)S(1)}, u32[]{:S(2)}, u32[]{:S(2)}) collective-permute-start(bf16[96,256]{1,0:T(8,128)(2,1)S(1)} %get-tuple-element.38), channel_id=1, source_target_pairs={{0,16},{1,17},{2,18},{3,19},{4,20},{5,21},{6,22},{7,23},{8,24},{9,... | collective-permute-start | bytes 147464 | tf_op jit(solution)/shard_map/ppermute | solution.py:91
  38.6 4.4 %collective-permute-start.11 = (bf16[96,256]{1,0:T(8,128)(2,1)S(1)}, bf16[96,256]{1,0:T(8,128)(2,1)S(1)}, u32[]{:S(2)}, u32[]{:S(2)}) collective-permute-start(bf16[96,256]{1,0:T(8,128)(2,1)S(1)} %get-tuple-element.39), channel_id=1, source_target_pairs={{0,24},{1,25},{2,26},{3,27},{4,28},{5,29},{6,30},{7,31},{8,0},{9,1... | collective-permute-start | bytes 147464 | tf_op jit(solution)/shard_map/ppermute | solution.py:91
  43.9 5.2 %collective-permute-start.14 = (bf16[96,256]{1,0:T(8,128)(2,1)S(1)}, bf16[96,256]{1,0:T(8,128)(2,1)S(1)}, u32[]{:S(2)}, u32[]{:S(2)}) collective-permute-start(bf16[96,256]{1,0:T(8,128)(2,1)S(1)} %get-tuple-element.40.refs_0_), channel_id=1, source_target_pairs={{0,24},{1,25},{2,26},{3,27},{4,28},{5,29},{6,30},{7,31},{8,0},{9,1... | collective-permute-start | bytes 147464 | tf_op jit(solution)/shard_map/ppermute | solution.py:91
  47.3 5.0 %collective-permute-start.13 = (bf16[96,256]{1,0:T(8,128)(2,1)S(1)}, bf16[96,256]{1,0:T(8,128)(2,1)S(1)}, u32[]{:S(2)}, u32[]{:S(2)}) collective-permute-start(bf16[96,256]{1,0:T(8,128)(2,1)S(1)} %get-tuple-element.40.refs_0_), channel_id=1, source_target_pairs={{0,16},{1,17},{2,18},{3,19},{4,20},{5,21},{6,22},{7,23},{8,24},{9,... | collective-permute-start | bytes 147464 | tf_op jit(solution)/shard_map/ppermute | solution.py:91
  47.3 5.9 %collective-permute-start.12 = (bf16[96,256]{1,0:T(8,128)(2,1)S(1)}, bf16[96,256]{1,0:T(8,128)(2,1)S(1)}, u32[]{:S(2)}, u32[]{:S(2)}) collective-permute-start(bf16[96,256]{1,0:T(8,128)(2,1)S(1)} %get-tuple-element.40.refs_0_), channel_id=1, source_target_pairs={{0,8},{1,9},{2,10},{3,11},{4,12},{5,13},{6,14},{7,15},{8,16},{9,17... | collective-permute-start | bytes 147464 | tf_op jit(solution)/shard_map/ppermute | solution.py:91
  53.3 12.8 %collective-permute-start.19 = (bf16[96,3072]{1,0:T(8,128)(2,1)S(1)}, bf16[96,3072]{1,0:T(8,128)(2,1)S(1)}, u32[]{:S(2)}, u32[]{:S(2)}) collective-permute-start(bf16[96,3072]{1,0:T(8,128)(2,1)S(1)} %get-tuple-element.41.refs_2_), channel_id=1, source_target_pairs={{0,8},{1,9},{2,10},{3,11},{4,12},{5,13},{6,14},{7,15},{8,0},{9,1},... | collective-permute-start | bytes 1769480 | tf_op jit(solution)/shard_map/ppermute | solution.py:91
  53.3 7.5 %collective-permute-start.26 = (bf16[4,96,256]{2,1,0:T(8,128)(2,1)S(1)}, bf16[4,96,256]{2,1,0:T(8,128)(2,1)S(1)}, u32[]{:S(2)}, u32[]{:S(2)}) collective-permute-start(bf16[4,96,256]{2,1,0:T(8,128)(2,1)S(1)} %get-tuple-element.43.refs_0_), channel_id=1, source_target_pairs={{0,5},{1,4},{2,7},{3,6},{4,1},{5,0},{6,3},{7,2},{8,13},{9,12},{10,... | collective-permute-start | bytes 589832 | tf_op jit(solution)/shard_map/ppermute | solution.py:91
  54.6 7.6 %collective-permute-start.24 = (bf16[4,96,256]{2,1,0:T(8,128)(2,1)S(1)}, bf16[4,96,256]{2,1,0:T(8,128)(2,1)S(1)}, u32[]{:S(2)}, u32[]{:S(2)}) collective-permute-start(bf16[4,96,256]{2,1,0:T(8,128)(2,1)S(1)} %get-tuple-element.43.refs_0_), channel_id=1, source_target_pairs={{0,4},{1,5},{2,6},{3,7},{4,0},{5,1},{6,2},{7,3},{8,12},{9,13},{10,... | collective-permute-start | bytes 589832 | tf_op jit(solution)/shard_map/ppermute | solution.py:91
  56.1 6.7 %collective-permute-start.22 = (bf16[4,96,256]{2,1,0:T(8,128)(2,1)S(1)}, bf16[4,96,256]{2,1,0:T(8,128)(2,1)S(1)}, u32[]{:S(2)}, u32[]{:S(2)}) collective-permute-start(bf16[4,96,256]{2,1,0:T(8,128)(2,1)S(1)} %get-tuple-element.43.refs_0_), channel_id=1, source_target_pairs={{0,1},{1,0},{2,3},{3,2},{4,5},{5,4},{6,7},{7,6},{8,9},{9,8},{10,11... | collective-permute-start | bytes 589832 | tf_op jit(solution)/shard_map/ppermute | solution.py:91
  56.9 5.9 %collective-permute-start.21 = (bf16[4,96,256]{2,1,0:T(8,128)(2,1)S(1)}, bf16[4,96,256]{2,1,0:T(8,128)(2,1)S(1)}, u32[]{:S(2)}, u32[]{:S(2)}) collective-permute-start(bf16[4,96,256]{2,1,0:T(8,128)(2,1)S(1)} %get-tuple-element.43.refs_0_), channel_id=1, source_target_pairs={{0,2},{1,3},{2,0},{3,1},{4,6},{5,7},{6,4},{7,5},{8,10},{9,11},{10,... | collective-permute-start | bytes 589832 | tf_op jit(solution)/shard_map/ppermute | solution.py:91
  60.8 5.2 %collective-permute-start.27 = (bf16[4,96,256]{2,1,0:T(8,128)(2,1)S(1)}, bf16[4,96,256]{2,1,0:T(8,128)(2,1)S(1)}, u32[]{:S(2)}, u32[]{:S(2)}) collective-permute-start(bf16[4,96,256]{2,1,0:T(8,128)(2,1)S(1)} %collective-permute-done.26.refs_6_), channel_id=1, source_target_pairs={{0,2},{1,3},{2,0},{3,1},{4,6},{5,7},{6,4},{7,5},{8,10},{9,11},{10,... | collective-permute-start | bytes 589832 | tf_op jit(solution)/shard_map/ppermute | solution.py:91
  62.8 10.5 %collective-permute-start.8 = (bf16[96,3072]{1,0:T(8,128)(2,1)S(1)}, bf16[96,3072]{1,0:T(8,128)(2,1)S(1)}, u32[]{:S(2)}, u32[]{:S(2)}) collective-permute-start(bf16[96,3072]{1,0:T(8,128)(2,1)S(1)} %get-tuple-element.35.refs_0_), channel_id=1, source_target_pairs={{0,2},{1,3},{2,0},{3,1},{4,6},{5,7},{6,4},{7,5},{8,10},{9,11},{10,... | collective-permute-start | bytes 1769480 | tf_op jit(solution)/shard_map/ppermute | solution.py:91
  62.8 10.5 %collective-permute-start.16 = (bf16[96,3072]{1,0:T(8,128)(2,1)S(1)}, bf16[96,3072]{1,0:T(8,128)(2,1)S(1)}, u32[]{:S(2)}, u32[]{:S(2)}) collective-permute-start(bf16[96,3072]{1,0:T(8,128)(2,1)S(1)} %get-tuple-element.41.refs_2_), channel_id=1, source_target_pairs={{0,2},{1,3},{2,0},{3,1},{4,6},{5,7},{6,4},{7,5},{8,10},{9,11},{10,... | collective-permute-start | bytes 1769480 | tf_op jit(solution)/shard_map/ppermute | solution.py:91
  66.1 7.3 %collective-permute-start.20 = (bf16[96,3072]{1,0:T(8,128)(2,1)S(1)}, bf16[96,3072]{1,0:T(8,128)(2,1)S(1)}, u32[]{:S(2)}, u32[]{:S(2)}) collective-permute-start(bf16[96,3072]{1,0:T(8,128)(2,1)S(1)} %collective-permute-done.19.refs_8_), channel_id=1, source_target_pairs={{0,2},{1,3},{2,0},{3,1},{4,6},{5,7},{6,4},{7,5},{8,10},{9,11},{10,... | collective-permute-start | bytes 1769480 | tf_op jit(solution)/shard_map/ppermute | solution.py:91
  66.1 7.2 %collective-permute-start.17 = (bf16[64,3072]{1,0:T(8,128)(2,1)S(1)}, bf16[64,3072]{1,0:T(8,128)(2,1)S(1)}, u32[]{:S(2)}, u32[]{:S(2)}) collective-permute-start(bf16[64,3072]{1,0:T(8,128)(2,1)S(1)} %collective-permute-done.6.refs_6_.refs_4_), channel_id=1, source_target_pairs={{0,2},{1,3},{2,0},{3,1},{4,6},{5,7},{6,4},{7,5},{8,10},{9,11},{10,... | collective-permute-start | bytes 1179656 | tf_op jit(solution)/shard_map/ppermute | solution.py:91
  (9 other events, 93.2 us)

commit v6 on v5

--- a/solution.py
+++ b/solution.py
@@ -105,7 +105,7 @@
     def cut(weight, projector):
         rows, width = weight.shape
         eighth = rows // 8
-        large = eighth // 48 * 32
+        large = eighth // 2
 
         def kernel(w_hbm, p_hbm, first_ref, second_ref, p_ref, sems):
             z, x, c, y = place()
@@ -232,9 +232,10 @@
             cost_estimate=cost(4 * own.size, 10 * own.size),
         )(own, *got, *parts, *wait)
 
-    def adam(own, got, moment_one, moment_two, step_count):
+    def adam(own, got, moment_one, moment_two, step_count, wait):
         def kernel(step_ref, own_ref, *refs):
-            got_refs, (m1, m2, first_ref, second_ref, low_ref) = refs[: len(got)], refs[len(got) :]
+            got_refs, (m1, m2) = refs[: len(got)], refs[len(got) : len(got) + 2]
+            first_ref, second_ref, low_ref = refs[-3:]
             projected = own_ref[...]
             for ref in got_refs:
                 projected = projected + ref[...].astype(F32)
@@ -256,20 +257,22 @@
                 shape(dims, F32),
                 shape(dims, BF16),
             ),
-            in_specs=[SMEM] + [VMEM] * (3 + len(got)),
+            in_specs=[SMEM] + [VMEM] * (3 + len(got)) + [ANY] * len(wait),
             out_specs=(VMEM,) * 3,
             compiler_params=params(4),
             cost_estimate=cost(20 * own.size, 24 * own.size),
-        )(step_count, own, *got, moment_one, moment_two)
-
-    def step_product(projector, rows, blocks):
+        )(step_count, own, *got, moment_one, moment_two, *wait)
+
+    def step_product(projector, rows, blocks, wait):
         rank = projector.shape[1]
         own = blocks[0][3].shape[1]
         span = 2 * n_y * own
         width = groups * span
 
         def kernel(p_ref, *refs):
-            columns, (out_hbm, low, out, sems) = refs[: len(blocks)], refs[len(blocks) :]
+            columns, refs = refs[: len(blocks)], refs[len(blocks) + len(wait) :]
+            out_hbm, done_ref, low, out, sems = refs
+            done_ref[...] = jnp.zeros_like(done_ref)
             z, x, c, y = place()
             for (dc, dx, dy, _), ref in zip(blocks, columns):
                 tc, tx, ty = (c + dc) % 2, (x + dx) % 2, (y + n_y - dy) % n_y
@@ -294,9 +297,9 @@
 
         return pl.pallas_call(
             kernel,
-            out_shape=shape((rows, width), F32),
-            in_specs=[VMEM] * (1 + len(blocks)),
-            out_specs=HBM,
+            out_shape=(shape((rows, width), F32), shape((8, 128), F32)),
+            in_specs=[VMEM] * (1 + len(blocks)) + [ANY] * len(wait),
+            out_specs=(HBM, VMEM),
             scratch_shapes=[
                 pltpu.VMEM((groups, span, rank), BF16),
                 pltpu.VMEM((groups, rows, span), F32),
@@ -304,7 +307,7 @@
             ],
             compiler_params=params(16),
             cost_estimate=cost(2 * rows * rank * width, 4 * rows * width),
-        )(projector, *[block[3] for block in blocks])
+        )(projector, *[block[3] for block in blocks], *wait)
 
     def own_product(cotangent, weight, begin, chunks, into, *wait):
         tokens, width = cotangent.shape
@@ -352,41 +355,52 @@
             cost_estimate=cost(2 * tokens * rows * width, 2 * (tokens + rows) * width),
         )(*operands, *wait)
 
-    def stack(values, piece, *wait):
+    def stack(values, pieces):
+        rows, width = sum(piece.shape[0] for piece in pieces), pieces[0].shape[1]
+
         def kernel(*refs):
             out_ref, piece_ref = refs[-2:]
             for k in range(len(values)):
                 out_ref[k] = refs[k][...]
-            piece_ref[...] = refs[len(values)][...]
+            begin = 0
+            for k, piece in enumerate(pieces):
+                piece_ref[begin : begin + piece.shape[0], :] = refs[len(values) + k][...]
+                begin += piece.shape[0]
 
         return pl.pallas_call(
             kernel,
             out_shape=(
                 shape((len(values),) + values[0].shape, values[0].dtype),
-                shape(piece.shape, piece.dtype),
+                shape((rows, width), pieces[0].dtype),
             ),
-            in_specs=[VMEM] * (len(values) + 1) + [ANY] * len(wait),
+            in_specs=[VMEM] * (len(values) + len(pieces)),
             out_specs=(VMEM, VMEM),
             compiler_params=params(4),
-            cost_estimate=cost(0, 2 * values[0].size),
-        )(*values, piece, *wait)
-
-    def relay(value, *wait):
+            cost_estimate=cost(0, 0),
+        )(*values, *pieces)
+
+    def relay(value, wait, sizes=None):
+        counts = sizes or (value.shape[0],)
+
         def kernel(ref, *refs):
-            refs[-1][...] = ref[...]
-
-        return pl.pallas_call(
-            kernel,
-            out_shape=shape(value.shape, value.dtype),
+            outs, begin = refs[len(wait) :], 0
+            for count, out_ref in zip(counts, outs):
+                out_ref[...] = ref[begin : begin + count]
+                begin += count
+
+        copies = pl.pallas_call(
+            kernel,
+            out_shape=tuple(shape((count,) + value.shape[1:], value.dtype) for count in counts),
             in_specs=[VMEM] + [ANY] * len(wait),
-            out_specs=VMEM,
+            out_specs=(VMEM,) * len(counts),
             compiler_params=params(4),
             cost_estimate=cost(0, 2 * value.size),
         )(value, *wait)
+        return copies if sizes else copies[0]
 
     def other_product(cotangent, pieces, into):
         tokens, width = cotangent.shape
-        rows = sum(piece.shape[0] for _, piece in pieces)
+        rows = sum(piece[3] for piece in pieces)
         step = 256 if rows % 256 == 0 else 128
         chunks = rows // step
 
@@ -395,10 +409,13 @@
             out_hbm, w, out, sems = refs[-4:]
             z, x, c, y = place()
             copies = []
-            for k, ((first, piece), ref) in enumerate(zip(pieces, w_refs)):
-                count = piece.shape[0]
+            for k, ((first, _, offset, count), ref) in enumerate(zip(pieces, w_refs)):
                 row = pl.multiple_of(first(z, x, c), 16)
-                copies.append(pltpu.make_async_copy(ref, w.at[pl.ds(row, count)], sems.at[k]))
+                copies.append(
+                    pltpu.make_async_copy(
+                        ref.at[pl.ds(offset, count)], w.at[pl.ds(row, count)], sems.at[k]
+                    )
+                )
                 copies[-1].start()
             for copy in copies:
                 copy.wait()
@@ -433,7 +450,7 @@
             ],
             compiler_params=params(8),
             cost_estimate=cost(2 * tokens * rows * width, 2 * (tokens + rows) * width),
-        )(cotangent, *[piece for _, piece in pieces], into)
+        )(cotangent, *[piece[1] for piece in pieces], into)
 
     def on_device(attn, cotangent, weight, projector, moment_one, moment_two, step_count):
         shard_rows, width = weight.shape
@@ -444,42 +461,50 @@
         first, second, own_projector = cut(weight, projector)
         over_y = [to_plane(first, 0, 1)]
         outgoing, keep = local_sums(attn, own_projector, cotangent)
-        over_y.append(to_plane(relay(second, over_y[0]), 0, 1))
-        sums = core_sum(keep, to_core(relay(outgoing, over_y[0])))
+        over_y.append(to_plane(relay(second, [over_y[0]]), 0, 1))
+        sums = core_sum(keep, to_core(relay(outgoing, [over_y[0]])))
+        over_z = to_z_pair(over_y[0])
         got = [to_plane(part, dx, dy) for (dx, dy), part in zip(plane, sums[1:])]
-        over_y[1] = relay(over_y[1], sums[1])
-        over_z = [to_z_pair(part) for part in over_y]
         grad_input, done = own_product(
-            cotangent, weight, 0, shard_rows // 256, None, over_y[1]
+            cotangent, weight, 0, shard_rows // 256, None, sums[1]
         )
-        sums = plane_sum(sums[0], got, over_y, [done] + over_z)
+        over_y[1] = relay(over_y[1], [done])
+        sums = plane_sum(sums[0], got, over_y, [done, over_z])
         own = sums[n_z]
 
         over_x = to_plane(own, 1, 0)
         got = [to_z(part, dz) for dz, part in zip(range(1, n_z), sums[1:n_z])]
         first_moment, second_moment, low_step = adam(
-            sums[0], got, moment_one, moment_two, step_count
+            sums[0], got, moment_one, moment_two, step_count, []
         )
-        column, over_x = stack(
-            [low_step] + [to_z(low_step, dz) for dz in range(1, n_z)], over_x
+        column, rest = stack(
+            [low_step] + [to_z(low_step, dz) for dz in range(1, n_z)], [over_x, over_y[1]]
         )
-        over_xz = to_z_pair(over_x)
+        rest = to_z_pair(rest)
 
         blocks = [(0, 0, 0, column), (1, 0, 0, to_core(column))]
         for dx, dy in plane:
             got = to_plane(column, dx, dy)
             blocks += [(0, dx, dy, got), (1, dx, dy, to_core(got))]
+        half = eighth // 2
+        other = [to_core(part) for part in (own, over_x, over_z)]
+        weight_step, done = step_product(own_projector, shard_rows, blocks, other)
+        late = relay(rest, [done])
         pieces = []
-        for dx, dz, parts in ((0, 0, [own]), (1, 0, [over_x]), (0, 1, over_z), (1, 1, [over_xz])):
-            begin = 0
-            for part in parts:
-                for dc in range(2):
+        for part, twin, held in (
+            (own, other[0], [(0, 0, 0, eighth)]),
+            (over_x, other[1], [(1, 0, 0, eighth)]),
+            (over_z, other[2], [(0, 1, 0, half)]),
+            (rest, to_core(late), [(1, 1, 0, eighth), (0, 1, half, eighth - half)]),
+        ):
+            for dc, array in enumerate((part, twin)):
+                offset = 0
+                for dx, dz, begin, count in held:
                     row = lambda z, x, c, dx=dx, dz=dz, dc=dc, begin=begin: (
                         (((x + dx) % 2) * 2 + (z + dz) % 2) * 2 + (c + dc) % 2
                     ) * eighth + begin
-                    pieces.append((row, to_core(part) if dc else part))
-                begin += part.shape[0]
-        weight_step = step_product(own_projector, shard_rows, blocks)
+                    pieces.append((row, array, offset, count))
+                    offset += count
         grad_input = other_product(cotangent, pieces, grad_input)
         return grad_input, weight_step, first_moment, second_moment
 

time: 79.2 us -> 77.4 us (0.977)
  starting transfers between devices: 27.9 us -> 25.7 us
  waiting for transfers between devices: 23.9 us -> 24.9 us
    ppermute x28 -> x26, starting transfers between devices: 27.9 us -> 25.7 us  [send(): return lax.ppermute(value, AXES, pairs)]
    ppermute x28 -> x26, waiting for transfers between devices: 23.9 us -> 24.9 us  [send(): return lax.ppermute(value, AXES, pairs)]
    pallas_call x4 -> x5, Pallas kernels: 4.31 us -> 4.38 us  [the longest x1 4.23 us: step_product(): pl.pallas_call(kernel, out_shape=(shape((rows, width), F32), shape((8, 12...]
  transfers between devices with their start and end apart: 28 -> 26, of which waited for: 14 -> 15; matrix products, arithmetic and copies ran while one was open for 0% -> 0% of each run, Pallas kernels for 23% -> 24%
where the time goes in v6:
time: 77.4 us; the launch traced here: 77.3 us
  starting transfers between devices  25.7 us (33%)
  Pallas kernels  25 us (32%)
  waiting for transfers between devices  24.9 us (32%)
  between operations  1.62 us (2%)
    ppermute x26, starting transfers between devices, send(): return lax.ppermute(value, AXES, pairs)  25.7 us
    ppermute x26, waiting for transfers between devices, send(): return lax.ppermute(value, AXES, pairs)  24.9 us
    pallas_call x1, Pallas kernels, local_sums(): pl.pallas_call(kernel, out_shape=(shape(dims, BF16), shape(dims, F32)), i...  6.86 us
    pallas_call x1, Pallas kernels, own_product(): pl.pallas_call(kernel, out_shape=(shape((tokens, rows * n_y), BF16), shap...  6.22 us
    pallas_call x1, Pallas kernels, other_product(): pl.pallas_call(kernel, out_shape=shape(into.shape, BF16), in_specs=[VMEM]...  4.93 us
    pallas_call x1, Pallas kernels, step_product(): pl.pallas_call(kernel, out_shape=(shape((rows, width), F32), shape((8, 12...  4.23 us
  transfers between devices with their start and end apart: 26, of which 15 were waited for; matrix products, arithmetic and copies ran while one was open for 0% of the time, Pallas kernels for 24%

profile of v6, /device:TPU:0, one launch (start us, length us, event | category | flops | bytes accessed | tf_op | source)
XLA Modules:
  0.0 77.3 jit_solution(16654088056720306396)
XLA Ops:
  0.6 1.4 %shard_map.102 = (bf16[48,3072]{1,0:T(8,128)(2,1)S(1)}, bf16[48,3072]{1,0:T(8,128)(2,1)S(1)}, bf16[1536,256]{1,0:T(8,128)(2,1)S(1)}) custom-call(bf16[768,3072]{1,0:T(8,128)(2,1)} %w_hbm.3, bf16[1536,256]{1,0:T(8,128)(2,1)} %p_hbm.1), custom_call_target="tpu_custom_call" | custom-call | tf_op jit(solution)/shard_map/pallas_call | solution.py:126
  2.1 3.0 %collective-permute-start = (bf16[48,3072]{1,0:T(8,128)(2,1)S(1)}, bf16[48,3072]{1,0:T(8,128)(2,1)S(1)}, u32[]{:S(2)}, u32[]{:S(2)}) collective-permute-start(bf16[48,3072]{1,0:T(8,128)(2,1)S(1)} %get-tuple-element.30), channel_id=1, source_target_pairs={{0,1},{1,0},{2,3},{3,2},{4,5},{5,4},{6,7},{7,6},{8,9},{9,8},{10,11... | collective-permute-start | bytes 884744 | tf_op jit(solution)/shard_map/ppermute | solution.py:91
  5.1 6.9 %shard_map.103 = (bf16[2,2,4,96,256]{4,3,2,1,0:T(8,128)(2,1)S(1)}, f32[2,2,4,96,256]{4,3,2,1,0:T(8,128)S(1)}) custom-call(bf16[576,1536]{1,0:T(8,128)(2,1)} %a_hbm.1, bf16[1536,256]{1,0:T(8,128)(2,1)S(1)} %get-tuple-element.27.p.p_ref, bf16[576,3072]{1,0:T(8,128)(2,1)} %g_ref.1), custom_call_target="tpu_custom_call" | custom-call | tf_op jit(solution)/shard_map/pallas_call | solution.py:165
  12.3 1.8 %collective-permute-start.5 = (bf16[48,3072]{1,0:T(8,128)(2,1)S(1)}, bf16[48,3072]{1,0:T(8,128)(2,1)S(1)}, u32[]{:S(2)}, u32[]{:S(2)}) collective-permute-start(bf16[48,3072]{1,0:T(8,128)(2,1)S(1)} %shard_map.106), channel_id=1, source_target_pairs={{0,1},{1,0},{2,3},{3,2},{4,5},{5,4},{6,7},{7,6},{8,9},{9,8},{10,11... | collective-permute-start | bytes 884744 | tf_op jit(solution)/shard_map/ppermute | solution.py:91
  14.1 1.6 %collective-permute-start.6 = (bf16[48,3072]{1,0:T(8,128)(2,1)S(1)}, bf16[48,3072]{1,0:T(8,128)(2,1)S(1)}, u32[]{:S(2)}, u32[]{:S(2)}) collective-permute-start(bf16[48,3072]{1,0:T(8,128)(2,1)S(1)} %collective-permute-done.refs_0_.refs_3_), channel_id=1, source_target_pairs={{0,8},{1,9},{2,10},{3,11},{4,12},{5,13},{6,14},{7,15},{8,0},{9,1},... | collective-permute-start | bytes 884744 | tf_op jit(solution)/shard_map/ppermute | solution.py:91
  15.8 1.6 %collective-permute-start.3 = (bf16[4,96,256]{2,1,0:T(8,128)(2,1)S(1)}, bf16[4,96,256]{2,1,0:T(8,128)(2,1)S(1)}, u32[]{:S(2)}, u32[]{:S(2)}) collective-permute-start(bf16[4,96,256]{2,1,0:T(8,128)(2,1)S(1)} %get-tuple-element.33), channel_id=1, source_target_pairs={{0,4},{1,5},{2,6},{3,7},{4,0},{5,1},{6,2},{7,3},{8,12},{9,13},{10,... | collective-permute-start | bytes 589832 | tf_op jit(solution)/shard_map/ppermute | solution.py:91
  17.9 1.4 %collective-permute-start.2 = (bf16[4,96,256]{2,1,0:T(8,128)(2,1)S(1)}, bf16[4,96,256]{2,1,0:T(8,128)(2,1)S(1)}, u32[]{:S(2)}, u32[]{:S(2)}) collective-permute-start(bf16[4,96,256]{2,1,0:T(8,128)(2,1)S(1)} %get-tuple-element.32.refs_0_), channel_id=1, source_target_pairs={{0,1},{1,0},{2,3},{3,2},{4,5},{5,4},{6,7},{7,6},{8,9},{9,8},{10,11... | collective-permute-start | bytes 589832 | tf_op jit(solution)/shard_map/ppermute | solution.py:91
  19.4 6.2 %shard_map.107 = (bf16[576,1536]{1,0:T(8,128)(2,1)}, f32[8,128]{1,0:T(8,128)S(1)}) custom-call(bf16[576,3072]{1,0:T(8,128)(2,1)S(1)} %copy-done, bf16[768,3072]{1,0:T(8,128)(2,1)S(1)} %bitcast.1, bf16[4,96,256]{2,1,0:T(8,128)(2,1)S(1)} %get-tuple-element.32.refs_0_), custom_call_target="tpu_custom_call" | custom-call | tf_op jit(solution)/shard_map/pallas_call | solution.py:343
  25.7 1.5 %collective-permute-done.4.refs_2_ = bf16[4,96,256]{2,1,0:T(8,128)(2,1)S(1)} collective-permute-done((bf16[4,96,256]{2,1,0:T(8,128)(2,1)S(1)}, bf16[4,96,256]{2,1,0:T(8,128)(2,1)S(1)}, u32[]{:S(2)}, u32[]{:S(2)}) %collective-permute-start.4) | collective-permute-done | bytes 196640 | tf_op jit(solution)/shard_map/ppermute | solution.py:91
  27.2 3.0 %collective-permute-done.2.refs_0_ = bf16[4,96,256]{2,1,0:T(8,128)(2,1)S(1)} collective-permute-done((bf16[4,96,256]{2,1,0:T(8,128)(2,1)S(1)}, bf16[4,96,256]{2,1,0:T(8,128)(2,1)S(1)}, u32[]{:S(2)}, u32[]{:S(2)}) %collective-permute-start.2) | collective-permute-done | bytes 196640 | tf_op jit(solution)/shard_map/ppermute | solution.py:91
  30.3 1.8 %collective-permute-start.8 = (bf16[96,3072]{1,0:T(8,128)(2,1)S(1)}, bf16[96,3072]{1,0:T(8,128)(2,1)S(1)}, u32[]{:S(2)}, u32[]{:S(2)}) collective-permute-start(bf16[96,3072]{1,0:T(8,128)(2,1)S(1)} %get-tuple-element.37.refs_0_), channel_id=1, source_target_pairs={{0,4},{1,5},{2,6},{3,7},{4,0},{5,1},{6,2},{7,3},{8,12},{9,13},{10,... | collective-permute-start | bytes 1769480 | tf_op jit(solution)/shard_map/ppermute | solution.py:91
  32.1 1.6 %collective-permute-start.11 = (bf16[96,256]{1,0:T(8,128)(2,1)S(1)}, bf16[96,256]{1,0:T(8,128)(2,1)S(1)}, u32[]{:S(2)}, u32[]{:S(2)}) collective-permute-start(bf16[96,256]{1,0:T(8,128)(2,1)S(1)} %get-tuple-element.39), channel_id=1, source_target_pairs={{0,8},{1,9},{2,10},{3,11},{4,12},{5,13},{6,14},{7,15},{8,16},{9,17... | collective-permute-start | bytes 147464 | tf_op jit(solution)/shard_map/ppermute | solution.py:91
  33.6 2.6 %collective-permute-start.12 = (bf16[96,256]{1,0:T(8,128)(2,1)S(1)}, bf16[96,256]{1,0:T(8,128)(2,1)S(1)}, u32[]{:S(2)}, u32[]{:S(2)}) collective-permute-start(bf16[96,256]{1,0:T(8,128)(2,1)S(1)} %get-tuple-element.40), channel_id=1, source_target_pairs={{0,16},{1,17},{2,18},{3,19},{4,20},{5,21},{6,22},{7,23},{8,24},{9,... | collective-permute-start | bytes 147464 | tf_op jit(solution)/shard_map/ppermute | solution.py:91
  36.2 1.3 %collective-permute-start.13 = (bf16[96,256]{1,0:T(8,128)(2,1)S(1)}, bf16[96,256]{1,0:T(8,128)(2,1)S(1)}, u32[]{:S(2)}, u32[]{:S(2)}) collective-permute-start(bf16[96,256]{1,0:T(8,128)(2,1)S(1)} %get-tuple-element.41), channel_id=1, source_target_pairs={{0,24},{1,25},{2,26},{3,27},{4,28},{5,29},{6,30},{7,31},{8,0},{9,1... | collective-permute-start | bytes 147464 | tf_op jit(solution)/shard_map/ppermute | solution.py:91
  38.5 1.5 %collective-permute-done.12.refs_1_ = bf16[96,256]{1,0:T(8,128)(2,1)S(1)} collective-permute-done((bf16[96,256]{1,0:T(8,128)(2,1)S(1)}, bf16[96,256]{1,0:T(8,128)(2,1)S(1)}, u32[]{:S(2)}, u32[]{:S(2)}) %collective-permute-start.12) | collective-permute-done | bytes 49184 | tf_op jit(solution)/shard_map/ppermute | solution.py:91
  41.3 3.0 %collective-permute-start.16 = (bf16[96,256]{1,0:T(8,128)(2,1)S(1)}, bf16[96,256]{1,0:T(8,128)(2,1)S(1)}, u32[]{:S(2)}, u32[]{:S(2)}) collective-permute-start(bf16[96,256]{1,0:T(8,128)(2,1)S(1)} %get-tuple-element.42.refs_0_), channel_id=1, source_target_pairs={{0,24},{1,25},{2,26},{3,27},{4,28},{5,29},{6,30},{7,31},{8,0},{9,1... | collective-permute-start | bytes 147464 | tf_op jit(solution)/shard_map/ppermute | solution.py:91
  46.1 3.2 %collective-permute-done.15.refs_2_ = bf16[96,256]{1,0:T(8,128)(2,1)S(1)} collective-permute-done((bf16[96,256]{1,0:T(8,128)(2,1)S(1)}, bf16[96,256]{1,0:T(8,128)(2,1)S(1)}, u32[]{:S(2)}, u32[]{:S(2)}) %collective-permute-start.15) | collective-permute-done | bytes 49184 | tf_op jit(solution)/shard_map/ppermute | solution.py:91
  50.8 1.4 %collective-permute-start.23 = (bf16[4,96,256]{2,1,0:T(8,128)(2,1)S(1)}, bf16[4,96,256]{2,1,0:T(8,128)(2,1)S(1)}, u32[]{:S(2)}, u32[]{:S(2)}) collective-permute-start(bf16[4,96,256]{2,1,0:T(8,128)(2,1)S(1)} %get-tuple-element.44.refs_0_), channel_id=1, source_target_pairs={{0,5},{1,4},{2,7},{3,6},{4,1},{5,0},{6,3},{7,2},{8,13},{9,12},{10,... | collective-permute-start | bytes 589832 | tf_op jit(solution)/shard_map/ppermute | solution.py:91
  52.4 1.6 %collective-permute-start.21 = (bf16[4,96,256]{2,1,0:T(8,128)(2,1)S(1)}, bf16[4,96,256]{2,1,0:T(8,128)(2,1)S(1)}, u32[]{:S(2)}, u32[]{:S(2)}) collective-permute-start(bf16[4,96,256]{2,1,0:T(8,128)(2,1)S(1)} %get-tuple-element.44.refs_0_), channel_id=1, source_target_pairs={{0,4},{1,5},{2,6},{3,7},{4,0},{5,1},{6,2},{7,3},{8,12},{9,13},{10,... | collective-permute-start | bytes 589832 | tf_op jit(solution)/shard_map/ppermute | solution.py:91
  54.6 5.0 %collective-permute-done.23.refs_6_ = bf16[4,96,256]{2,1,0:T(8,128)(2,1)S(1)} collective-permute-done((bf16[4,96,256]{2,1,0:T(8,128)(2,1)S(1)}, bf16[4,96,256]{2,1,0:T(8,128)(2,1)S(1)}, u32[]{:S(2)}, u32[]{:S(2)}) %collective-permute-start.23) | collective-permute-done | bytes 196640 | tf_op jit(solution)/shard_map/ppermute | solution.py:91
  59.6 3.8 %collective-permute-done.21.refs_4_ = bf16[4,96,256]{2,1,0:T(8,128)(2,1)S(1)} collective-permute-done((bf16[4,96,256]{2,1,0:T(8,128)(2,1)S(1)}, bf16[4,96,256]{2,1,0:T(8,128)(2,1)S(1)}, u32[]{:S(2)}, u32[]{:S(2)}) %collective-permute-start.21) | collective-permute-done | bytes 196640 | tf_op jit(solution)/shard_map/ppermute | solution.py:91
  65.4 4.2 %shard_map.112 = (f32[768,3072]{1,0:T(8,128)}, f32[8,128]{1,0:T(8,128)S(1)}) custom-call(bf16[1536,256]{1,0:T(8,128)(2,1)S(1)} %get-tuple-element.27.p.p_ref, bf16[4,96,256]{2,1,0:T(8,128)(2,1)S(1)} %get-tuple-element.44.refs_0_, bf16[4,96,256]{2,1,0:T(8,128)(2,1)S(1)} %collective-permute-done.18.refs_1_, ...), custom_call_target="tpu_custom_call" | custom-call | tf_op jit(solution)/shard_map/pallas_call | solution.py:298
  70.0 2.2 %collective-permute-done.25.refs_8_.refs_9_ = bf16[144,3072]{1,0:T(8,128)(2,1)S(1)} collective-permute-done((bf16[144,3072]{1,0:T(8,128)(2,1)S(1)}, bf16[144,3072]{1,0:T(8,128)(2,1)S(1)}, u32[]{:S(2)}, u32[]{:S(2)}) %collective-permute-start.25) | collective-permute-done | bytes 884768 | tf_op jit(solution)/shard_map/ppermute | solution.py:91
  72.2 4.9 %shard_map.114 = bf16[576,1536]{1,0:T(8,128)(2,1)} custom-call(bf16[576,3072]{1,0:T(8,128)(2,1)S(1)} %copy-done, bf16[96,3072]{1,0:T(8,128)(2,1)S(1)} %get-tuple-element.37.refs_0_, bf16[96,3072]{1,0:T(8,128)(2,1)S(1)} %collective-permute-done.7.refs_8_.refs_1_, ...), custom_call_target="tpu_custom_call", output_to_operand_aliasing={{}: (11, {})} | custom-call | tf_op jit(solution)/shard_map/pallas_call | solution.py:440
  (52 shorter events, 9.0 us)
Async XLA Ops:
  2.1 10.0 %collective-permute-start = (bf16[48,3072]{1,0:T(8,128)(2,1)S(1)}, bf16[48,3072]{1,0:T(8,128)(2,1)S(1)}, u32[]{:S(2)}, u32[]{:S(2)}) collective-permute-start(bf16[48,3072]{1,0:T(8,128)(2,1)S(1)} %get-tuple-element.30), channel_id=1, source_target_pairs={{0,1},{1,0},{2,3},{3,2},{4,5},{5,4},{6,7},{7,6},{8,9},{9,8},{10,11... | collective-permute-start | bytes 884744 | tf_op jit(solution)/shard_map/ppermute | solution.py:91
  12.2 3.5 %collective-permute-start.1 = (bf16[2,2,4,96,256]{4,3,2,1,0:T(8,128)(2,1)S(1)}, bf16[2,2,4,96,256]{4,3,2,1,0:T(8,128)(2,1)S(1)}, u32[]{:S(2)}, u32[]{:S(2)}) collective-permute-start(bf16[2,2,4,96,256]{4,3,2,1,0:T(8,128)(2,1)S(1)} %shard_map.104), channel_id=1, source_target_pairs={{0,2},{1,3},{2,0},{3,1},{4,6},{5,7},{6,4},{7,5},{8,10},{9,11},{10,... | collective-permute-start | bytes 2359304 | tf_op jit(solution)/shard_map/ppermute | solution.py:91
  12.3 13.3 %collective-permute-start.5 = (bf16[48,3072]{1,0:T(8,128)(2,1)S(1)}, bf16[48,3072]{1,0:T(8,128)(2,1)S(1)}, u32[]{:S(2)}, u32[]{:S(2)}) collective-permute-start(bf16[48,3072]{1,0:T(8,128)(2,1)S(1)} %shard_map.106), channel_id=1, source_target_pairs={{0,1},{1,0},{2,3},{3,2},{4,5},{5,4},{6,7},{7,6},{8,9},{9,8},{10,11... | collective-permute-start | bytes 884744 | tf_op jit(solution)/shard_map/ppermute | solution.py:91
  14.1 11.6 %collective-permute-start.6 = (bf16[48,3072]{1,0:T(8,128)(2,1)S(1)}, bf16[48,3072]{1,0:T(8,128)(2,1)S(1)}, u32[]{:S(2)}, u32[]{:S(2)}) collective-permute-start(bf16[48,3072]{1,0:T(8,128)(2,1)S(1)} %collective-permute-done.refs_0_.refs_3_), channel_id=1, source_target_pairs={{0,8},{1,9},{2,10},{3,11},{4,12},{5,13},{6,14},{7,15},{8,0},{9,1},... | collective-permute-start | bytes 884744 | tf_op jit(solution)/shard_map/ppermute | solution.py:91
  15.8 9.9 %collective-permute-start.3 = (bf16[4,96,256]{2,1,0:T(8,128)(2,1)S(1)}, bf16[4,96,256]{2,1,0:T(8,128)(2,1)S(1)}, u32[]{:S(2)}, u32[]{:S(2)}) collective-permute-start(bf16[4,96,256]{2,1,0:T(8,128)(2,1)S(1)} %get-tuple-element.33), channel_id=1, source_target_pairs={{0,4},{1,5},{2,6},{3,7},{4,0},{5,1},{6,2},{7,3},{8,12},{9,13},{10,... | collective-permute-start | bytes 589832 | tf_op jit(solution)/shard_map/ppermute | solution.py:91
  17.4 9.8 %collective-permute-start.4 = (bf16[4,96,256]{2,1,0:T(8,128)(2,1)S(1)}, bf16[4,96,256]{2,1,0:T(8,128)(2,1)S(1)}, u32[]{:S(2)}, u32[]{:S(2)}) collective-permute-start(bf16[4,96,256]{2,1,0:T(8,128)(2,1)S(1)} %get-tuple-element.34), channel_id=1, source_target_pairs={{0,5},{1,4},{2,7},{3,6},{4,1},{5,0},{6,3},{7,2},{8,13},{9,12},{10,... | collective-permute-start | bytes 589832 | tf_op jit(solution)/shard_map/ppermute | solution.py:91
  17.9 12.2 %collective-permute-start.2 = (bf16[4,96,256]{2,1,0:T(8,128)(2,1)S(1)}, bf16[4,96,256]{2,1,0:T(8,128)(2,1)S(1)}, u32[]{:S(2)}, u32[]{:S(2)}) collective-permute-start(bf16[4,96,256]{2,1,0:T(8,128)(2,1)S(1)} %get-tuple-element.32.refs_0_), channel_id=1, source_target_pairs={{0,1},{1,0},{2,3},{3,2},{4,5},{5,4},{6,7},{7,6},{8,9},{9,8},{10,11... | collective-permute-start | bytes 589832 | tf_op jit(solution)/shard_map/ppermute | solution.py:91
  30.3 20.3 %collective-permute-start.8 = (bf16[96,3072]{1,0:T(8,128)(2,1)S(1)}, bf16[96,3072]{1,0:T(8,128)(2,1)S(1)}, u32[]{:S(2)}, u32[]{:S(2)}) collective-permute-start(bf16[96,3072]{1,0:T(8,128)(2,1)S(1)} %get-tuple-element.37.refs_0_), channel_id=1, source_target_pairs={{0,4},{1,5},{2,6},{3,7},{4,0},{5,1},{6,2},{7,3},{8,12},{9,13},{10,... | collective-permute-start | bytes 1769480 | tf_op jit(solution)/shard_map/ppermute | solution.py:91
  32.1 6.4 %collective-permute-start.11 = (bf16[96,256]{1,0:T(8,128)(2,1)S(1)}, bf16[96,256]{1,0:T(8,128)(2,1)S(1)}, u32[]{:S(2)}, u32[]{:S(2)}) collective-permute-start(bf16[96,256]{1,0:T(8,128)(2,1)S(1)} %get-tuple-element.39), channel_id=1, source_target_pairs={{0,8},{1,9},{2,10},{3,11},{4,12},{5,13},{6,14},{7,15},{8,16},{9,17... | collective-permute-start | bytes 147464 | tf_op jit(solution)/shard_map/ppermute | solution.py:91
  33.6 6.4 %collective-permute-start.12 = (bf16[96,256]{1,0:T(8,128)(2,1)S(1)}, bf16[96,256]{1,0:T(8,128)(2,1)S(1)}, u32[]{:S(2)}, u32[]{:S(2)}) collective-permute-start(bf16[96,256]{1,0:T(8,128)(2,1)S(1)} %get-tuple-element.40), channel_id=1, source_target_pairs={{0,16},{1,17},{2,18},{3,19},{4,20},{5,21},{6,22},{7,23},{8,24},{9,... | collective-permute-start | bytes 147464 | tf_op jit(solution)/shard_map/ppermute | solution.py:91
  36.2 4.2 %collective-permute-start.13 = (bf16[96,256]{1,0:T(8,128)(2,1)S(1)}, bf16[96,256]{1,0:T(8,128)(2,1)S(1)}, u32[]{:S(2)}, u32[]{:S(2)}) collective-permute-start(bf16[96,256]{1,0:T(8,128)(2,1)S(1)} %get-tuple-element.41), channel_id=1, source_target_pairs={{0,24},{1,25},{2,26},{3,27},{4,28},{5,29},{6,30},{7,31},{8,0},{9,1... | collective-permute-start | bytes 147464 | tf_op jit(solution)/shard_map/ppermute | solution.py:91
  37.6 16.5 %collective-permute-start.7 = (bf16[96,3072]{1,0:T(8,128)(2,1)S(1)}, bf16[96,3072]{1,0:T(8,128)(2,1)S(1)}, u32[]{:S(2)}, u32[]{:S(2)}) collective-permute-start(bf16[96,3072]{1,0:T(8,128)(2,1)S(1)} %get-tuple-element.37.refs_0_), channel_id=1, source_target_pairs={{0,2},{1,3},{2,0},{3,1},{4,6},{5,7},{6,4},{7,5},{8,10},{9,11},{10,... | collective-permute-start | bytes 1769480 | tf_op jit(solution)/shard_map/ppermute | solution.py:91
  41.3 4.8 %collective-permute-start.16 = (bf16[96,256]{1,0:T(8,128)(2,1)S(1)}, bf16[96,256]{1,0:T(8,128)(2,1)S(1)}, u32[]{:S(2)}, u32[]{:S(2)}) collective-permute-start(bf16[96,256]{1,0:T(8,128)(2,1)S(1)} %get-tuple-element.42.refs_0_), channel_id=1, source_target_pairs={{0,24},{1,25},{2,26},{3,27},{4,28},{5,29},{6,30},{7,31},{8,0},{9,1... | collective-permute-start | bytes 147464 | tf_op jit(solution)/shard_map/ppermute | solution.py:91
  44.4 5.0 %collective-permute-start.15 = (bf16[96,256]{1,0:T(8,128)(2,1)S(1)}, bf16[96,256]{1,0:T(8,128)(2,1)S(1)}, u32[]{:S(2)}, u32[]{:S(2)}) collective-permute-start(bf16[96,256]{1,0:T(8,128)(2,1)S(1)} %get-tuple-element.42.refs_0_), channel_id=1, source_target_pairs={{0,16},{1,17},{2,18},{3,19},{4,20},{5,21},{6,22},{7,23},{8,24},{9,... | collective-permute-start | bytes 147464 | tf_op jit(solution)/shard_map/ppermute | solution.py:91
  44.4 6.2 %collective-permute-start.14 = (bf16[96,256]{1,0:T(8,128)(2,1)S(1)}, bf16[96,256]{1,0:T(8,128)(2,1)S(1)}, u32[]{:S(2)}, u32[]{:S(2)}) collective-permute-start(bf16[96,256]{1,0:T(8,128)(2,1)S(1)} %get-tuple-element.42.refs_0_), channel_id=1, source_target_pairs={{0,8},{1,9},{2,10},{3,11},{4,12},{5,13},{6,14},{7,15},{8,16},{9,17... | collective-permute-start | bytes 147464 | tf_op jit(solution)/shard_map/ppermute | solution.py:91
  50.7 18.9 %collective-permute-start.17 = (bf16[144,3072]{1,0:T(8,128)(2,1)S(1)}, bf16[144,3072]{1,0:T(8,128)(2,1)S(1)}, u32[]{:S(2)}, u32[]{:S(2)}) collective-permute-start(bf16[144,3072]{1,0:T(8,128)(2,1)S(1)} %get-tuple-element.43), channel_id=1, source_target_pairs={{0,8},{1,9},{2,10},{3,11},{4,12},{5,13},{6,14},{7,15},{8,0},{9,1},... | collective-permute-start | bytes 2654216 | tf_op jit(solution)/shard_map/ppermute | solution.py:91
  50.8 1.6 %collective-permute-start.10 = (bf16[48,3072]{1,0:T(8,128)(2,1)S(1)}, bf16[48,3072]{1,0:T(8,128)(2,1)S(1)}, u32[]{:S(2)}, u32[]{:S(2)}) collective-permute-start(bf16[48,3072]{1,0:T(8,128)(2,1)S(1)} %collective-permute-done.6.refs_6_.refs_4_), channel_id=1, source_target_pairs={{0,2},{1,3},{2,0},{3,1},{4,6},{5,7},{6,4},{7,5},{8,10},{9,11},{10,... | collective-permute-start | bytes 884744 | tf_op jit(solution)/shard_map/ppermute | solution.py:91
  50.8 8.7 %collective-permute-start.23 = (bf16[4,96,256]{2,1,0:T(8,128)(2,1)S(1)}, bf16[4,96,256]{2,1,0:T(8,128)(2,1)S(1)}, u32[]{:S(2)}, u32[]{:S(2)}) collective-permute-start(bf16[4,96,256]{2,1,0:T(8,128)(2,1)S(1)} %get-tuple-element.44.refs_0_), channel_id=1, source_target_pairs={{0,5},{1,4},{2,7},{3,6},{4,1},{5,0},{6,3},{7,2},{8,13},{9,12},{10,... | collective-permute-start | bytes 589832 | tf_op jit(solution)/shard_map/ppermute | solution.py:91
  52.2 13.2 %collective-permute-start.9 = (bf16[96,3072]{1,0:T(8,128)(2,1)S(1)}, bf16[96,3072]{1,0:T(8,128)(2,1)S(1)}, u32[]{:S(2)}, u32[]{:S(2)}) collective-permute-start(bf16[96,3072]{1,0:T(8,128)(2,1)S(1)} %collective-permute-done.8.refs_4_.refs_2_), channel_id=1, source_target_pairs={{0,2},{1,3},{2,0},{3,1},{4,6},{5,7},{6,4},{7,5},{8,10},{9,11},{10,... | collective-permute-start | bytes 1769480 | tf_op jit(solution)/shard_map/ppermute | solution.py:91
  52.4 11.0 %collective-permute-start.21 = (bf16[4,96,256]{2,1,0:T(8,128)(2,1)S(1)}, bf16[4,96,256]{2,1,0:T(8,128)(2,1)S(1)}, u32[]{:S(2)}, u32[]{:S(2)}) collective-permute-start(bf16[4,96,256]{2,1,0:T(8,128)(2,1)S(1)} %get-tuple-element.44.refs_0_), channel_id=1, source_target_pairs={{0,4},{1,5},{2,6},{3,7},{4,0},{5,1},{6,2},{7,3},{8,12},{9,13},{10,... | collective-permute-start | bytes 589832 | tf_op jit(solution)/shard_map/ppermute | solution.py:91
  54.1 9.3 %collective-permute-start.19 = (bf16[4,96,256]{2,1,0:T(8,128)(2,1)S(1)}, bf16[4,96,256]{2,1,0:T(8,128)(2,1)S(1)}, u32[]{:S(2)}, u32[]{:S(2)}) collective-permute-start(bf16[4,96,256]{2,1,0:T(8,128)(2,1)S(1)} %get-tuple-element.44.refs_0_), channel_id=1, source_target_pairs={{0,1},{1,0},{2,3},{3,2},{4,5},{5,4},{6,7},{7,6},{8,9},{9,8},{10,11... | collective-permute-start | bytes 589832 | tf_op jit(solution)/shard_map/ppermute | solution.py:91
  59.6 4.3 %collective-permute-start.18 = (bf16[4,96,256]{2,1,0:T(8,128)(2,1)S(1)}, bf16[4,96,256]{2,1,0:T(8,128)(2,1)S(1)}, u32[]{:S(2)}, u32[]{:S(2)}) collective-permute-start(bf16[4,96,256]{2,1,0:T(8,128)(2,1)S(1)} %get-tuple-element.44.refs_0_), channel_id=1, source_target_pairs={{0,2},{1,3},{2,0},{3,1},{4,6},{5,7},{6,4},{7,5},{8,10},{9,11},{10,... | collective-permute-start | bytes 589832 | tf_op jit(solution)/shard_map/ppermute | solution.py:91
  63.4 1.7 %collective-permute-start.22 = (bf16[4,96,256]{2,1,0:T(8,128)(2,1)S(1)}, bf16[4,96,256]{2,1,0:T(8,128)(2,1)S(1)}, u32[]{:S(2)}, u32[]{:S(2)}) collective-permute-start(bf16[4,96,256]{2,1,0:T(8,128)(2,1)S(1)} %collective-permute-done.21.refs_4_), channel_id=1, source_target_pairs={{0,2},{1,3},{2,0},{3,1},{4,6},{5,7},{6,4},{7,5},{8,10},{9,11},{10,... | collective-permute-start | bytes 589832 | tf_op jit(solution)/shard_map/ppermute | solution.py:91
  69.7 2.5 %collective-permute-start.25 = (bf16[144,3072]{1,0:T(8,128)(2,1)S(1)}, bf16[144,3072]{1,0:T(8,128)(2,1)S(1)}, u32[]{:S(2)}, u32[]{:S(2)}) collective-permute-start(bf16[144,3072]{1,0:T(8,128)(2,1)S(1)} %shard_map.113), channel_id=1, source_target_pairs={{0,2},{1,3},{2,0},{3,1},{4,6},{5,7},{6,4},{7,5},{8,10},{9,11},{10,... | collective-permute-start | bytes 2654216 | tf_op jit(solution)/shard_map/ppermute | solution.py:91
  (7 other events, 72.8 us)

commit v7 on v6

--- a/solution.py
+++ b/solution.py
@@ -263,14 +263,14 @@
             cost_estimate=cost(20 * own.size, 24 * own.size),
         )(step_count, own, *got, moment_one, moment_two, *wait)
 
-    def step_product(projector, rows, blocks, wait):
+    def step_product(projector, rows, blocks, wait, begin, count, into=None):
         rank = projector.shape[1]
         own = blocks[0][3].shape[1]
         span = 2 * n_y * own
         width = groups * span
 
         def kernel(p_ref, *refs):
-            columns, refs = refs[: len(blocks)], refs[len(blocks) + len(wait) :]
+            columns, refs = refs[: len(blocks)], refs[len(blocks) + len(wait) + (into is not None) :]
             out_hbm, done_ref, low, out, sems = refs
             done_ref[...] = jnp.zeros_like(done_ref)
             z, x, c, y = place()
@@ -281,15 +281,15 @@
                     row = pl.multiple_of((tc * n_y + ty) * own, own)
                     low[tz * 2 + tx, pl.ds(row, own), :] = ref[dz]
             copies = []
-            for k in range(groups):
+            for k in range(count):
                 out[k] = 0.25 * lax.dot_general(
                     p_ref[pl.ds(pl.multiple_of(y * rows, 16), rows), :],
-                    low[k],
+                    low[begin + k],
                     (((1,), (1,)), ((), ())),
                     preferred_element_type=F32,
                 )
                 copies.append(
-                    pltpu.make_async_copy(out.at[k], out_hbm.at[:, pl.ds(k * span, span)], sems.at[k])
+                    pltpu.make_async_copy(out.at[k], out_hbm.at[:, pl.ds((begin + k) * span, span)], sems.at[k])
                 )
                 copies[-1].start()
             for copy in copies:
@@ -298,16 +298,19 @@
         return pl.pallas_call(
             kernel,
             out_shape=(shape((rows, width), F32), shape((8, 128), F32)),
-            in_specs=[VMEM] * (1 + len(blocks)) + [ANY] * len(wait),
+            in_specs=[VMEM] * (1 + len(blocks))
+            + [ANY] * len(wait)
+            + [HBM] * (into is not None),
             out_specs=(HBM, VMEM),
+            input_output_aliases={} if into is None else {1 + len(blocks) + len(wait): 0},
             scratch_shapes=[
                 pltpu.VMEM((groups, span, rank), BF16),
-                pltpu.VMEM((groups, rows, span), F32),
-                pltpu.SemaphoreType.DMA((groups,)),
+                pltpu.VMEM((count, rows, span), F32),
+                pltpu.SemaphoreType.DMA((count,)),
             ],
             compiler_params=params(16),
             cost_estimate=cost(2 * rows * rank * width, 4 * rows * width),
-        )(projector, *[block[3] for block in blocks], *wait)
+        )(projector, *[block[3] for block in blocks], *wait, *([] if into is None else [into]))
 
     def own_product(cotangent, weight, begin, chunks, into, *wait):
         tokens, width = cotangent.shape
@@ -488,8 +491,13 @@
             blocks += [(0, dx, dy, got), (1, dx, dy, to_core(got))]
         half = eighth // 2
         other = [to_core(part) for part in (own, over_x, over_z)]
-        weight_step, done = step_product(own_projector, shard_rows, blocks, other)
+        weight_step, done = step_product(
+            own_projector, shard_rows, blocks, other[:2], 0, groups // 2
+        )
         late = relay(rest, [done])
+        weight_step, done = step_product(
+            own_projector, shard_rows, blocks, [late], groups // 2, groups // 2, weight_step
+        )
         pieces = []
         for part, twin, held in (
             (own, other[0], [(0, 0, 0, eighth)]),

time: 77.4 us -> 77.1 us (level)
  waiting for transfers between devices: 24.9 us -> 22.4 us
  Pallas kernels: 25 us -> 26.9 us
    ppermute x26, waiting for transfers between devices: 24.9 us -> 22.4 us  [send(): return lax.ppermute(value, AXES, pairs)]
    pallas_call x1 -> x2, Pallas kernels: 4.23 us -> 6.06 us  [step_product(): pl.pallas_call(kernel, out_shape=(shape((rows, width), F32), shape((8, 12...]
  transfers between devices with their start and end apart: 26 -> 26, of which waited for: 15 -> 13; matrix products, arithmetic and copies ran while one was open for 0% -> 0% of each run, Pallas kernels for 24% -> 26%
where the time goes in v7:
time: 77.1 us; the launch traced here: 77 us
  Pallas kernels  26.9 us (35%)
  starting transfers between devices  26.1 us (34%)
  waiting for transfers between devices  22.4 us (29%)
  between operations  1.62 us (2%)
    ppermute x26, starting transfers between devices, send(): return lax.ppermute(value, AXES, pairs)  26.1 us
    ppermute x26, waiting for transfers between devices, send(): return lax.ppermute(value, AXES, pairs)  22.4 us
    pallas_call x1, Pallas kernels, local_sums(): pl.pallas_call(kernel, out_shape=(shape(dims, BF16), shape(dims, F32)), i...  6.86 us
    pallas_call x1, Pallas kernels, own_product(): pl.pallas_call(kernel, out_shape=(shape((tokens, rows * n_y), BF16), shap...  6.23 us
    pallas_call x2, Pallas kernels, step_product(): pl.pallas_call(kernel, out_shape=(shape((rows, width), F32), shape((8, 12...  6.06 us
    pallas_call x1, Pallas kernels, other_product(): pl.pallas_call(kernel, out_shape=shape(into.shape, BF16), in_specs=[VMEM]...  4.97 us
  transfers between devices with their start and end apart: 26, of which 13 were waited for; matrix products, arithmetic and copies ran while one was open for 0% of the time, Pallas kernels for 26%

profile of v7, /device:TPU:0, one launch (start us, length us, event | category | flops | bytes accessed | tf_op | source)
XLA Modules:
  0.0 77.0 jit_solution(4990757578951832568)
XLA Ops:
  0.6 1.4 %shard_map.102 = (bf16[48,3072]{1,0:T(8,128)(2,1)S(1)}, bf16[48,3072]{1,0:T(8,128)(2,1)S(1)}, bf16[1536,256]{1,0:T(8,128)(2,1)S(1)}) custom-call(bf16[768,3072]{1,0:T(8,128)(2,1)} %w_hbm.3, bf16[1536,256]{1,0:T(8,128)(2,1)} %p_hbm.1), custom_call_target="tpu_custom_call" | custom-call | tf_op jit(solution)/shard_map/pallas_call | solution.py:126
  2.1 3.0 %collective-permute-start = (bf16[48,3072]{1,0:T(8,128)(2,1)S(1)}, bf16[48,3072]{1,0:T(8,128)(2,1)S(1)}, u32[]{:S(2)}, u32[]{:S(2)}) collective-permute-start(bf16[48,3072]{1,0:T(8,128)(2,1)S(1)} %get-tuple-element.31), channel_id=1, source_target_pairs={{0,1},{1,0},{2,3},{3,2},{4,5},{5,4},{6,7},{7,6},{8,9},{9,8},{10,11... | collective-permute-start | bytes 884744 | tf_op jit(solution)/shard_map/ppermute | solution.py:91
  5.1 6.9 %shard_map.103 = (bf16[2,2,4,96,256]{4,3,2,1,0:T(8,128)(2,1)S(1)}, f32[2,2,4,96,256]{4,3,2,1,0:T(8,128)S(1)}) custom-call(bf16[576,1536]{1,0:T(8,128)(2,1)} %a_hbm.1, bf16[1536,256]{1,0:T(8,128)(2,1)S(1)} %get-tuple-element.28.p.p_ref, bf16[576,3072]{1,0:T(8,128)(2,1)} %g_ref.1), custom_call_target="tpu_custom_call" | custom-call | tf_op jit(solution)/shard_map/pallas_call | solution.py:165
  12.3 1.8 %collective-permute-start.5 = (bf16[48,3072]{1,0:T(8,128)(2,1)S(1)}, bf16[48,3072]{1,0:T(8,128)(2,1)S(1)}, u32[]{:S(2)}, u32[]{:S(2)}) collective-permute-start(bf16[48,3072]{1,0:T(8,128)(2,1)S(1)} %shard_map.106), channel_id=1, source_target_pairs={{0,1},{1,0},{2,3},{3,2},{4,5},{5,4},{6,7},{7,6},{8,9},{9,8},{10,11... | collective-permute-start | bytes 884744 | tf_op jit(solution)/shard_map/ppermute | solution.py:91
  14.1 1.6 %collective-permute-start.6 = (bf16[48,3072]{1,0:T(8,128)(2,1)S(1)}, bf16[48,3072]{1,0:T(8,128)(2,1)S(1)}, u32[]{:S(2)}, u32[]{:S(2)}) collective-permute-start(bf16[48,3072]{1,0:T(8,128)(2,1)S(1)} %collective-permute-done.refs_0_.refs_3_), channel_id=1, source_target_pairs={{0,8},{1,9},{2,10},{3,11},{4,12},{5,13},{6,14},{7,15},{8,0},{9,1},... | collective-permute-start | bytes 884744 | tf_op jit(solution)/shard_map/ppermute | solution.py:91
  16.5 1.5 %collective-permute-start.3 = (bf16[4,96,256]{2,1,0:T(8,128)(2,1)S(1)}, bf16[4,96,256]{2,1,0:T(8,128)(2,1)S(1)}, u32[]{:S(2)}, u32[]{:S(2)}) collective-permute-start(bf16[4,96,256]{2,1,0:T(8,128)(2,1)S(1)} %get-tuple-element.34), channel_id=1, source_target_pairs={{0,4},{1,5},{2,6},{3,7},{4,0},{5,1},{6,2},{7,3},{8,12},{9,13},{10,... | collective-permute-start | bytes 589832 | tf_op jit(solution)/shard_map/ppermute | solution.py:91
  19.4 6.2 %shard_map.107 = (bf16[576,1536]{1,0:T(8,128)(2,1)}, f32[8,128]{1,0:T(8,128)S(1)}) custom-call(bf16[576,3072]{1,0:T(8,128)(2,1)S(1)} %copy-done, bf16[768,3072]{1,0:T(8,128)(2,1)S(1)} %bitcast.1, bf16[4,96,256]{2,1,0:T(8,128)(2,1)S(1)} %get-tuple-element.33.refs_0_), custom_call_target="tpu_custom_call" | custom-call | tf_op jit(solution)/shard_map/pallas_call | solution.py:346
  25.6 4.5 %collective-permute-done.2.refs_0_ = bf16[4,96,256]{2,1,0:T(8,128)(2,1)S(1)} collective-permute-done((bf16[4,96,256]{2,1,0:T(8,128)(2,1)S(1)}, bf16[4,96,256]{2,1,0:T(8,128)(2,1)S(1)}, u32[]{:S(2)}, u32[]{:S(2)}) %collective-permute-start.2) | collective-permute-done | bytes 196640 | tf_op jit(solution)/shard_map/ppermute | solution.py:91
  30.3 1.8 %collective-permute-start.8 = (bf16[96,3072]{1,0:T(8,128)(2,1)S(1)}, bf16[96,3072]{1,0:T(8,128)(2,1)S(1)}, u32[]{:S(2)}, u32[]{:S(2)}) collective-permute-start(bf16[96,3072]{1,0:T(8,128)(2,1)S(1)} %get-tuple-element.38.refs_0_), channel_id=1, source_target_pairs={{0,4},{1,5},{2,6},{3,7},{4,0},{5,1},{6,2},{7,3},{8,12},{9,13},{10,... | collective-permute-start | bytes 1769480 | tf_op jit(solution)/shard_map/ppermute | solution.py:91
  32.1 1.6 %collective-permute-start.11 = (bf16[96,256]{1,0:T(8,128)(2,1)S(1)}, bf16[96,256]{1,0:T(8,128)(2,1)S(1)}, u32[]{:S(2)}, u32[]{:S(2)}) collective-permute-start(bf16[96,256]{1,0:T(8,128)(2,1)S(1)} %get-tuple-element.40), channel_id=1, source_target_pairs={{0,8},{1,9},{2,10},{3,11},{4,12},{5,13},{6,14},{7,15},{8,16},{9,17... | collective-permute-start | bytes 147464 | tf_op jit(solution)/shard_map/ppermute | solution.py:91
  33.7 2.6 %collective-permute-start.12 = (bf16[96,256]{1,0:T(8,128)(2,1)S(1)}, bf16[96,256]{1,0:T(8,128)(2,1)S(1)}, u32[]{:S(2)}, u32[]{:S(2)}) collective-permute-start(bf16[96,256]{1,0:T(8,128)(2,1)S(1)} %get-tuple-element.41), channel_id=1, source_target_pairs={{0,16},{1,17},{2,18},{3,19},{4,20},{5,21},{6,22},{7,23},{8,24},{9,... | collective-permute-start | bytes 147464 | tf_op jit(solution)/shard_map/ppermute | solution.py:91
  38.5 1.5 %collective-permute-done.12.refs_1_ = bf16[96,256]{1,0:T(8,128)(2,1)S(1)} collective-permute-done((bf16[96,256]{1,0:T(8,128)(2,1)S(1)}, bf16[96,256]{1,0:T(8,128)(2,1)S(1)}, u32[]{:S(2)}, u32[]{:S(2)}) %collective-permute-start.12) | collective-permute-done | bytes 49184 | tf_op jit(solution)/shard_map/ppermute | solution.py:91
  41.9 3.0 %collective-permute-start.15 = (bf16[96,256]{1,0:T(8,128)(2,1)S(1)}, bf16[96,256]{1,0:T(8,128)(2,1)S(1)}, u32[]{:S(2)}, u32[]{:S(2)}) collective-permute-start(bf16[96,256]{1,0:T(8,128)(2,1)S(1)} %get-tuple-element.43.refs_0_), channel_id=1, source_target_pairs={{0,16},{1,17},{2,18},{3,19},{4,20},{5,21},{6,22},{7,23},{8,24},{9,... | collective-permute-start | bytes 147464 | tf_op jit(solution)/shard_map/ppermute | solution.py:91
  45.1 2.2 %collective-permute-done.14.refs_1_ = bf16[96,256]{1,0:T(8,128)(2,1)S(1)} collective-permute-done((bf16[96,256]{1,0:T(8,128)(2,1)S(1)}, bf16[96,256]{1,0:T(8,128)(2,1)S(1)}, u32[]{:S(2)}, u32[]{:S(2)}) %collective-permute-start.14) | collective-permute-done | bytes 49184 | tf_op jit(solution)/shard_map/ppermute | solution.py:91
  48.1 1.5 %collective-permute-done.16.refs_3_ = bf16[96,256]{1,0:T(8,128)(2,1)S(1)} collective-permute-done((bf16[96,256]{1,0:T(8,128)(2,1)S(1)}, bf16[96,256]{1,0:T(8,128)(2,1)S(1)}, u32[]{:S(2)}, u32[]{:S(2)}) %collective-permute-start.16) | collective-permute-done | bytes 49184 | tf_op jit(solution)/shard_map/ppermute | solution.py:91
  50.5 1.5 %collective-permute-start.19 = (bf16[4,96,256]{2,1,0:T(8,128)(2,1)S(1)}, bf16[4,96,256]{2,1,0:T(8,128)(2,1)S(1)}, u32[]{:S(2)}, u32[]{:S(2)}) collective-permute-start(bf16[4,96,256]{2,1,0:T(8,128)(2,1)S(1)} %get-tuple-element.45.refs_0_), channel_id=1, source_target_pairs={{0,1},{1,0},{2,3},{3,2},{4,5},{5,4},{6,7},{7,6},{8,9},{9,8},{10,11... | collective-permute-start | bytes 589832 | tf_op jit(solution)/shard_map/ppermute | solution.py:91
  52.5 1.4 %collective-permute-start.23 = (bf16[4,96,256]{2,1,0:T(8,128)(2,1)S(1)}, bf16[4,96,256]{2,1,0:T(8,128)(2,1)S(1)}, u32[]{:S(2)}, u32[]{:S(2)}) collective-permute-start(bf16[4,96,256]{2,1,0:T(8,128)(2,1)S(1)} %get-tuple-element.45.refs_0_), channel_id=1, source_target_pairs={{0,5},{1,4},{2,7},{3,6},{4,1},{5,0},{6,3},{7,2},{8,13},{9,12},{10,... | collective-permute-start | bytes 589832 | tf_op jit(solution)/shard_map/ppermute | solution.py:91
  54.0 3.4 %collective-permute-done.19.refs_2_ = bf16[4,96,256]{2,1,0:T(8,128)(2,1)S(1)} collective-permute-done((bf16[4,96,256]{2,1,0:T(8,128)(2,1)S(1)}, bf16[4,96,256]{2,1,0:T(8,128)(2,1)S(1)}, u32[]{:S(2)}, u32[]{:S(2)}) %collective-permute-start.19) | collective-permute-done | bytes 196640 | tf_op jit(solution)/shard_map/ppermute | solution.py:91
  57.4 2.4 %collective-permute-done.21.refs_4_ = bf16[4,96,256]{2,1,0:T(8,128)(2,1)S(1)} collective-permute-done((bf16[4,96,256]{2,1,0:T(8,128)(2,1)S(1)}, bf16[4,96,256]{2,1,0:T(8,128)(2,1)S(1)}, u32[]{:S(2)}, u32[]{:S(2)}) %collective-permute-start.21) | collective-permute-done | bytes 196640 | tf_op jit(solution)/shard_map/ppermute | solution.py:91
  59.8 2.9 %collective-permute-done.23.refs_6_ = bf16[4,96,256]{2,1,0:T(8,128)(2,1)S(1)} collective-permute-done((bf16[4,96,256]{2,1,0:T(8,128)(2,1)S(1)}, bf16[4,96,256]{2,1,0:T(8,128)(2,1)S(1)}, u32[]{:S(2)}, u32[]{:S(2)}) %collective-permute-start.23) | collective-permute-done | bytes 196640 | tf_op jit(solution)/shard_map/ppermute | solution.py:91
  62.7 1.4 %collective-permute-done.24.refs_7_ = bf16[4,96,256]{2,1,0:T(8,128)(2,1)S(1)} collective-permute-done((bf16[4,96,256]{2,1,0:T(8,128)(2,1)S(1)}, bf16[4,96,256]{2,1,0:T(8,128)(2,1)S(1)}, u32[]{:S(2)}, u32[]{:S(2)}) %collective-permute-start.24) | collective-permute-done | bytes 196640 | tf_op jit(solution)/shard_map/ppermute | solution.py:91
  64.1 2.7 %shard_map.112 = (f32[768,3072]{1,0:T(8,128)}, f32[8,128]{1,0:T(8,128)S(1)}) custom-call(bf16[1536,256]{1,0:T(8,128)(2,1)S(1)} %get-tuple-element.28.p.p_ref, bf16[4,96,256]{2,1,0:T(8,128)(2,1)S(1)} %get-tuple-element.45.refs_0_, bf16[4,96,256]{2,1,0:T(8,128)(2,1)S(1)} %collective-permute-done.18.refs_1_, ...), custom_call_target="tpu_custom_call" | custom-call | tf_op jit(solution)/shard_map/pallas_call | solution.py:298
  68.5 3.3 %shard_map.115 = (f32[768,3072]{1,0:T(8,128)}, f32[8,128]{1,0:T(8,128)}) custom-call(bf16[1536,256]{1,0:T(8,128)(2,1)S(1)} %get-tuple-element.28.p.p_ref, bf16[4,96,256]{2,1,0:T(8,128)(2,1)S(1)} %get-tuple-element.45.refs_0_, bf16[4,96,256]{2,1,0:T(8,128)(2,1)S(1)} %collective-permute-done.18.refs_1_, ...), custom_call_target="tpu_custom_call", output_to_operand_aliasing={{0}: (10, {})} | custom-call | tf_op jit(solution)/shard_map/pallas_call | solution.py:298
  71.9 5.0 %shard_map.114 = bf16[576,1536]{1,0:T(8,128)(2,1)} custom-call(bf16[576,3072]{1,0:T(8,128)(2,1)S(1)} %copy-done, bf16[96,3072]{1,0:T(8,128)(2,1)S(1)} %get-tuple-element.38.refs_0_, bf16[96,3072]{1,0:T(8,128)(2,1)S(1)} %collective-permute-done.7.refs_8_.refs_1_, ...), custom_call_target="tpu_custom_call", output_to_operand_aliasing={{}: (11, {})} | custom-call | tf_op jit(solution)/shard_map/pallas_call | solution.py:443
  (53 shorter events, 10.2 us)
Async XLA Ops:
  2.1 10.0 %collective-permute-start = (bf16[48,3072]{1,0:T(8,128)(2,1)S(1)}, bf16[48,3072]{1,0:T(8,128)(2,1)S(1)}, u32[]{:S(2)}, u32[]{:S(2)}) collective-permute-start(bf16[48,3072]{1,0:T(8,128)(2,1)S(1)} %get-tuple-element.31), channel_id=1, source_target_pairs={{0,1},{1,0},{2,3},{3,2},{4,5},{5,4},{6,7},{7,6},{8,9},{9,8},{10,11... | collective-permute-start | bytes 884744 | tf_op jit(solution)/shard_map/ppermute | solution.py:91
  12.2 3.5 %collective-permute-start.1 = (bf16[2,2,4,96,256]{4,3,2,1,0:T(8,128)(2,1)S(1)}, bf16[2,2,4,96,256]{4,3,2,1,0:T(8,128)(2,1)S(1)}, u32[]{:S(2)}, u32[]{:S(2)}) collective-permute-start(bf16[2,2,4,96,256]{4,3,2,1,0:T(8,128)(2,1)S(1)} %shard_map.104), channel_id=1, source_target_pairs={{0,2},{1,3},{2,0},{3,1},{4,6},{5,7},{6,4},{7,5},{8,10},{9,11},{10,... | collective-permute-start | bytes 2359304 | tf_op jit(solution)/shard_map/ppermute | solution.py:91
  12.3 13.3 %collective-permute-start.5 = (bf16[48,3072]{1,0:T(8,128)(2,1)S(1)}, bf16[48,3072]{1,0:T(8,128)(2,1)S(1)}, u32[]{:S(2)}, u32[]{:S(2)}) collective-permute-start(bf16[48,3072]{1,0:T(8,128)(2,1)S(1)} %shard_map.106), channel_id=1, source_target_pairs={{0,1},{1,0},{2,3},{3,2},{4,5},{5,4},{6,7},{7,6},{8,9},{9,8},{10,11... | collective-permute-start | bytes 884744 | tf_op jit(solution)/shard_map/ppermute | solution.py:91
  14.1 11.6 %collective-permute-start.6 = (bf16[48,3072]{1,0:T(8,128)(2,1)S(1)}, bf16[48,3072]{1,0:T(8,128)(2,1)S(1)}, u32[]{:S(2)}, u32[]{:S(2)}) collective-permute-start(bf16[48,3072]{1,0:T(8,128)(2,1)S(1)} %collective-permute-done.refs_0_.refs_3_), channel_id=1, source_target_pairs={{0,8},{1,9},{2,10},{3,11},{4,12},{5,13},{6,14},{7,15},{8,0},{9,1},... | collective-permute-start | bytes 884744 | tf_op jit(solution)/shard_map/ppermute | solution.py:91
  15.8 14.4 %collective-permute-start.2 = (bf16[4,96,256]{2,1,0:T(8,128)(2,1)S(1)}, bf16[4,96,256]{2,1,0:T(8,128)(2,1)S(1)}, u32[]{:S(2)}, u32[]{:S(2)}) collective-permute-start(bf16[4,96,256]{2,1,0:T(8,128)(2,1)S(1)} %get-tuple-element.33.refs_0_), channel_id=1, source_target_pairs={{0,1},{1,0},{2,3},{3,2},{4,5},{5,4},{6,7},{7,6},{8,9},{9,8},{10,11... | collective-permute-start | bytes 589832 | tf_op jit(solution)/shard_map/ppermute | solution.py:91
  16.5 13.7 %collective-permute-start.3 = (bf16[4,96,256]{2,1,0:T(8,128)(2,1)S(1)}, bf16[4,96,256]{2,1,0:T(8,128)(2,1)S(1)}, u32[]{:S(2)}, u32[]{:S(2)}) collective-permute-start(bf16[4,96,256]{2,1,0:T(8,128)(2,1)S(1)} %get-tuple-element.34), channel_id=1, source_target_pairs={{0,4},{1,5},{2,6},{3,7},{4,0},{5,1},{6,2},{7,3},{8,12},{9,13},{10,... | collective-permute-start | bytes 589832 | tf_op jit(solution)/shard_map/ppermute | solution.py:91
  18.0 12.2 %collective-permute-start.4 = (bf16[4,96,256]{2,1,0:T(8,128)(2,1)S(1)}, bf16[4,96,256]{2,1,0:T(8,128)(2,1)S(1)}, u32[]{:S(2)}, u32[]{:S(2)}) collective-permute-start(bf16[4,96,256]{2,1,0:T(8,128)(2,1)S(1)} %get-tuple-element.35), channel_id=1, source_target_pairs={{0,5},{1,4},{2,7},{3,6},{4,1},{5,0},{6,3},{7,2},{8,13},{9,12},{10,... | collective-permute-start | bytes 589832 | tf_op jit(solution)/shard_map/ppermute | solution.py:91
  30.3 19.2 %collective-permute-start.8 = (bf16[96,3072]{1,0:T(8,128)(2,1)S(1)}, bf16[96,3072]{1,0:T(8,128)(2,1)S(1)}, u32[]{:S(2)}, u32[]{:S(2)}) collective-permute-start(bf16[96,3072]{1,0:T(8,128)(2,1)S(1)} %get-tuple-element.38.refs_0_), channel_id=1, source_target_pairs={{0,4},{1,5},{2,6},{3,7},{4,0},{5,1},{6,2},{7,3},{8,12},{9,13},{10,... | collective-permute-start | bytes 1769480 | tf_op jit(solution)/shard_map/ppermute | solution.py:91
  32.1 6.4 %collective-permute-start.11 = (bf16[96,256]{1,0:T(8,128)(2,1)S(1)}, bf16[96,256]{1,0:T(8,128)(2,1)S(1)}, u32[]{:S(2)}, u32[]{:S(2)}) collective-permute-start(bf16[96,256]{1,0:T(8,128)(2,1)S(1)} %get-tuple-element.40), channel_id=1, source_target_pairs={{0,8},{1,9},{2,10},{3,11},{4,12},{5,13},{6,14},{7,15},{8,16},{9,17... | collective-permute-start | bytes 147464 | tf_op jit(solution)/shard_map/ppermute | solution.py:91
  33.7 6.4 %collective-permute-start.12 = (bf16[96,256]{1,0:T(8,128)(2,1)S(1)}, bf16[96,256]{1,0:T(8,128)(2,1)S(1)}, u32[]{:S(2)}, u32[]{:S(2)}) collective-permute-start(bf16[96,256]{1,0:T(8,128)(2,1)S(1)} %get-tuple-element.41), channel_id=1, source_target_pairs={{0,16},{1,17},{2,18},{3,19},{4,20},{5,21},{6,22},{7,23},{8,24},{9,... | collective-permute-start | bytes 147464 | tf_op jit(solution)/shard_map/ppermute | solution.py:91
  36.2 4.2 %collective-permute-start.13 = (bf16[96,256]{1,0:T(8,128)(2,1)S(1)}, bf16[96,256]{1,0:T(8,128)(2,1)S(1)}, u32[]{:S(2)}, u32[]{:S(2)}) collective-permute-start(bf16[96,256]{1,0:T(8,128)(2,1)S(1)} %get-tuple-element.42), channel_id=1, source_target_pairs={{0,24},{1,25},{2,26},{3,27},{4,28},{5,29},{6,30},{7,31},{8,0},{9,1... | collective-permute-start | bytes 147464 | tf_op jit(solution)/shard_map/ppermute | solution.py:91
  37.6 14.4 %collective-permute-start.7 = (bf16[96,3072]{1,0:T(8,128)(2,1)S(1)}, bf16[96,3072]{1,0:T(8,128)(2,1)S(1)}, u32[]{:S(2)}, u32[]{:S(2)}) collective-permute-start(bf16[96,3072]{1,0:T(8,128)(2,1)S(1)} %get-tuple-element.38.refs_0_), channel_id=1, source_target_pairs={{0,2},{1,3},{2,0},{3,1},{4,6},{5,7},{6,4},{7,5},{8,10},{9,11},{10,... | collective-permute-start | bytes 1769480 | tf_op jit(solution)/shard_map/ppermute | solution.py:91
  41.3 6.0 %collective-permute-start.14 = (bf16[96,256]{1,0:T(8,128)(2,1)S(1)}, bf16[96,256]{1,0:T(8,128)(2,1)S(1)}, u32[]{:S(2)}, u32[]{:S(2)}) collective-permute-start(bf16[96,256]{1,0:T(8,128)(2,1)S(1)} %get-tuple-element.43.refs_0_), channel_id=1, source_target_pairs={{0,8},{1,9},{2,10},{3,11},{4,12},{5,13},{6,14},{7,15},{8,16},{9,17... | collective-permute-start | bytes 147464 | tf_op jit(solution)/shard_map/ppermute | solution.py:91
  41.9 6.1 %collective-permute-start.15 = (bf16[96,256]{1,0:T(8,128)(2,1)S(1)}, bf16[96,256]{1,0:T(8,128)(2,1)S(1)}, u32[]{:S(2)}, u32[]{:S(2)}) collective-permute-start(bf16[96,256]{1,0:T(8,128)(2,1)S(1)} %get-tuple-element.43.refs_0_), channel_id=1, source_target_pairs={{0,16},{1,17},{2,18},{3,19},{4,20},{5,21},{6,22},{7,23},{8,24},{9,... | collective-permute-start | bytes 147464 | tf_op jit(solution)/shard_map/ppermute | solution.py:91
  44.9 4.6 %collective-permute-start.16 = (bf16[96,256]{1,0:T(8,128)(2,1)S(1)}, bf16[96,256]{1,0:T(8,128)(2,1)S(1)}, u32[]{:S(2)}, u32[]{:S(2)}) collective-permute-start(bf16[96,256]{1,0:T(8,128)(2,1)S(1)} %get-tuple-element.43.refs_0_), channel_id=1, source_target_pairs={{0,24},{1,25},{2,26},{3,27},{4,28},{5,29},{6,30},{7,31},{8,0},{9,1... | collective-permute-start | bytes 147464 | tf_op jit(solution)/shard_map/ppermute | solution.py:91
  49.6 18.2 %collective-permute-start.17 = (bf16[144,3072]{1,0:T(8,128)(2,1)S(1)}, bf16[144,3072]{1,0:T(8,128)(2,1)S(1)}, u32[]{:S(2)}, u32[]{:S(2)}) collective-permute-start(bf16[144,3072]{1,0:T(8,128)(2,1)S(1)} %get-tuple-element.44), channel_id=1, source_target_pairs={{0,8},{1,9},{2,10},{3,11},{4,12},{5,13},{6,14},{7,15},{8,0},{9,1},... | collective-permute-start | bytes 2654216 | tf_op jit(solution)/shard_map/ppermute | solution.py:91
  49.9 14.2 %collective-permute-start.9 = (bf16[96,3072]{1,0:T(8,128)(2,1)S(1)}, bf16[96,3072]{1,0:T(8,128)(2,1)S(1)}, u32[]{:S(2)}, u32[]{:S(2)}) collective-permute-start(bf16[96,3072]{1,0:T(8,128)(2,1)S(1)} %collective-permute-done.8.refs_4_.refs_2_), channel_id=1, source_target_pairs={{0,2},{1,3},{2,0},{3,1},{4,6},{5,7},{6,4},{7,5},{8,10},{9,11},{10,... | collective-permute-start | bytes 1769480 | tf_op jit(solution)/shard_map/ppermute | solution.py:91
  50.5 6.9 %collective-permute-start.19 = (bf16[4,96,256]{2,1,0:T(8,128)(2,1)S(1)}, bf16[4,96,256]{2,1,0:T(8,128)(2,1)S(1)}, u32[]{:S(2)}, u32[]{:S(2)}) collective-permute-start(bf16[4,96,256]{2,1,0:T(8,128)(2,1)S(1)} %get-tuple-element.45.refs_0_), channel_id=1, source_target_pairs={{0,1},{1,0},{2,3},{3,2},{4,5},{5,4},{6,7},{7,6},{8,9},{9,8},{10,11... | collective-permute-start | bytes 589832 | tf_op jit(solution)/shard_map/ppermute | solution.py:91
  52.0 7.8 %collective-permute-start.21 = (bf16[4,96,256]{2,1,0:T(8,128)(2,1)S(1)}, bf16[4,96,256]{2,1,0:T(8,128)(2,1)S(1)}, u32[]{:S(2)}, u32[]{:S(2)}) collective-permute-start(bf16[4,96,256]{2,1,0:T(8,128)(2,1)S(1)} %get-tuple-element.45.refs_0_), channel_id=1, source_target_pairs={{0,4},{1,5},{2,6},{3,7},{4,0},{5,1},{6,2},{7,3},{8,12},{9,13},{10,... | collective-permute-start | bytes 589832 | tf_op jit(solution)/shard_map/ppermute | solution.py:91
  52.5 10.1 %collective-permute-start.23 = (bf16[4,96,256]{2,1,0:T(8,128)(2,1)S(1)}, bf16[4,96,256]{2,1,0:T(8,128)(2,1)S(1)}, u32[]{:S(2)}, u32[]{:S(2)}) collective-permute-start(bf16[4,96,256]{2,1,0:T(8,128)(2,1)S(1)} %get-tuple-element.45.refs_0_), channel_id=1, source_target_pairs={{0,5},{1,4},{2,7},{3,6},{4,1},{5,0},{6,3},{7,2},{8,13},{9,12},{10,... | collective-permute-start | bytes 589832 | tf_op jit(solution)/shard_map/ppermute | solution.py:91
  57.4 5.3 %collective-permute-start.20 = (bf16[4,96,256]{2,1,0:T(8,128)(2,1)S(1)}, bf16[4,96,256]{2,1,0:T(8,128)(2,1)S(1)}, u32[]{:S(2)}, u32[]{:S(2)}) collective-permute-start(bf16[4,96,256]{2,1,0:T(8,128)(2,1)S(1)} %collective-permute-done.19.refs_2_), channel_id=1, source_target_pairs={{0,2},{1,3},{2,0},{3,1},{4,6},{5,7},{6,4},{7,5},{8,10},{9,11},{10,... | collective-permute-start | bytes 589832 | tf_op jit(solution)/shard_map/ppermute | solution.py:91
  59.8 2.9 %collective-permute-start.22 = (bf16[4,96,256]{2,1,0:T(8,128)(2,1)S(1)}, bf16[4,96,256]{2,1,0:T(8,128)(2,1)S(1)}, u32[]{:S(2)}, u32[]{:S(2)}) collective-permute-start(bf16[4,96,256]{2,1,0:T(8,128)(2,1)S(1)} %collective-permute-done.21.refs_4_), channel_id=1, source_target_pairs={{0,2},{1,3},{2,0},{3,1},{4,6},{5,7},{6,4},{7,5},{8,10},{9,11},{10,... | collective-permute-start | bytes 589832 | tf_op jit(solution)/shard_map/ppermute | solution.py:91
  67.9 3.9 %collective-permute-start.25 = (bf16[144,3072]{1,0:T(8,128)(2,1)S(1)}, bf16[144,3072]{1,0:T(8,128)(2,1)S(1)}, u32[]{:S(2)}, u32[]{:S(2)}) collective-permute-start(bf16[144,3072]{1,0:T(8,128)(2,1)S(1)} %shard_map.113.refs_8_), channel_id=1, source_target_pairs={{0,2},{1,3},{2,0},{3,1},{4,6},{5,7},{6,4},{7,5},{8,10},{9,11},{10,... | collective-permute-start | bytes 2654216 | tf_op jit(solution)/shard_map/ppermute | solution.py:91
  68.0 3.8 %collective-permute-start.10 = (bf16[48,3072]{1,0:T(8,128)(2,1)S(1)}, bf16[48,3072]{1,0:T(8,128)(2,1)S(1)}, u32[]{:S(2)}, u32[]{:S(2)}) collective-permute-start(bf16[48,3072]{1,0:T(8,128)(2,1)S(1)} %collective-permute-done.6.refs_6_.refs_4_), channel_id=1, source_target_pairs={{0,2},{1,3},{2,0},{3,1},{4,6},{5,7},{6,4},{7,5},{8,10},{9,11},{10,... | collective-permute-start | bytes 884744 | tf_op jit(solution)/shard_map/ppermute | solution.py:91
  (7 other events, 89.4 us)
